TPU v7x, 32 devices: a whole 2x2x4 slice. The times are simulated.
32 devices in a mesh: dp: 4 (over z), row: 2 (over core), col: 4 (over y, x).
Axes of the slice: x: 2, y: 2, z: 4, core: 2. Of those that a mesh axis runs over, the one named last changes fastest.
Arguments:
- tokens: bfloat16 [6144, 2560], P(('dp', 'row'), 'col'), may hold values from -6 to 6
- cotangent: bfloat16 [6144, 2560], P(('dp', 'row'), 'col'), may hold values from -6 to 6
- rec_in: bfloat16 [2, 2560, 2560], P(None, 'col', 'row'), may hold values from -0.125 to 0.125
- rec_out: bfloat16 [2560, 2560], P('row', 'col'), may hold values from -0.5 to 0.5
- gates: bfloat16 [2, 10, 256, 256], P(None, 'row'), may hold values from -0.375 to 0.375
- gate_bias: float32 [2, 2560], P(None, 'row'), may hold values from -3 to 3
- decay: float32 [2560], P('row')
- conv_w: float32 [4, 2560], P(None, 'row'), may hold values from -3 to 3
- conv_b: float32 [2560], P('row'), may hold values from -3 to 3
- gains: float32 [2, 2560], P(None, 'col'), may hold values from 0.5 to 1.5
- mlp_in: bfloat16 [2, 2560, 7680], P(None, 'col', 'row'), may hold values from -0.125 to 0.125
- mlp_out: bfloat16 [7680, 2560], P('row', 'col'), may hold values from -0.125 to 0.125
- lengths: int32 [16], replicated, may hold values from 1 to 1024, as said below
- order: int32 [16], replicated, may hold values from 0 to 15, as said below
Outputs:
- result: bfloat16 [6144, 2560], P(('dp', 'row'), 'col')
- grad_input: bfloat16 [6144, 2560], P(('dp', 'row'), 'col')
- grad_rec_in: float32 [2, 2560, 2560], P(None, ('col', 'dp'), 'row')
- grad_rec_out: float32 [2560, 2560], P('row', ('col', 'dp'))
- grad_gates: float32 [2, 10, 256, 256], P(None, 'row')
- grad_gate_bias: float32 [2, 2560], P(None, 'row')
- grad_decay: float32 [2560], P('row')
- grad_conv_w: float32 [4, 2560], P(None, 'row')
- grad_conv_b: float32 [2560], P('row')
- grad_gains: float32 [2, 2560], P(None, 'col')
- grad_mlp_in: float32 [2, 2560, 7680], P(None, ('col', 'dp'), 'row')
- grad_mlp_out: float32 [7680, 2560], P('row', ('col', 'dp'))
- stats: float32 [4], replicated
Inputs may be any that keep to these rules, and one draw needn't show every extreme that they name: Group g takes the sequences order[4 * g] to order[4 g + 3] in that order; their lengths add up to exactly 1536 in every group, and every group has one sequence of 1024 tokens. `order`: A permutation of the sequence numbers.
All inputs are finite; a program needn't handle non-finite values.
Results may differ from a plain program's by a relative error of at most 0.013.
Values may be sent and summed in bfloat16 or wider, within the bound.
A program may use at most 320 MiB of HBM per device.

v0:
```python
import jax
import jax.numpy as jnp
from jax import lax
from jax.sharding import PartitionSpec as P

epsilon = 1e-06


def shifted(x, axis, by):
    length = lax.axis_size(axis)
    pairs = [(i, i + by) for i in range(length) if 0 <= i + by < length]
    return lax.ppermute(x, axis, pairs)


def prefix(x, axis, combine, identity, reverse):
    length, index = (lax.axis_size(axis), lax.axis_index(axis))
    everything = jax.tree.map(lambda part: lax.all_gather(part, axis), x)
    start = jax.tree.map(
        lambda part, zero: jnp.broadcast_to(jnp.asarray(zero, part.dtype), part.shape), x, identity
    )

    def turn(k, before):
        at = length - 1 - k if reverse else k
        reached = at > index if reverse else at < index
        new = combine(before, jax.tree.map(lambda part: part[at], everything))
        return jax.tree.map(lambda a, b: jnp.where(reached, a, b), new, before)

    return lax.fori_loop(0, length, turn, start)


def compose(first, second):
    return (first[0] * second[0], second[0] * first[1] + second[1])


def gelu(values):
    return jax.nn.gelu(values, approximate=True)


def seq_tables(lengths, order):
    number = lengths.shape[0]
    slots = jnp.arange(number, dtype=jnp.int32)
    chosen = (order[:, None] == slots[None, :]).astype(jnp.int32)
    group_lengths = jnp.sum(chosen * lengths[None, :], axis=1)
    input_offsets = jnp.cumsum(lengths) - lengths
    group_offsets = jnp.cumsum(group_lengths) - group_lengths
    input_starts = jnp.sum(chosen * input_offsets[None, :], axis=1)
    inverse = jnp.sum(chosen * slots[:, None], axis=0)
    return (slots, input_offsets, group_offsets, input_starts, inverse)


def locate(rows, tables):
    slots, input_offsets, group_offsets, input_starts, inverse = tables
    which = jnp.sum((rows[:, None] >= group_offsets[None, :]).astype(jnp.int32), axis=1) - 1
    match = (which[:, None] == slots[None, :]).astype(jnp.int32)
    places = rows - jnp.sum(match * group_offsets[None, :], axis=1)
    source = jnp.sum(match * input_starts[None, :], axis=1) + places
    return (source, places)


def home(rows, tables):
    slots, input_offsets, group_offsets, input_starts, inverse = tables
    which = jnp.sum((rows[:, None] >= input_offsets[None, :]).astype(jnp.int32), axis=1) - 1
    match = (which[:, None] == slots[None, :]).astype(jnp.int32)
    places = rows - jnp.sum(match * input_offsets[None, :], axis=1)
    target = jnp.sum(match * inverse[None, :], axis=1)
    second = (target[:, None] == slots[None, :]).astype(jnp.int32)
    return jnp.sum(second * group_offsets[None, :], axis=1) + places


def lru_coeffs(pre, inputs, decay, reset):
    input_gate = jax.nn.sigmoid(pre[0])
    rate_gate = jax.nn.sigmoid(pre[1])
    log_decay = -8.0 * rate_gate * jax.nn.softplus(decay)
    decay_factor = jnp.where(reset, 0.0, jnp.exp(log_decay))
    scaling = jnp.where(reset, 1.0, jnp.sqrt(-jnp.expm1(2.0 * log_decay)))
    return (decay_factor, inputs * input_gate * scaling)


def picker(wanted, carry, pieces):
    row_count = pieces[0].shape[0]
    inside = ((wanted >= 0) & (wanted < row_count))[:, None]
    clipped = jnp.clip(wanted, 0, row_count - 1)
    return tuple(
        (
            jnp.where(inside, jnp.take(piece, clipped, axis=0), kept)
            for piece, kept in zip(pieces, carry)
        )
    )


def rows_then_cols(local, product):
    gathered = lax.all_gather(local, "row", axis=0, tiled=True)
    return (lax.psum_scatter(product(gathered), "col", scatter_dimension=0, tiled=True), gathered)


def cols_then_rows(local, product):
    gathered = lax.all_gather(local, "col", axis=0, tiled=True)
    return (lax.psum_scatter(product(gathered), "row", scatter_dimension=0, tiled=True), gathered)


def norm_sums(values):
    return lax.psum(values, "col")


def spread(values):
    return (
        lax.psum_scatter(
            values[0].astype(jnp.bfloat16), "dp", scatter_dimension=1, tiled=True
        ).astype(jnp.float32),
        lax.psum_scatter(
            values[1].astype(jnp.bfloat16), "dp", scatter_dimension=1, tiled=True
        ).astype(jnp.float32),
        lax.psum_scatter(
            values[2].astype(jnp.bfloat16), "dp", scatter_dimension=1, tiled=True
        ).astype(jnp.float32),
        lax.psum_scatter(
            values[3].astype(jnp.bfloat16), "dp", scatter_dimension=1, tiled=True
        ).astype(jnp.float32),
    )


def body(
    tokens,
    cotangent,
    rec_in,
    rec_out,
    gates,
    gate_bias,
    decay,
    conv_w,
    conv_b,
    gains,
    mlp_in,
    mlp_out,
    lengths,
    order,
):
    n_row = lax.axis_size("row")
    n_col = lax.axis_size("col")
    half = tokens.shape[0]
    group = half * n_row
    quarter = group // n_col
    width = tokens.shape[1] * n_col
    taps = conv_w.shape[0]
    blocks = gates.shape[1]
    block_width = gates.shape[2]
    channels = blocks * block_width
    dp_index = lax.axis_index("dp")
    row_index = lax.axis_index("row")
    col_index = lax.axis_index("col")
    tables = seq_tables(lengths, order)
    base_row = dp_index * group
    stream_rows = base_row + row_index * half + jnp.arange(half, dtype=jnp.int32)
    source, _ = locate(stream_rows, tables)
    empty = jnp.zeros_like(tokens)
    arrived, upstream = picker(
        source,
        (empty, empty),
        (
            lax.all_gather(tokens, ("dp", "row"), axis=0, tiled=True),
            lax.all_gather(cotangent, ("dp", "row"), axis=0, tiled=True),
        ),
    )
    scan_rows = base_row + col_index * quarter + jnp.arange(quarter + taps - 1, dtype=jnp.int32)
    _, places_ext = locate(scan_rows, tables)
    places = places_ext[:quarter]
    inputs_f = arrived.astype(jnp.float32)
    (sumsq_one,) = norm_sums((jnp.sum(inputs_f * inputs_f, axis=-1),))
    scale_one = lax.rsqrt(sumsq_one / width + epsilon)[:, None]
    normed_one = (inputs_f * scale_one * gains[0]).astype(jnp.bfloat16)
    parts_one, normed_one_all = rows_then_cols(
        normed_one,
        lambda rows: jnp.einsum("td,jdf->tjf", rows, rec_in, preferred_element_type=jnp.float32),
    )
    x_branch = parts_one[:, 0]
    y_branch = parts_one[:, 1]
    earlier = shifted(x_branch[quarter - (taps - 1) :], "col", 1)
    x_ext = jnp.concatenate([earlier, x_branch], axis=0)
    mixed = conv_b[None, :] + jnp.zeros_like(x_branch)
    for tap_index in range(taps):
        lagged = x_ext[taps - 1 - tap_index : taps - 1 - tap_index + quarter]
        mixed = mixed + jnp.where(
            (places >= tap_index)[:, None], conv_w[tap_index][None, :] * lagged, 0.0
        )
    conv_low = mixed.astype(jnp.bfloat16)
    conv_f = conv_low.astype(jnp.float32)
    conv_blocks = conv_low.reshape(quarter, blocks, block_width)
    pre = (
        jnp.einsum(
            "tnb,jnbc->jtnc", conv_blocks, gates, preferred_element_type=jnp.float32
        ).reshape(2, quarter, channels)
        + gate_bias[:, None, :]
    )
    reset = (places == 0)[:, None]
    decay_factor, inject = lru_coeffs(pre, conv_f, decay, reset)
    cum_decay, cum_state = lax.associative_scan(compose, (decay_factor, inject))
    identity = (jnp.ones((channels,), jnp.float32), jnp.zeros((channels,), jnp.float32))
    _, state_in = prefix((cum_decay[-1], cum_state[-1]), "col", compose, identity, False)
    state = cum_state + cum_decay * state_in[None, :]
    branch = (state * gelu(y_branch)).astype(jnp.bfloat16)
    out_one, branch_all = cols_then_rows(
        branch, lambda rows: jnp.dot(rows, rec_out, preferred_element_type=jnp.float32)
    )
    resid = inputs_f + out_one
    sumsq_two, sumsq_out_one = norm_sums(
        (jnp.sum(resid * resid, axis=-1), jnp.sum(out_one * out_one, axis=-1))
    )
    scale_two = lax.rsqrt(sumsq_two / width + epsilon)[:, None]
    normed_two = (resid * scale_two * gains[1]).astype(jnp.bfloat16)
    parts_two, normed_two_all = rows_then_cols(
        normed_two,
        lambda rows: jnp.einsum("td,jdf->tjf", rows, mlp_in, preferred_element_type=jnp.float32),
    )
    gate_part = parts_two[:, 0]
    up_part = parts_two[:, 1]
    hidden = (gelu(gate_part) * up_part).astype(jnp.bfloat16)
    out_two, hidden_all = cols_then_rows(
        hidden, lambda rows: jnp.dot(rows, mlp_out, preferred_element_type=jnp.float32)
    )
    output = (resid + out_two).astype(jnp.bfloat16)
    upstream_f = upstream.astype(jnp.float32)
    d_hidden, upstream_all = rows_then_cols(
        upstream,
        lambda rows: jnp.einsum("td,fd->tf", rows, mlp_out, preferred_element_type=jnp.float32),
    )
    grad_mlp_out = jnp.einsum(
        "tf,td->fd", hidden_all, upstream_all, preferred_element_type=jnp.float32
    )
    _, glu_back = jax.vjp(lambda gate_v, up_v: gelu(gate_v) * up_v, gate_part, up_part)
    d_gate, d_up = glu_back(d_hidden)
    d_parts_two = jnp.stack([d_gate, d_up], axis=1).astype(jnp.bfloat16)
    d_normed_two, d_parts_two_all = cols_then_rows(
        d_parts_two,
        lambda rows: jnp.einsum("tjf,jdf->td", rows, mlp_in, preferred_element_type=jnp.float32),
    )
    grad_mlp_in = jnp.einsum(
        "td,tjf->jdf", normed_two_all, d_parts_two_all, preferred_element_type=jnp.float32
    )
    gained_two = gains[1] * d_normed_two
    inner_two, sumsq_out_two = norm_sums(
        (jnp.sum(gained_two * resid, axis=-1), jnp.sum(out_two * out_two, axis=-1))
    )
    grad_gain_two = jnp.sum(d_normed_two * resid * scale_two, axis=0)
    d_resid = (
        upstream_f + scale_two * gained_two - resid * scale_two**3 * (inner_two / width)[:, None]
    )
    d_out_one = d_resid.astype(jnp.bfloat16)
    d_branch, d_out_one_all = rows_then_cols(
        d_out_one,
        lambda rows: jnp.einsum("td,fd->tf", rows, rec_out, preferred_element_type=jnp.float32),
    )
    grad_rec_out = jnp.einsum(
        "tf,td->fd", branch_all, d_out_one_all, preferred_element_type=jnp.float32
    )
    _, mix_back = jax.vjp(lambda state_v, gate_v: state_v * gelu(gate_v), state, y_branch)
    d_state, d_y_branch = mix_back(d_branch)
    rev_decay, rev_message = lax.associative_scan(
        compose, (decay_factor, decay_factor * d_state), reverse=True
    )
    _, message_in = prefix((rev_decay[0], rev_message[0]), "col", compose, identity, True)
    message = rev_message + rev_decay * message_in[None, :]
    message_next = jnp.concatenate([message[1:], message_in[None, :]], axis=0)
    grad_state = d_state + message_next
    state_prev = jnp.concatenate([state_in[None, :], state[:-1]], axis=0)
    _, coef_back = jax.vjp(
        lambda pre_v, conv_v, decay_v: lru_coeffs(pre_v, conv_v, decay_v, reset), pre, conv_f, decay
    )
    d_pre, d_conv, grad_decay = coef_back((grad_state * state_prev, grad_state))
    d_pre_low = d_pre.astype(jnp.bfloat16)
    d_pre_blocks = d_pre_low.reshape(2, quarter, blocks, block_width)
    d_conv = d_conv + jnp.einsum(
        "jtnc,jnbc->tnb", d_pre_blocks, gates, preferred_element_type=jnp.float32
    ).reshape(quarter, channels)
    grad_gates = jnp.einsum(
        "tnb,jtnc->jnbc", conv_blocks, d_pre_blocks, preferred_element_type=jnp.float32
    )
    grad_gate_bias = jnp.sum(d_pre_low.astype(jnp.float32), axis=1)
    later = shifted(d_conv[: taps - 1], "col", -1)
    d_ext = jnp.concatenate([d_conv, later], axis=0)
    d_x_branch = jnp.zeros_like(d_conv)
    tap_grads = []
    for tap_index in range(taps):
        ahead = d_ext[tap_index : tap_index + quarter]
        valid_ahead = (places_ext[tap_index : tap_index + quarter] >= tap_index)[:, None]
        d_x_branch = d_x_branch + jnp.where(valid_ahead, conv_w[tap_index][None, :] * ahead, 0.0)
        lagged = x_ext[taps - 1 - tap_index : taps - 1 - tap_index + quarter]
        tap_grads.append(
            jnp.sum(jnp.where((places >= tap_index)[:, None], d_conv * lagged, 0.0), axis=0)
        )
    grad_conv_w = jnp.stack(tap_grads, axis=0)
    grad_conv_b = jnp.sum(d_conv, axis=0)
    d_parts_one = jnp.stack([d_x_branch, d_y_branch], axis=1).astype(jnp.bfloat16)
    d_normed_one, d_parts_one_all = cols_then_rows(
        d_parts_one,
        lambda rows: jnp.einsum("tjf,jdf->td", rows, rec_in, preferred_element_type=jnp.float32),
    )
    grad_rec_in = jnp.einsum(
        "td,tjf->jdf", normed_one_all, d_parts_one_all, preferred_element_type=jnp.float32
    )
    gained_one = gains[0] * d_normed_one
    (inner_one,) = norm_sums((jnp.sum(gained_one * inputs_f, axis=-1),))
    grad_gain_one = jnp.sum(d_normed_one * inputs_f * scale_one, axis=0)
    d_input = (
        d_resid + scale_one * gained_one - inputs_f * scale_one**3 * (inner_one / width)[:, None]
    )
    grad_rec_in, grad_rec_out, grad_mlp_in, grad_mlp_out = spread(
        (grad_rec_in, grad_rec_out, grad_mlp_in, grad_mlp_out)
    )
    grad_gates, grad_gate_bias, grad_decay, grad_conv_w, grad_conv_b = lax.psum(
        (grad_gates, grad_gate_bias, grad_decay, grad_conv_w, grad_conv_b), ("dp", "col")
    )
    local_sums = jnp.stack(
        [jnp.sum(sumsq_one), jnp.sum(sumsq_out_one), jnp.sum(sumsq_two), jnp.sum(sumsq_out_two)]
    )
    grad_gains, totals = lax.psum(
        (jnp.stack([grad_gain_one, grad_gain_two], axis=0), local_sums), ("dp", "row")
    )
    stats = jnp.sqrt(totals / (lax.axis_size("dp") * group * width))
    given_rows = (dp_index * n_row + row_index) * half + jnp.arange(half, dtype=jnp.int32)
    wanted = home(given_rows, tables)
    result, grad_input = picker(
        wanted,
        (empty, empty),
        (
            lax.all_gather(output, ("dp", "row"), axis=0, tiled=True),
            lax.all_gather(d_input.astype(jnp.bfloat16), ("dp", "row"), axis=0, tiled=True),
        ),
    )
    return (
        result,
        grad_input,
        grad_rec_in,
        grad_rec_out,
        grad_gates,
        grad_gate_bias,
        grad_decay,
        grad_conv_w,
        grad_conv_b,
        grad_gains,
        grad_mlp_in,
        grad_mlp_out,
        stats,
    )


def solution(mesh):
    placed = (
        P(("dp", "row"), "col"),
        P(("dp", "row"), "col"),
        P(None, "col", "row"),
        P("row", "col"),
        P(None, "row", None, None),
        P(None, "row"),
        P("row"),
        P(None, "row"),
        P("row"),
        P(None, "col"),
        P(None, "col", "row"),
        P("row", "col"),
        P(),
        P(),
    )
    return jax.shard_map(
        body,
        mesh=mesh,
        in_specs=placed,
        out_specs=(
            P(("dp", "row"), "col"),
            P(("dp", "row"), "col"),
            P(None, ("col", "dp"), "row"),
            P("row", ("col", "dp")),
            P(None, "row", None, None),
            P(None, "row"),
            P("row"),
            P(None, "row"),
            P("row"),
            P(None, "col"),
            P(None, ("col", "dp"), "row"),
            P("row", ("col", "dp")),
            P(),
        ),
        check_vma=False,
    )
```

profile of v0, /device:TPU:0, one launch (start us, length us, event | category | flops | bytes accessed | tf_op | source)
XLA Modules:
  0.0 3186.4 jit_solution(6519108278140212785)
XLA Ops:
  13.3 76.9 %all-gather.17.cloned.1.call-done = bf16[6144,640]{1,0:T(8,128)(2,1)} async-done(((bf16[768,640]{1,0:T(8,128)(2,1)}), bf16[6144,640]{1,0:T(8,128)(2,1)}) %all-gather.17.cloned.1.call-update) | async-done | bytes 7864336 | tf_op jit(solution)/shard_map/all_gather | solution.py:160
  134.1 146.3 %reduce-scatter.11.cloned.1.call-done = f32[384,2,1280]{2,0,1:T(8,128)} async-done(((f32[1536,2,1280]{2,0,1:T(8,128)}), f32[384,2,1280]{2,0,1:T(8,128)}) %reduce-scatter.11.cloned.1.call-update) | async-done | bytes 3932176 | tf_op jit(solution)/shard_map/reduce_scatter | solution.py:93
  567.0 50.6 %all-gather.21.cloned.1.call-done = bf16[1536,1280]{1,0:T(8,128)(2,1)} async-done(((bf16[384,1280]{1,0:T(8,128)(2,1)}), bf16[1536,1280]{1,0:T(8,128)(2,1)}) %all-gather.21.cloned.1.call-update) | async-done | bytes 3932176 | tf_op jit(solution)/shard_map/all_gather | solution.py:97
  625.5 71.4 %all-gather.29.cloned.1.call-done = bf16[6144,640]{1,0:T(8,128)(2,1)} async-done(((bf16[768,640]{1,0:T(8,128)(2,1)}), bf16[6144,640]{1,0:T(8,128)(2,1)}) %all-gather.29.cloned.1.call-update) | async-done | bytes 7864336 | tf_op jit(solution)/shard_map/all_gather | solution.py:161
  727.3 16.5 fusion.108
  744.3 28.7 fusion.56
  773.1 179.1 %reduce-scatter.19.cloned.1.call-done = f32[384,3840]{1,0:T(8,128)} async-done(((f32[1536,3840]{1,0:T(8,128)}), f32[384,3840]{1,0:T(8,128)}) %reduce-scatter.19.cloned.1.call-update) | async-done | bytes 5898256 | tf_op jit(solution)/shard_map/reduce_scatter | solution.py:93
  952.2 401.7 %reduce-scatter.15.cloned.1.call-done = f32[384,2,3840]{2,0,1:T(8,128)} async-done(((f32[1536,2,3840]{2,0,1:T(8,128)}), f32[384,2,3840]{2,0,1:T(8,128)}) %reduce-scatter.15.cloned.1.call-update) | async-done | bytes 11796496 | tf_op jit(solution)/shard_map/reduce_scatter | solution.py:93
  1367.9 213.8 %all-gather.33.cloned.1.call-done = bf16[1536,2,3840]{2,0,1:T(8,128)(2,1)} async-done(((bf16[384,2,3840]{2,0,1:T(8,128)(2,1)}), bf16[1536,2,3840]{2,0,1:T(8,128)(2,1)}) %all-gather.33.cloned.1.call-update) | async-done | bytes 23592976 | tf_op jit(solution)/shard_map/all_gather | solution.py:97
  1581.7 25.2 convolution_bitcast_fusion.1
  1607.1 92.9 %all-gather.25.cloned.1.call-done = bf16[1536,3840]{1,0:T(8,128)(2,1)} async-done(((bf16[384,3840]{1,0:T(8,128)(2,1)}), bf16[1536,3840]{1,0:T(8,128)(2,1)}) %all-gather.25.cloned.1.call-update) | async-done | bytes 11796496 | tf_op jit(solution)/shard_map/all_gather | solution.py:97
  1793.3 47.1 %reduce-scatter.23.cloned.1.call-done = f32[384,1280]{1,0:T(8,128)} async-done(((f32[1536,1280]{1,0:T(8,128)}), f32[384,1280]{1,0:T(8,128)}) %reduce-scatter.23.cloned.1.call-update) | async-done | bytes 1966096 | tf_op jit(solution)/shard_map/reduce_scatter | solution.py:93
  2095.9 15.7 rev.9
  2111.6 15.7 rev.8
  2185.3 84.1 %all-gather.37.cloned.1.call-done = bf16[1536,2,1280]{2,0,1:T(8,128)(2,1)} async-done(((bf16[384,2,1280]{2,0,1:T(8,128)(2,1)}), bf16[1536,2,1280]{2,0,1:T(8,128)(2,1)}) %all-gather.37.cloned.1.call-update) | async-done | bytes 7864336 | tf_op jit(solution)/shard_map/all_gather | solution.py:97
  2305.7 24.8 convert_bitcast_fusion
  2330.4 26.5 copy.94
  2404.4 19.1 reduce-scatter.27.cloned.1.call-done
  2425.4 76.5 %all-gather.27.cloned.1.call-done = bf16[6144,640]{1,0:T(8,128)(2,1)} async-done(((bf16[768,640]{1,0:T(8,128)(2,1)}), bf16[6144,640]{1,0:T(8,128)(2,1)}) %all-gather.27.cloned.1.call-update) | async-done | bytes 7864336 | tf_op jit(solution)/shard_map/all_gather | solution.py:325
  2509.8 76.3 %all-reduce.68 = (f32[2,1280]{1,0:T(2,128)}, f32[1280]{0:T(1024)}, f32[4,1280]{1,0:T(4,128)}, f32[1280]{0:T(1024)}) all-reduce(f32[2,1280]{1,0:T(2,128)S(1)} %get-tuple-element.388, f32[1280]{0:T(1024)S(1)} %get-tuple-element.493, f32[4,1280]{1,0:T(4,128)S(1)} %pad_maximum_fusion.32, ...), channel_id=1, replica_groups=mesh['dp'=4,'row'=2,'col'=4] {'dp','col'}, use_global_device_ids=true, to_apply=%region_38.40 | all-reduce | flops 10240 | bytes 81920 | tf_op jit(solution)/shard_map/psum | solution.py:309
  2586.1 56.9 %all-reduce.75.cloned.1.call-done = f32[2,5,256,256]{2,3,0,1:T(8,128)} async-done(((f32[2,5,256,256]{2,3,0,1:T(8,128)}), f32[2,5,256,256]{2,3,0,1:T(8,128)}) %all-reduce.75.cloned.1.call-update) | async-done | bytes 2621456 | tf_op jit(solution)/shard_map/psum | solution.py:309
  2650.0 16.7 all-reduce.69
  2667.2 422.4 %all-reduce.77.cloned.1.call-done = (bf16[2,640,1280]{2,0,1:T(2,128)(2,1)}, bf16[2,640,3840]{2,0,1:T(2,128)(2,1)}) async-done(((bf16[2,640,1280]{2,0,1:T(2,128)(2,1)}, bf16[2,640,3840]{2,0,1:T(2,128)(2,1)}), (bf16[2,640,1280]{2,0,1:T(2,128)(2,1)}, bf16[2,640,3840]{2,0,1:T(2,128)(2,1)})) %all-reduce.77.cloned.1.call-update) | async-done | bytes 13107216
  3098.5 69.8 %all-gather.39.cloned.1.call-done = bf16[6144,640]{1,0:T(8,128)(2,1)} async-done(((bf16[768,640]{1,0:T(8,128)(2,1)}), bf16[6144,640]{1,0:T(8,128)(2,1)}) %all-gather.39.cloned.1.call-update) | async-done | bytes 7864336 | tf_op jit(solution)/shard_map/all_gather | solution.py:326
  (693 shorter events, 915.5 us)
Async XLA Ops:
  7.2 82.9 %all-gather.17.cloned.1.call-start = ((), (), s32[]{:S(2)}) async-start(), calls=%async_computation.10 | async-start | bytes 8847360 | tf_op jit(solution)/shard_map/all_gather | solution.py:160
  7.9 113.3 %all-gather.19.cloned.1.call-start = ((), (), s32[]{:S(2)}) async-start(), calls=%async_computation.11 | async-start | bytes 2949120 | tf_op jit(solution)/shard_map/all_gather | solution.py:92
  114.0 166.4 %reduce-scatter.11.cloned.1.call-start = ((), (), s32[]{:S(2)}) async-start(), calls=%async_computation.12 | async-start | bytes 19660800 | tf_op jit(solution)/shard_map/reduce_scatter | solution.py:93
  132.5 485.1 %all-gather.21.cloned.1.call-start = ((), (), s32[]{:S(2)}) async-start(), calls=%async_computation.13 | async-start | bytes 4915200 | tf_op jit(solution)/shard_map/all_gather | solution.py:97
  566.4 130.5 %all-gather.29.cloned.1.call-start = ((), (), s32[]{:S(2)}) async-start(), calls=%async_computation.20 | async-start | bytes 8847360 | tf_op jit(solution)/shard_map/all_gather | solution.py:161
  567.0 143.1 %reduce-scatter.13.cloned.1.call-start = ((), (), s32[]{:S(2)}) async-start(), calls=%async_computation.14 | async-start | bytes 5898240 | tf_op jit(solution)/shard_map/reduce_scatter | solution.py:98
  625.4 101.8 %all-gather.31.cloned.1.call-start = ((), (), s32[]{:S(2)}) async-start(), calls=%async_computation.21 | async-start | bytes 2949120 | tf_op jit(solution)/shard_map/all_gather | solution.py:92
  707.3 37.0 %all-gather.23.cloned.1.call-start = ((), (), s32[]{:S(2)}) async-start(), calls=%async_computation.15 | async-start | bytes 2949120 | tf_op jit(solution)/shard_map/all_gather | solution.py:92
  727.2 225.0 %reduce-scatter.19.cloned.1.call-start = ((), (), s32[]{:S(2)}) async-start(), calls=%async_computation.22 | async-start | bytes 29491200 | tf_op jit(solution)/shard_map/reduce_scatter | solution.py:93
  743.8 610.0 %reduce-scatter.15.cloned.1.call-start = ((), (), s32[]{:S(2)}) async-start(), calls=%async_computation.16 | async-start | bytes 58982400 | tf_op jit(solution)/shard_map/reduce_scatter | solution.py:93
  773.0 808.7 %all-gather.33.cloned.1.call-start = ((), (), s32[]{:S(2)}) async-start(), calls=%async_computation.23 | async-start | bytes 29491200 | tf_op jit(solution)/shard_map/all_gather | solution.py:97
  1367.2 332.8 %all-gather.25.cloned.1.call-start = ((), (), s32[]{:S(2)}) async-start(), calls=%async_computation.17 | async-start | bytes 14745600 | tf_op jit(solution)/shard_map/all_gather | solution.py:97
  1367.8 347.2 %reduce-scatter.21.cloned.1.call-start = ((), (), s32[]{:S(2)}) async-start(), calls=%async_computation.24 | async-start | bytes 5898240 | tf_op jit(solution)/shard_map/reduce_scatter | solution.py:98
  1606.9 123.1 %reduce-scatter.17.cloned.1.call-start = ((), (), s32[]{:S(2)}) async-start(), calls=%async_computation.18 | async-start | bytes 5898240 | tf_op jit(solution)/shard_map/reduce_scatter | solution.py:98
  1715.0 32.2 %all-gather.35.cloned.1.call-start = ((), (), s32[]{:S(2)}) async-start(), calls=%async_computation.25 | async-start | bytes 2949120 | tf_op jit(solution)/shard_map/all_gather | solution.py:92
  1735.5 104.9 %reduce-scatter.23.cloned.1.call-start = ((), (), s32[]{:S(2)}) async-start(), calls=%async_computation.26 | async-start | bytes 9830400 | tf_op jit(solution)/shard_map/reduce_scatter | solution.py:93
  1755.7 513.6 %all-gather.37.cloned.1.call-start = ((), (), s32[]{:S(2)}) async-start(), calls=%async_computation.27 | async-start | bytes 9830400 | tf_op jit(solution)/shard_map/all_gather | solution.py:97
  2185.2 192.9 %reduce-scatter.25.cloned.1.call-start = ((), (), s32[]{:S(2)}) async-start(), calls=%async_computation.28 | async-start | bytes 5898240 | tf_op jit(solution)/shard_map/reduce_scatter | solution.py:98
  2279.2 122.3 %reduce-scatter.29.cloned.1.call-start = ((), (), s32[]{:S(2)}) async-start(), calls=%async_computation.32 | async-start | bytes 6144000 | tf_op jit(solution)/shard_map/reduce_scatter | solution.py:116
  2293.0 130.4 %reduce-scatter.27.cloned.1.call-start = ((), (), s32[]{:S(2)}) async-start(), calls=%async_computation.30 | async-start | bytes 2048000 | tf_op jit(solution)/shard_map/reduce_scatter | solution.py:110
  2299.8 202.1 %all-gather.27.cloned.1.call-start = ((), (), s32[]{:S(2)}) async-start(), calls=%async_computation.19 | async-start | bytes 8847360 | tf_op jit(solution)/shard_map/all_gather | solution.py:325
  2300.5 342.4 %all-reduce.75.cloned.1.call-start = ((), (), s32[]{:S(2)}) async-start(), calls=%async_computation.31 | async-start | bytes 5242880 | tf_op jit(solution)/shard_map/psum | solution.py:309
  2305.5 784.1 %all-reduce.77.cloned.1.call-start = ((), (), s32[]{:S(2)}) async-start(), calls=%async_computation.33 | async-start | bytes 26214400
  2378.0 790.3 %all-gather.39.cloned.1.call-start = ((), (), s32[]{:S(2)}) async-start(), calls=%async_computation.29 | async-start | bytes 8847360 | tf_op jit(solution)/shard_map/all_gather | solution.py:326
  (115 other events, 6070.2 us)
Sparse Core Ops, SparseCore 0:
  9.7 80.4 all-gather.16
  114.1 7.0 all-gather.18
  132.6 147.6 reduce-scatter.10
  566.5 51.0 all-gather.20
  619.1 77.7 all-gather.28
  699.6 10.4 reduce-scatter.12
  711.6 11.5 all-gather.30
  727.3 9.6 all-gather.22
  743.9 208.1 reduce-scatter.18
  955.1 398.6 reduce-scatter.14
  1367.4 214.2 all-gather.32
  1584.1 115.9 all-gather.24
  1702.4 11.8 reduce-scatter.20
  1717.0 12.9 reduce-scatter.16
  1735.6 11.5 all-gather.34
  1755.8 84.5 reduce-scatter.22
  2185.3 83.9 all-gather.36
  2279.3 11.8 reduce-scatter.24
  2294.1 89.5 reduce-scatter.28
  2386.6 36.8 reduce-scatter.26
  2425.1 76.7 all-gather.26
  2508.0 134.8 all-reduce.74
  2645.5 443.9 all-reduce.76
  3091.6 76.6 all-gather.38
where the time goes:
time: 3210 us; the launch traced here: 3190 us
  waiting for transfers between devices  2040 us (64%)
  local copies, waits for them, and re-layouts  535 us (17%)
  other arithmetic  229 us (7%)
  matrix products  189 us (6%)
  blocking collectives  169 us (5%)
    reduce_scatter x4, waiting for transfers between devices, rows_then_cols(): lax.psum_scatter(product(gathered), 'col', scatter_dimension=0, tiled=True)  774 us
    all_gather x4, waiting for transfers between devices, cols_then_rows(): gathered = lax.all_gather(local, 'col', axis=0, tiled=True)  441 us
    unnamed x25, waiting for transfers between devices  425 us
    slice x60, local copies, waits for them, and re-layouts, body(): lax.associative_scan(compose, (decay_factor, decay_factor * d_state), rev...  165 us
    slice x55, local copies, waits for them, and re-layouts, body(): cum_decay, cum_state = lax.associative_scan(compose, (decay_factor, inject))  112 us
    all_gather x1, waiting for transfers between devices, body(): lax.all_gather(tokens, ('dp', 'row'), axis=0, tiled=True)  76.9 us
    all_gather x1, waiting for transfers between devices, body(): lax.all_gather(output, ('dp', 'row'), axis=0, tiled=True)  76.5 us
    psum x1, blocking collectives, body(): lax.psum((grad_gates, grad_gate_bias, grad_decay, grad_conv_w, grad_conv_...  76.3 us
  transfers between devices with their start and end apart: 26, of which 20 were waited for; matrix products, arithmetic and copies ran while one was open for 9% of the time, Pallas kernels for 0%

commit v1 on v0

v1 whole, which is shorter than its diff:
```python
import functools

import jax
import jax.numpy as jnp
from jax import lax
from jax.experimental import pallas as pl
from jax.experimental.pallas import tpu as pltpu
from jax.sharding import PartitionSpec as P

epsilon = 1e-06
LANES = 128
MESH = pl.DeviceIdType.MESH
low = jnp.bfloat16
f32 = jnp.float32


def gelu(values):
    return jax.nn.gelu(values, approximate=True)


def window_tile(col, tiles, n_col, wide):
    spare = wide * n_col - tiles
    return col * wide - jnp.maximum(col - (n_col - 1 - spare), 0)


def spare_window(col, tiles, n_col, wide):
    spare = wide * n_col - tiles
    return col > n_col - 1 - spare


def weights_kernel(
    geo, rec_in, rec_out, mlp_in, mlp_out, w_rec, w_out, w_in, w_down, send, recv, local
):
    n_col, part, bw, tiles, wide = geo
    col = lax.axis_index("col")
    barrier = pltpu.get_barrier_semaphore()
    for k in range(1, n_col):
        pl.semaphore_signal(
            barrier, inc=1, device_id={"col": lax.rem(col + k, n_col)}, device_id_type=MESH
        )
    pl.semaphore_wait(barrier, n_col - 1)
    shared = n_col * bw
    span = wide * LANES
    here = pl.ds(pl.multiple_of(col * part, LANES), part)

    def pieces(dest):
        blk = pl.multiple_of(dest * bw, LANES)
        tile = pl.multiple_of(shared + lax.div(dest, 2) * LANES, LANES)
        win = pl.multiple_of(window_tile(dest, tiles, n_col, wide) * LANES, LANES)
        return [
            (mlp_in.at[:, :, pl.ds(win, span)], w_in.at[:, here, :]),
            (mlp_out.at[pl.ds(win, span), :], w_down.at[:, here]),
            (rec_in.at[0, :, pl.ds(blk, bw)], w_rec.at[here, pl.ds(0, bw)]),
            (rec_in.at[0, :, pl.ds(shared, bw)], w_rec.at[here, pl.ds(bw, bw)]),
            (rec_in.at[1, :, pl.ds(blk, bw)], w_rec.at[here, pl.ds(2 * bw, bw)]),
            (rec_in.at[1, :, pl.ds(tile, LANES)], w_rec.at[here, pl.ds(3 * bw, LANES)]),
            (rec_out.at[pl.ds(blk, bw), :], w_out.at[pl.ds(0, bw), here]),
            (rec_out.at[pl.ds(tile, LANES), :], w_out.at[pl.ds(bw, LANES), here]),
        ]

    copies = []
    for k in range(1, n_col):
        dest = lax.rem(col + k, n_col)
        for i, (src, dst) in enumerate(pieces(dest)):
            copy = pltpu.make_async_remote_copy(
                src_ref=src,
                dst_ref=dst,
                send_sem=send.at[k - 1, i],
                recv_sem=recv.at[k - 1, i],
                device_id={"col": dest},
                device_id_type=MESH,
            )
            copy.start()
            copies.append(copy)
    for i, (src, dst) in enumerate(pieces(col)):
        copy = pltpu.make_async_copy(src, dst, local.at[i])
        copy.start()
        copies.append(copy)
    for copy in copies:
        copy.wait()


def gather_weights(rec_in, rec_out, mlp_in, mlp_out, n_col, bw, wide):
    part = rec_in.shape[1]
    width = part * n_col
    tiles = mlp_out.shape[0] // LANES
    span = wide * LANES
    geo = (n_col, part, bw, tiles, wide)
    anywhere = pl.BlockSpec(memory_space=pl.ANY)
    return pl.pallas_call(
        functools.partial(weights_kernel, geo),
        out_shape=(
            jax.ShapeDtypeStruct((width, 3 * bw + LANES), low),
            jax.ShapeDtypeStruct((bw + LANES, width), low),
            jax.ShapeDtypeStruct((2, width, span), low),
            jax.ShapeDtypeStruct((span, width), low),
        ),
        in_specs=[anywhere] * 4,
        out_specs=(anywhere,) * 4,
        scratch_shapes=[
            pltpu.SemaphoreType.DMA((n_col - 1, 8)),
            pltpu.SemaphoreType.DMA((n_col - 1, 8)),
            pltpu.SemaphoreType.DMA((8,)),
        ],
        compiler_params=pltpu.CompilerParams(collective_id=1, has_side_effects=True),
        name="weights",
    )(rec_in, rec_out, mlp_in, mlp_out)


def scan_kernel(reverse, a_ref, u_ref, h_ref, p_ref, carry):
    step = pl.program_id(0)
    rows = a_ref.shape[0]

    @pl.when(step == 0)
    def _():
        carry[0:1] = jnp.zeros_like(carry[0:1])
        carry[1:2] = jnp.ones_like(carry[1:2])

    for lane in range(a_ref.shape[1] // LANES):
        at = slice(lane * LANES, (lane + 1) * LANES)
        a = a_ref[:, at]
        u = u_ref[:, at]
        index = lax.broadcasted_iota(jnp.int32, a.shape, 0)
        by = 1
        while by < rows:
            turn = rows - by if reverse else by
            inside = index < rows - by if reverse else index >= by
            a_far = jnp.where(inside, pltpu.roll(a, turn, 0), 1.0)
            u_far = jnp.where(inside, pltpu.roll(u, turn, 0), 0.0)
            u = u + a * u_far
            a = a * a_far
            by *= 2
        h = u + a * carry[0:1, at]
        p = a * carry[1:2, at]
        h_ref[:, at] = h
        p_ref[:, at] = p
        edge = 0 if reverse else rows - 1
        carry[0:1, at] = h[edge : edge + 1]
        carry[1:2, at] = p[edge : edge + 1]


def scan_rows(decay, inject, reverse, rows=256):
    length, channels = decay.shape
    steps = length // rows
    block = pl.BlockSpec((rows, channels), lambda i: (steps - 1 - i if reverse else i, 0))
    shape = jax.ShapeDtypeStruct(decay.shape, f32)
    return pl.pallas_call(
        functools.partial(scan_kernel, reverse),
        grid=(steps,),
        out_shape=(shape, shape),
        in_specs=[block, block],
        out_specs=(block, block),
        scratch_shapes=[pltpu.VMEM((8, channels), f32)],
        name="scan_back" if reverse else "scan",
    )(decay, inject)


def outer_kernel(n_dp, left_ref, right_ref, out_ref):
    total = lax.dot_general(
        left_ref[...], right_ref[...], (((0,), (0,)), ((), ())), preferred_element_type=f32
    )
    rows = total.shape[0] // n_dp
    for k in range(n_dp):
        out_ref[k, 0] = total[k * rows : (k + 1) * rows].astype(out_ref.dtype)


def outer(left, right, n_dp, n_col, columns):
    length, width = left.shape
    part = width // n_col
    count = right.shape[1]
    return pl.pallas_call(
        functools.partial(outer_kernel, n_dp),
        grid=(n_col, count // columns),
        out_shape=jax.ShapeDtypeStruct((n_dp, n_col, part // n_dp, count), low),
        in_specs=[
            pl.BlockSpec((length, part), lambda i, j: (0, i)),
            pl.BlockSpec((length, columns), lambda i, j: (0, j)),
        ],
        out_specs=pl.BlockSpec((n_dp, 1, part // n_dp, columns), lambda i, j: (0, i, 0, j)),
        compiler_params=pltpu.CompilerParams(vmem_limit_bytes=48 * 1024 * 1024),
        cost_estimate=pl.CostEstimate(
            flops=2 * length * width * count,
            bytes_accessed=2 * (length * width + length * count + width * count),
            transcendentals=0,
        ),
        name="outer",
    )(left, right)


def deal_back(grads, n_col):
    summed = lax.psum_scatter(grads, "dp", scatter_dimension=0, tiled=False)
    return lax.all_to_all(summed, "col", 0, 0, tiled=False)


def gather_rows(local):
    return lax.all_gather(local, ("row", "col"), axis=0, tiled=True)


def scatter_rows(partial):
    return lax.psum_scatter(
        partial.astype(low), ("row", "col"), scatter_dimension=0, tiled=True
    ).astype(f32)


def dot(a, b, dims=((1,), (0,))):
    return lax.dot_general(a, b, (dims, ((), ())), preferred_element_type=f32)


def neighbour(x, axis, by):
    length = lax.axis_size(axis)
    pairs = [(i, i + by) for i in range(length) if 0 <= i + by < length]
    return lax.ppermute(x, axis, pairs)


def places_of(rows, lengths):
    ends = jnp.cumsum(lengths)
    starts = ends - lengths
    inside = (rows[:, None] >= starts[None, :]) & (rows[:, None] < ends[None, :])
    return rows - jnp.sum(jnp.where(inside, starts[None, :], 0), axis=1)


def lru_coeffs(pre_in, pre_rate, inputs, decay, reset):
    input_gate = jax.nn.sigmoid(pre_in)
    rate_gate = jax.nn.sigmoid(pre_rate)
    log_decay = -8.0 * rate_gate * jax.nn.softplus(decay)
    decay_factor = jnp.where(reset, 0.0, jnp.exp(log_decay))
    scaling = jnp.where(reset, 1.0, jnp.sqrt(-jnp.expm1(2.0 * log_decay)))
    return (decay_factor, inputs * input_gate * scaling)


def body(
    tokens,
    cotangent,
    rec_in,
    rec_out,
    gates,
    gate_bias,
    decay,
    conv_w,
    conv_b,
    gains,
    mlp_in,
    mlp_out,
    lengths,
    order,
):
    n_dp, n_row, n_col = (lax.axis_size(a) for a in ("dp", "row", "col"))
    dp, row, col = (lax.axis_index(a) for a in ("dp", "row", "col"))
    given, part = tokens.shape
    own = given // n_col
    group = given * n_row
    width = part * n_col
    taps = conv_w.shape[0]
    blocks, bw = gates.shape[1], gates.shape[2]
    half = rec_out.shape[0]
    hidden_half = mlp_out.shape[0]
    tiles = hidden_half // LANES
    wide = -(-tiles // n_col)
    span = wide * LANES
    shared = n_col * bw
    chans = bw + LANES

    w_rec, w_out, w_in, w_down = gather_weights(rec_in, rec_out, mlp_in, mlp_out, n_col, bw, wide)
    w_x, w_y = w_rec[:, : 2 * bw], w_rec[:, 2 * bw :]

    def own_rows(x):
        dealt = lax.all_to_all(x.reshape(n_col, own, part), "col", 0, 0)
        return dealt.transpose(1, 0, 2).reshape(own, width)

    def home_rows(x):
        dealt = lax.all_to_all(x.reshape(own, n_col, part).transpose(1, 0, 2), "col", 0, 0)
        return dealt.reshape(given, part)

    tile_at = shared + (col // 2) * LANES
    tile_owner = col % 2 == 0

    def own_channels(x):
        blk = lax.dynamic_slice_in_dim(x, col * bw, bw, axis=-1)
        tile = lax.dynamic_slice_in_dim(x, tile_at, LANES, axis=-1)
        return jnp.concatenate([blk, tile], axis=-1)

    def block_channels(x):
        blk = lax.dynamic_slice_in_dim(x, col * bw, bw, axis=-1)
        return jnp.concatenate([blk, x[..., shared:]], axis=-1)

    bias = own_channels(gate_bias)
    decay_o = own_channels(decay)
    conv_w_c = block_channels(conv_w)
    conv_b_c = block_channels(conv_b)
    conv_w_o = own_channels(conv_w)
    gates_blk = lax.dynamic_index_in_dim(gates, col, axis=1, keepdims=False)
    gates_five = gates[:, n_col]
    gates_tile = lax.dynamic_slice_in_dim(gates_five, (col // 2) * LANES, LANES, axis=2)
    gates_rows = lax.dynamic_slice_in_dim(gates_five, (col // 2) * LANES, LANES, axis=1)
    channel_ok = (jnp.arange(chans) < bw) | tile_owner
    hidden_ok = (jnp.arange(span) >= LANES) | ~spare_window(col, tiles, n_col, wide)

    base = dp * group
    places_ext = places_of(base + jnp.arange(group + taps - 1, dtype=jnp.int32), lengths)
    places = places_ext[:group]
    reset = (places == 0)[:, None]
    gains_all = lax.all_gather(gains, "col", axis=1, tiled=True)

    inputs = own_rows(tokens).astype(f32)
    upstream_low = own_rows(cotangent)
    upstream = upstream_low.astype(f32)
    sumsq_one = jnp.sum(inputs * inputs, axis=-1, keepdims=True)
    scale_one = lax.rsqrt(sumsq_one / width + epsilon)
    normed_one = (inputs * scale_one * gains_all[0]).astype(low)
    n1 = gather_rows(normed_one)
    n1_before = neighbour(n1[group - 16 :], "dp", 1)
    x_branch = dot(n1, w_x)
    y_branch = dot(n1, w_y)
    x_before = dot(n1_before, w_x)[16 - (taps - 1) :]
    x_ext = jnp.concatenate([x_before, x_branch], axis=0)
    mixed = conv_b_c[None, :] + jnp.zeros_like(x_branch)
    for t in range(taps):
        lagged = x_ext[taps - 1 - t : taps - 1 - t + group]
        mixed = mixed + jnp.where((places >= t)[:, None], conv_w_c[t][None, :] * lagged, 0.0)
    conv_low = mixed.astype(low)
    conv_blk, conv_five = conv_low[:, :bw], conv_low[:, bw:]
    conv_o = jnp.concatenate(
        [conv_blk, lax.dynamic_slice_in_dim(conv_five, (col // 2) * LANES, LANES, axis=1)], axis=1
    ).astype(f32)
    pre = [
        jnp.concatenate([dot(conv_blk, gates_blk[j]), dot(conv_five, gates_tile[j])], axis=1)
        + bias[j][None, :]
        for j in range(2)
    ]
    factor, inject = lru_coeffs(pre[0], pre[1], conv_o, decay_o, reset)
    local_state, since = scan_rows(factor, inject, False)
    state_in = neighbour(local_state[group - 8 :], "dp", 1)[7:]
    state = local_state + since * state_in
    branch = jnp.where(channel_ok, state * gelu(y_branch), 0.0).astype(low)
    out_one = scatter_rows(dot(branch, w_out))
    resid = inputs + out_one
    sumsq_two = jnp.sum(resid * resid, axis=-1, keepdims=True)
    scale_two = lax.rsqrt(sumsq_two / width + epsilon)
    normed_two = (resid * scale_two * gains_all[1]).astype(low)

    n2 = gather_rows(normed_two)
    gate_part = dot(n2, w_in[0])
    up_part = dot(n2, w_in[1])
    g_all = gather_rows(upstream_low)
    d_hidden = jnp.where(hidden_ok, dot(g_all, w_down, ((1,), (1,))), 0.0)
    hidden = jnp.where(hidden_ok, gelu(gate_part) * up_part, 0.0).astype(low)
    _, glu_back = jax.vjp(lambda gate_v, up_v: gelu(gate_v) * up_v, gate_part, up_part)
    d_gate, d_up = glu_back(d_hidden)
    d_glu = jnp.concatenate([d_gate.astype(low), d_up.astype(low)], axis=1)
    g_down = outer(g_all, hidden, n_dp, n_col, 512)
    g_in = outer(n2, d_glu, n_dp, n_col, 512)
    d_normed_two = scatter_rows(
        dot(d_glu[:, :span], w_in[0], ((1,), (1,))) + dot(d_glu[:, span:], w_in[1], ((1,), (1,)))
    )
    out_two = scatter_rows(dot(hidden, w_down))
    result = (resid + out_two).astype(low)

    gained_two = gains_all[1] * d_normed_two
    inner_two = jnp.sum(gained_two * resid, axis=-1, keepdims=True)
    grad_gain_two = jnp.sum(d_normed_two * resid * scale_two, axis=0)
    d_resid = upstream + scale_two * gained_two - resid * scale_two**3 * (inner_two / width)
    d_out = gather_rows(d_resid.astype(low))

    d_branch = jnp.where(channel_ok, dot(d_out, w_out, ((1,), (1,))), 0.0)
    g_out = outer(d_out, branch, n_dp, n_col, chans)
    _, mix_back = jax.vjp(lambda state_v, gate_v: state_v * gelu(gate_v), state, y_branch)
    d_state, d_y = mix_back(d_branch)
    message, until = scan_rows(factor, factor * d_state, True)
    message_in = neighbour(message[:8], "dp", -1)[:1]
    message = message + until * message_in
    grad_state = d_state + jnp.concatenate([message[1:], message_in], axis=0)
    state_prev = jnp.concatenate([state_in, state[:-1]], axis=0)
    _, coef_back = jax.vjp(
        lambda a, b, c, d: lru_coeffs(a, b, c, d, reset), pre[0], pre[1], conv_o, decay_o
    )
    d_pre_in, d_pre_rate, d_conv, g_decay = coef_back((grad_state * state_prev, grad_state))
    d_pre = [d_pre_in.astype(low), d_pre_rate.astype(low)]
    tiles_here = jnp.concatenate([d[:, bw:] for d in d_pre], axis=1)
    tiles_there = lax.ppermute(tiles_here, "col", [(i, i ^ 2) for i in range(n_col)])
    low_half = col // 2 == 0
    d_conv_parts = []
    d_five = []
    for j in range(2):
        here = d_pre[j][:, bw:]
        there = tiles_there[:, j * LANES : (j + 1) * LANES]
        d_five.append(
            jnp.where(
                low_half,
                jnp.concatenate([here, there], axis=1),
                jnp.concatenate([there, here], axis=1),
            )
        )
        d_conv_parts.append(
            jnp.concatenate(
                [
                    dot(d_pre[j][:, :bw], gates_blk[j], ((1,), (1,))),
                    dot(d_five[j], gates_rows[j], ((1,), (1,))),
                ],
                axis=1,
            )
        )
    d_conv = d_conv + d_conv_parts[0] + d_conv_parts[1]
    g_gates = jnp.stack(
        [
            jnp.concatenate(
                [
                    dot(conv_blk, d_pre[j][:, :bw], ((0,), (0,))),
                    dot(conv_five, d_pre[j][:, bw:], ((0,), (0,))),
                ],
                axis=1,
            )
            for j in range(2)
        ]
    )
    g_bias = [jnp.sum(d.astype(f32), axis=0) for d in d_pre]
    later = neighbour(d_conv[:8], "dp", -1)[: taps - 1]
    d_ext = jnp.concatenate([d_conv, later], axis=0)
    x_own = jnp.concatenate(
        [x_ext[:, :bw], lax.dynamic_slice_in_dim(x_ext, bw + (col // 2) * LANES, LANES, axis=1)],
        axis=1,
    )
    d_x = jnp.zeros_like(d_conv)
    g_taps = []
    for t in range(taps):
        ahead = d_ext[t : t + group]
        valid = (places_ext[t : t + group] >= t)[:, None]
        d_x = d_x + jnp.where(valid, conv_w_o[t][None, :] * ahead, 0.0)
        lagged = x_own[taps - 1 - t : taps - 1 - t + group]
        g_taps.append(jnp.sum(jnp.where((places >= t)[:, None], d_conv * lagged, 0.0), axis=0))
    g_conv_b = jnp.sum(d_conv, axis=0)
    d_x_low = jnp.where(channel_ok, d_x, 0.0).astype(low)
    d_y_low = jnp.where(channel_ok, d_y, 0.0).astype(low)
    d_rec = jnp.concatenate([d_x_low, d_y_low], axis=1)
    w_x_own = jnp.concatenate(
        [w_x[:, :bw], lax.dynamic_slice_in_dim(w_x, bw + (col // 2) * LANES, LANES, axis=1)], axis=1
    )
    d_normed_one = scatter_rows(
        dot(d_x_low, w_x_own, ((1,), (1,))) + dot(d_y_low, w_y, ((1,), (1,)))
    )
    g_rec = outer(n1, d_rec, n_dp, n_col, chans)
    gained_one = gains_all[0] * d_normed_one
    inner_one = jnp.sum(gained_one * inputs, axis=-1, keepdims=True)
    grad_gain_one = jnp.sum(d_normed_one * inputs * scale_one, axis=0)
    d_input = d_resid + scale_one * gained_one - inputs * scale_one**3 * (inner_one / width)

    result = home_rows(result)
    grad_input = home_rows(d_input.astype(low))

    def windows(got, first):
        return [
            got[c][..., first + (LANES if c > n_col - 1 - (wide * n_col - tiles) else 0) : first + span]
            for c in range(n_col)
        ]

    def channels_of(got, first):
        return [got[c][..., first : first + bw] for c in range(n_col)] + [
            got[c][..., first + bw : first + chans] for c in range(0, n_col, 2)
        ]

    down = deal_back(g_down, n_col)
    grad_mlp_out = jnp.concatenate(windows(down, 0), axis=-1).astype(f32).T
    into = deal_back(g_in, n_col)
    grad_mlp_in = jnp.stack(
        [jnp.concatenate(windows(into[..., j * span : (j + 1) * span], 0), axis=-1) for j in range(2)]
    ).astype(f32)
    outs = deal_back(g_out, n_col)
    grad_rec_out = jnp.concatenate(channels_of(outs, 0), axis=-1).astype(f32).T
    recs = deal_back(g_rec, n_col)
    grad_rec_in = jnp.stack(
        [jnp.concatenate(channels_of(recs, j * chans), axis=-1) for j in range(2)]
    ).astype(f32)

    gate_parts = lax.all_gather(lax.psum(g_gates.astype(low), "dp"), "col", axis=0).astype(f32)
    five = jnp.concatenate([gate_parts[c, :, :, bw:] for c in range(0, n_col, 2)], axis=-1)
    grad_gates = jnp.stack([gate_parts[c, :, :, :bw] for c in range(n_col)] + [five], axis=1)

    small = jnp.where(channel_ok, jnp.stack(g_bias + [g_decay] + g_taps + [g_conv_b]), 0.0)
    placed = jnp.zeros((small.shape[0], n_row * half), f32)
    placed = lax.dynamic_update_slice(placed, small[:, :bw], (0, row * half + col * bw))
    tile_spot = (0, row * half + tile_at)
    placed = lax.dynamic_update_slice(placed, small[:, bw:], tile_spot)
    square_sums = jnp.stack(
        [jnp.sum(sumsq_one), jnp.sum(out_one * out_one), jnp.sum(sumsq_two), jnp.sum(out_two * out_two)]
    )
    stat_row = jnp.pad(square_sums, (0, width - 4))[None, :]
    rows_all = jnp.concatenate(
        [placed, grad_gain_one[None, :], grad_gain_two[None, :], stat_row], axis=0
    )
    sums = lax.psum(rows_all, ("dp", "row", "col"))
    mine = lax.dynamic_slice_in_dim(sums[:8], row * half, half, axis=1)
    grad_gains = lax.dynamic_slice_in_dim(sums[8:10], col * part, part, axis=1)
    stats = jnp.sqrt(sums[10, :4] / (n_dp * group * width))
    return (
        result,
        grad_input,
        grad_rec_in,
        grad_rec_out,
        grad_gates,
        mine[0:2],
        mine[2],
        mine[3 : 3 + taps],
        mine[3 + taps],
        grad_gains,
        grad_mlp_in,
        grad_mlp_out,
        stats,
    )


def solution(mesh):
    placed = (
        P(("dp", "row"), "col"),
        P(("dp", "row"), "col"),
        P(None, "col", "row"),
        P("row", "col"),
        P(None, "row", None, None),
        P(None, "row"),
        P("row"),
        P(None, "row"),
        P("row"),
        P(None, "col"),
        P(None, "col", "row"),
        P("row", "col"),
        P(),
        P(),
    )
    return jax.shard_map(
        body,
        mesh=mesh,
        in_specs=placed,
        out_specs=(
            P(("dp", "row"), "col"),
            P(("dp", "row"), "col"),
            P(None, ("col", "dp"), "row"),
            P("row", ("col", "dp")),
            P(None, "row", None, None),
            P(None, "row"),
            P("row"),
            P(None, "row"),
            P("row"),
            P(None, "col"),
            P(None, ("col", "dp"), "row"),
            P("row", ("col", "dp")),
            P(),
        ),
        check_vma=False,
    )
```

time: 3210 us -> 1580 us (0.49)
  waiting for transfers between devices: 2040 us -> 817 us
  local copies, waits for them, and re-layouts: 535 us -> 53.7 us
  Pallas kernels: 0 us -> 350 us
  other arithmetic: 229 us -> 87.7 us
  blocking collectives: 169 us -> 54.1 us
  matrix products: 189 us -> 153 us
    all_gather x12 -> x5, waiting for transfers between devices: 755 us -> 116 us  [the longest x4 116 us: gather_rows(): return lax.all_gather(local, ('row', 'col'), axis=0, tiled=True)]
    unnamed x25 -> x15, waiting for transfers between devices: 425 us -> 0.24 us
    pallas_call x0 -> x7, Pallas kernels: none -> 350 us  [the longest x1 272 us: gather_weights(): pl.pallas_call(functools.partial(weights_kernel, geo), out_shape=(jax.Sha...]
    reduce_scatter x10 -> x8, waiting for transfers between devices: 798 us -> 514 us  [the longest x4 265 us: scatter_rows(): lax.psum_scatter(partial.astype(low), ('row', 'col'), scatter_dimension=0...]
    slice x119 -> x26, local copies, waits for them, and re-layouts: 279 us -> 14.9 us  [the longest x1 1.91 us: body(): w_x, w_y = (w_rec[:, :2 * bw], w_rec[:, 2 * bw:])]
    psum x6 -> x0, blocking collectives: 138 us -> none  [the longest x1 76.3 us: body(): lax.psum((grad_gates, grad_gate_bias, grad_decay, grad_conv_w, grad_conv_...]
    pad x60 -> x0, local copies, waits for them, and re-layouts: 122 us -> none  [the longest x30 61.3 us: body(): cum_decay, cum_state = lax.associative_scan(compose, (decay_factor, inject))]
    add x64 -> x2, other arithmetic: 91.4 us -> 2.99 us  [the longest x1 2.99 us: body(): message = message + until * message_in]
  transfers between devices with their start and end apart: 26 -> 26, of which waited for: 20 -> 20; matrix products, arithmetic and copies ran while one was open for 9% -> 9% of each run, Pallas kernels for 0% -> 21%
where the time goes in v1:
time: 1580 us; the launch traced here: 1570 us
  waiting for transfers between devices  817 us (52%)
  Pallas kernels  350 us (22%)
  matrix products  153 us (10%)
  other arithmetic  87.7 us (6%)
  blocking collectives  54.1 us (3%)
  local copies, waits for them, and re-layouts  53.7 us (3%)
  starting transfers between devices  36.7 us (2%)
    pallas_call x1, Pallas kernels, gather_weights(): pl.pallas_call(functools.partial(weights_kernel, geo), out_shape=(jax.Sha...  272 us
    reduce_scatter x4, waiting for transfers between devices, scatter_rows(): lax.psum_scatter(partial.astype(low), ('row', 'col'), scatter_dimension=0...  265 us
    reduce_scatter x4, waiting for transfers between devices, deal_back(): summed = lax.psum_scatter(grads, 'dp', scatter_dimension=0, tiled=False)  250 us
    dot_general x25, matrix products, dot(): return lax.dot_general(a, b, (dims, ((), ())), preferred_element_type=f32)  153 us
    all_gather x4, waiting for transfers between devices, gather_rows(): return lax.all_gather(local, ('row', 'col'), axis=0, tiled=True)  116 us
    psum x1, waiting for transfers between devices, body(): sums = lax.psum(rows_all, ('dp', 'row', 'col'))  112 us
    pallas_call x4, Pallas kernels, outer(): pl.pallas_call(functools.partial(outer_kernel, n_dp), grid=(n_col, count...  63.4 us
    all_to_all x3, waiting for transfers between devices, deal_back(): return lax.all_to_all(summed, 'col', 0, 0, tiled=False)  48.4 us
  transfers between devices with their start and end apart: 26, of which 20 were waited for; matrix products, arithmetic and copies ran while one was open for 9% of the time, Pallas kernels for 21%

profile of v1, /device:TPU:0, one launch (start us, length us, event | category | flops | bytes accessed | tf_op | source)
XLA Modules:
  0.0 1567.8 jit_solution(5289877895840721791)
XLA Ops:
  12.4 16.1 %all_gather.21 = f32[2,2560]{1,0:T(2,128)S(1)} all-gather(f32[2,640]{1,0:T(2,128)} %param.23), channel_id=1, replica_groups=mesh['dp'=4,'row'=2,'col'=4] {'col'}, dimensions={1}, use_global_device_ids=true | all-gather | bytes 25600 | tf_op jit(solution)/shard_map/all_gather | solution.py:302
  35.2 272.0 %weights.1 = (bf16[2560,896]{1,0:T(8,128)(2,1)}, bf16[384,2560]{1,0:T(8,128)(2,1)}, bf16[2,2560,1024]{2,1,0:T(8,128)(2,1)}, bf16[1024,2560]{1,0:T(8,128)(2,1)}) custom-call(bf16[2,640,1280]{2,1,0:T(8,128)(2,1)} %rec_in.1, bf16[1280,640]{1,0:T(8,128)(2,1)} %rec_out.1, bf16[2,640,3840]{2,1,0:T(8,128)(2,1)} %mlp_in.1, bf16[3840,640]{1,0:T(8,128)(2,1)} %mlp_out.1), custom_call_target="tpu_custom_call" | custom-call | tf_op jit(solution)/shard_map/weights/pallas_call | solution.py:90
  368.3 70.1 %reduce-scatter.9.cloned.1.call-done = bf16[192,2560]{1,0:T(8,128)(2,1)} async-done(((bf16[1536,2560]{1,0:T(8,128)(2,1)}), bf16[192,2560]{1,0:T(8,128)(2,1)}) %reduce-scatter.9.cloned.1.call-update) | async-done | bytes 983056 | tf_op jit(solution)/shard_map/reduce_scatter | solution.py:200
  443.6 22.2 %all_to_all.40 = bf16[4,192,640]{2,1,0:T(8,128)(2,1)S(1)} all-to-all(bf16[4,192,640]{2,1,0:T(8,128)(2,1)S(1)} %bitcast.193), channel_id=1, replica_groups=mesh['dp'=4,'row'=2,'col'=4] {'col'}, dimensions={0} | all-to-all | bytes 1966080 | tf_op jit(solution)/shard_map/all_to_all | solution.py:267
  467.4 33.0 %all-gather.8.cloned.1.call-done.left_ref = bf16[1536,2560]{1,0:T(8,128)(2,1)} async-done(((bf16[192,2560]{1,0:T(8,128)(2,1)}), bf16[1536,2560]{1,0:T(8,128)(2,1)}) %all-gather.8.cloned.1.call-update) | async-done | bytes 7864336 | tf_op jit(solution)/shard_map/all_gather | solution.py:196
  500.4 14.0 fusion.9
  524.8 30.3 %all-gather.10.cloned.1.call-done.left_ref = bf16[1536,2560]{1,0:T(8,128)(2,1)} async-done(((bf16[192,2560]{1,0:T(8,128)(2,1)}), bf16[1536,2560]{1,0:T(8,128)(2,1)}) %all-gather.10.cloned.1.call-update) | async-done | bytes 7864336 | tf_op jit(solution)/shard_map/all_gather | solution.py:196
  555.1 19.6 %fusion.7 = (bf16[1536,1024]{1,0:T(8,128)(2,1)S(1)}, bf16[1536,1024]{1,0:T(8,128)(2,1)S(1)}, bf16[1536,1024]{1,0:T(8,128)(2,1)S(1)}) fusion(pred[1024]{0:T(1024)(128)(4,1)S(1)} %fusion.158, f32[1536,1024]{1,0:T(8,128)} %fusion.13, f32[1536,1024]{1,0:T(8,128)} %fusion.9, bf16[1024,2560]{1,0:T(8,128)(2,1)} %get-tuple-element.26, ...), kind=kOutput, calls=%fused_computation.21 | convolution fusion | flops 8097103872 | bytes 35128320 | tf_op jit(solution)/shard_map/dot_general | solution.py:206
  574.7 15.9 %fusion.11 = f32[1536,2560]{1,0:T(8,128)} fusion(bf16[1536,1024]{1,0:T(8,128)(2,1)S(1)} %get-tuple-element.118, bf16[2,2560,1024]{2,1,0:T(8,128)(2,1)} %get-tuple-element.25), kind=kOutput, calls=%fused_computation.27 | convolution fusion | flops 8053063680 | bytes 24117248 | tf_op jit(solution)/shard_map/dot_general | solution.py:206
  590.6 14.9 add_convert_fusion.1
  605.5 69.5 %reduce-scatter.13.cloned.1.call-done = bf16[192,2560]{1,0:T(8,128)(2,1)} async-done(((bf16[1536,2560]{1,0:T(8,128)(2,1)}), bf16[192,2560]{1,0:T(8,128)(2,1)}) %reduce-scatter.13.cloned.1.call-update) | async-done | bytes 983056 | tf_op jit(solution)/shard_map/reduce_scatter | solution.py:200
  682.2 52.3 %all-gather.12.cloned.1.call-done.left_ref = bf16[1536,2560]{1,0:T(8,128)(2,1)} async-done(((bf16[192,2560]{1,0:T(8,128)(2,1)}), bf16[1536,2560]{1,0:T(8,128)(2,1)}) %all-gather.12.cloned.1.call-update) | async-done | bytes 7864336 | tf_op jit(solution)/shard_map/all_gather | solution.py:196
  786.8 13.9 outer.7
  807.4 27.9 %outer.6 = bf16[4,4,160,2048]{3,2,1,0:T(8,128)(2,1)} custom-call(bf16[1536,2560]{1,0:T(8,128)(2,1)} %all-gather.8.cloned.1.call-done.left_ref, bf16[1536,2048]{1,0:T(8,128)(2,1)} %pad_maximum_fusion.right_ref), custom_call_target="tpu_custom_call" | custom-call | flops 16106127360 | bytes 24641536 | tf_op jit(solution)/shard_map/outer/pallas_call | solution.py:171
  885.7 13.7 outer.4
  921.3 12.7 convolution_convert_fusion
  934.0 15.8 %all_to_all.41 = bf16[4,160,1024]{2,1,0:T(8,128)(2,1)} all-to-all(bf16[4,160,1024]{2,1,0:T(8,128)(2,1)} %bitcast.191), channel_id=1, replica_groups=mesh['dp'=4,'row'=2,'col'=4] {'col'}, dimensions={0} | all-to-all | bytes 2621440 | tf_op jit(solution)/shard_map/all_to_all | solution.py:192
  949.7 150.3 %reduce-scatter.21.cloned.1.call-done = bf16[1,4,160,2048]{3,2,1,0:T(8,128)(2,1)} async-done(((bf16[4,4,160,2048]{3,2,1,0:T(8,128)(2,1)}), bf16[1,4,160,2048]{3,2,1,0:T(8,128)(2,1)}) %reduce-scatter.21.cloned.1.call-update) | async-done | bytes 2621456 | tf_op jit(solution)/shard_map/reduce_scatter | solution.py:191
  1107.5 34.1 %all-to-all-done.6 = bf16[4,160,2048]{2,1,0:T(8,128)(2,1)S(1)} async-done(((bf16[4,160,2048]{2,1,0:T(8,128)(2,1)}), bf16[4,160,2048]{2,1,0:T(8,128)(2,1)S(1)}, u32[]{:S(2)}, u32[]{:S(2)}) %all-to-all-start.6) | async-done | bytes 2621472 | tf_op jit(solution)/shard_map/all_to_all | solution.py:192
  1152.5 38.9 %reduce-scatter.19.cloned.1.call-done = bf16[1,4,160,384]{3,2,1,0:T(8,128)(2,1)} async-done(((bf16[4,4,160,384]{3,2,1,0:T(8,128)(2,1)}), bf16[1,4,160,384]{3,2,1,0:T(8,128)(2,1)}) %reduce-scatter.19.cloned.1.call-update) | async-done | bytes 491536 | tf_op jit(solution)/shard_map/reduce_scatter | solution.py:191
  1205.2 60.5 %reduce-scatter.17.cloned.1.call-done = bf16[1,4,160,768]{3,2,1,0:T(8,128)(2,1)} async-done(((bf16[4,4,160,768]{3,2,1,0:T(8,128)(2,1)}), bf16[1,4,160,768]{3,2,1,0:T(8,128)(2,1)}) %reduce-scatter.17.cloned.1.call-update) | async-done | bytes 983056 | tf_op jit(solution)/shard_map/reduce_scatter | solution.py:191
  1285.1 54.2 %reduce-scatter.15.cloned.1.call-done = bf16[192,2560]{1,0:T(8,128)(2,1)} async-done(((bf16[1536,2560]{1,0:T(8,128)(2,1)}), bf16[192,2560]{1,0:T(8,128)(2,1)}) %reduce-scatter.15.cloned.1.call-update) | async-done | bytes 983056 | tf_op jit(solution)/shard_map/reduce_scatter | solution.py:200
  1341.1 70.9 %reduce-scatter.11.cloned.1.call-done = bf16[192,2560]{1,0:T(8,128)(2,1)} async-done(((bf16[1536,2560]{1,0:T(8,128)(2,1)}), bf16[192,2560]{1,0:T(8,128)(2,1)}) %reduce-scatter.11.cloned.1.call-update) | async-done | bytes 983056 | tf_op jit(solution)/shard_map/reduce_scatter | solution.py:200
  1441.4 112.3 %all-reduce.6.cloned.1.call-done = f32[11,2560]{1,0:T(8,128)} async-done(((f32[11,2560]{1,0:T(8,128)}), f32[11,2560]{1,0:T(8,128)}) %all-reduce.6.cloned.1.call-update) | async-done | bytes 112656 | tf_op jit(solution)/shard_map/psum | solution.py:489
  (412 shorter events, 317.5 us)
Async XLA Ops:
  7.2 21.4 %all-to-all-start = ((bf16[4,192,640]{2,1,0:T(8,128)(2,1)}), bf16[4,192,640]{2,1,0:T(8,128)(2,1)S(1)}, u32[]{:S(2)}, u32[]{:S(2)}) async-start(bf16[4,192,640]{2,1,0:T(8,128)(2,1)} %bitcast.192), calls=%async_computation | async-start | bytes 1966080 | tf_op jit(solution)/shard_map/all_to_all | solution.py:267
  12.4 298.4 %all-gather.6.cloned.1.call-start = ((), (), s32[]{:S(2)}) async-start(), calls=%async_computation.16 | async-start | bytes 8847360 | tf_op jit(solution)/shard_map/all_gather | solution.py:196
  32.3 406.1 %reduce-scatter.9.cloned.1.call-start = ((), (), s32[]{:S(2)}) async-start(), calls=%async_computation.17 | async-start | bytes 8847360 | tf_op jit(solution)/shard_map/reduce_scatter | solution.py:200
  311.7 11.0 collective-permute-start
  368.3 132.1 %all-gather.8.cloned.1.call-start = ((), (), s32[]{:S(2)}) async-start(), calls=%async_computation.18 | async-start | bytes 8847360 | tf_op jit(solution)/shard_map/all_gather | solution.py:196
  443.5 111.6 %all-gather.10.cloned.1.call-start = ((), (), s32[]{:S(2)}) async-start(), calls=%async_computation.20 | async-start | bytes 8847360 | tf_op jit(solution)/shard_map/all_gather | solution.py:196
  466.8 208.2 %reduce-scatter.13.cloned.1.call-start = ((), (), s32[]{:S(2)}) async-start(), calls=%async_computation.21 | async-start | bytes 8847360 | tf_op jit(solution)/shard_map/reduce_scatter | solution.py:200
  605.5 129.0 %all-gather.12.cloned.1.call-start = ((), (), s32[]{:S(2)}) async-start(), calls=%async_computation.22 | async-start | bytes 8847360 | tf_op jit(solution)/shard_map/all_gather | solution.py:196
  682.1 153.3 %all-reduce.4.cloned.1.call-start = ((), (), s32[]{:S(2)}) async-start(), calls=%async_computation.26 | async-start | bytes 786432 | tf_op jit(solution)/shard_map/psum | solution.py:473
  786.7 147.2 %reduce-scatter.23.cloned.1.call-start = ((), (), s32[]{:S(2)}) async-start(), calls=%async_computation.30 | async-start | bytes 6553600 | tf_op jit(solution)/shard_map/reduce_scatter | solution.py:191
  800.7 299.3 %reduce-scatter.21.cloned.1.call-start = ((), (), s32[]{:S(2)}) async-start(), calls=%async_computation.29 | async-start | bytes 13107200 | tf_op jit(solution)/shard_map/reduce_scatter | solution.py:191
  835.4 312.0 %all-gather.14.cloned.1.call-start = ((), (), s32[]{:S(2)}) async-start(), calls=%async_computation.27 | async-start | bytes 1966080 | tf_op jit(solution)/shard_map/all_gather | solution.py:473
  837.4 354.0 %reduce-scatter.19.cloned.1.call-start = ((), (), s32[]{:S(2)}) async-start(), calls=%async_computation.25 | async-start | bytes 2457600 | tf_op jit(solution)/shard_map/reduce_scatter | solution.py:191
  844.6 19.0 %collective-permute-start.3 = (bf16[1536,256]{1,0:T(8,128)(2,1)}, bf16[1536,256]{1,0:T(8,128)(2,1)}, u32[]{:S(2)}, u32[]{:S(2)}) collective-permute-start(bf16[1536,256]{1,0:T(8,128)(2,1)} %pad_maximum_fusion.6), channel_id=1, source_target_pairs={{0,2},{1,3},{2,0},{3,1},{4,6},{5,7},{6,4},{7,5},{8,10},{9,11},{10,... | collective-permute-start | bytes 2359304 | tf_op jit(solution)/shard_map/ppermute | solution.py:379
  853.7 411.9 %reduce-scatter.17.cloned.1.call-start = ((), (), s32[]{:S(2)}) async-start(), calls=%async_computation.24 | async-start | bytes 4915200 | tf_op jit(solution)/shard_map/reduce_scatter | solution.py:191
  871.6 9.6 collective-permute-start.4
  899.4 439.9 %reduce-scatter.15.cloned.1.call-start = ((), (), s32[]{:S(2)}) async-start(), calls=%async_computation.23 | async-start | bytes 8847360 | tf_op jit(solution)/shard_map/reduce_scatter | solution.py:200
  921.2 490.8 %reduce-scatter.11.cloned.1.call-start = ((), (), s32[]{:S(2)}) async-start(), calls=%async_computation.19 | async-start | bytes 8847360 | tf_op jit(solution)/shard_map/reduce_scatter | solution.py:200
  1100.0 41.6 %all-to-all-start.6 = ((bf16[4,160,2048]{2,1,0:T(8,128)(2,1)}), bf16[4,160,2048]{2,1,0:T(8,128)(2,1)S(1)}, u32[]{:S(2)}, u32[]{:S(2)}) async-start(bf16[4,160,2048]{2,1,0:T(8,128)(2,1)} %bitcast.190), calls=%async_computation.13 | async-start | bytes 5242880 | tf_op jit(solution)/shard_map/all_to_all | solution.py:192
  1191.4 12.0 all-to-all-start.5
  1265.7 16.5 %all-to-all-start.4 = ((bf16[4,160,768]{2,1,0:T(8,128)(2,1)}), bf16[4,160,768]{2,1,0:T(8,128)(2,1)S(1)}, u32[]{:S(2)}, u32[]{:S(2)}) async-start(bf16[4,160,768]{2,1,0:T(8,128)(2,1)} %bitcast.194), calls=%async_computation.9 | async-start | bytes 1966080 | tf_op jit(solution)/shard_map/all_to_all | solution.py:192
  1418.7 16.7 %all-to-all-start.1 = ((bf16[4,192,640]{2,1,0:T(8,128)(2,1)}), bf16[4,192,640]{2,1,0:T(8,128)(2,1)S(1)}, u32[]{:S(2)}, u32[]{:S(2)}) async-start(bf16[4,192,640]{2,1,0:T(8,128)(2,1)} %bitcast.175), calls=%async_computation.3 | async-start | bytes 1966080 | tf_op jit(solution)/shard_map/all_to_all | solution.py:271
  1422.3 131.4 %all-reduce.6.cloned.1.call-start = ((), (), s32[]{:S(2)}) async-start(), calls=%async_computation.28 | async-start | bytes 327680 | tf_op jit(solution)/shard_map/psum | solution.py:489
  1435.4 123.8 %all-to-all-start.3 = ((bf16[4,192,640]{2,1,0:T(8,128)(2,1)}), bf16[4,192,640]{2,1,0:T(8,128)(2,1)S(1)}, u32[]{:S(2)}, u32[]{:S(2)}) async-start(bf16[4,192,640]{2,1,0:T(8,128)(2,1)} %bitcast.173), calls=%async_computation.7 | async-start | bytes 1966080 | tf_op jit(solution)/shard_map/all_to_all | solution.py:271
  (101 other events, 3330.4 us)
Sparse Core Ops, SparseCore 0:
  32.4 196.3 all-gather.5
  368.4 69.9 reduce-scatter.8
  443.6 56.7 all-gather.7
  502.9 52.1 all-gather.9
  605.6 69.3 reduce-scatter.12
  682.3 52.1 all-gather.11
  786.8 36.1 all-reduce.3
  825.4 93.5 reduce-scatter.22
  921.5 178.4 reduce-scatter.20
  1101.8 45.5 all-gather.13
  1149.9 41.5 reduce-scatter.18
  1193.7 71.9 reduce-scatter.16
  1269.5 69.7 reduce-scatter.14
  1342.6 69.3 reduce-scatter.10
  1429.3 124.3 all-reduce.5

commit v2 on v1

v2 whole, which is shorter than its diff:
```python
import functools

import jax
import jax.numpy as jnp
from jax import lax
from jax.experimental import pallas as pl
from jax.experimental.pallas import tpu as pltpu
from jax.sharding import PartitionSpec as P

epsilon = 1e-06
LANES = 128
ROWS = 16
MIB = 1024 * 1024
MESH = pl.DeviceIdType.MESH
low = jnp.bfloat16
f32 = jnp.float32
anywhere = pl.BlockSpec(memory_space=pl.ANY)
in_vmem = pl.BlockSpec(memory_space=pltpu.VMEM)


def gelu(values):
    return jax.nn.gelu(values, approximate=True)


def window_tile(col, tiles, n_col, wide):
    spare = wide * n_col - tiles
    return col * wide - jnp.maximum(col - (n_col - 1 - spare), 0)


def spare_window(col, tiles, n_col, wide):
    spare = wide * n_col - tiles
    return col > n_col - 1 - spare


class Place:
    def __init__(self):
        self.dp, self.row, self.col = (lax.axis_index(a) for a in ("dp", "row", "col"))

    def chip(self, k):
        return jnp.bitwise_xor(self.col, k)

    def device(self, name):
        if name == "core":
            return {"row": 1 - self.row}
        if name == "z":
            return {"dp": jnp.bitwise_xor(self.dp, 1)}
        if name in ("next", "prev"):
            n_dp = lax.axis_size("dp")
            return {"dp": lax.rem(self.dp + (1 if name == "next" else n_dp - 1), n_dp)}
        if name[0] == "d":
            return {"dp": jnp.bitwise_xor(self.dp, int(name[1:]))}
        return {"col": self.chip({"x": 1, "y": 2, "xy": 3}[name])}

    def meet(self, names):
        barrier = pltpu.get_barrier_semaphore()
        for name in names:
            pl.semaphore_signal(
                barrier, inc=1, device_id=self.device(name), device_id_type=MESH
            )
        pl.semaphore_wait(barrier, len(names))


class Copies:
    def __init__(self, place, send, recv):
        self.place, self.send, self.recv = place, send, recv
        self.made, self.landed, self.left, self.local = [], set(), set(), []

    def start(self, src, dst, to):
        i = len(self.made)
        copy = pltpu.make_async_remote_copy(
            src_ref=src,
            dst_ref=dst,
            send_sem=self.send.at[i],
            recv_sem=self.recv.at[i],
            device_id=self.place.device(to),
            device_id_type=MESH,
        )
        copy.start()
        self.made.append(copy)
        return i

    def land(self, *numbers):
        for i in numbers:
            if i not in self.landed:
                self.made[i].wait_recv()
                self.landed.add(i)

    def leave(self, *numbers):
        for i in numbers:
            if i not in self.left:
                self.made[i].wait_send()
                self.left.add(i)

    def keep(self, src, dst, sem):
        copy = pltpu.make_async_copy(src, dst, sem)
        copy.start()
        self.local.append(copy)
        return copy

    def finish(self):
        self.land(*range(len(self.made)))
        self.leave(*range(len(self.made)))


def share(rows):
    far = rows * 9 // 20 // ROWS * ROWS
    return rows - far, far


class Dealer:
    def __init__(self, copies):
        self.copies = copies
        self.waiting = []

    def deal(self, piece):
        place = self.copies.place
        odd = lax.rem(place.dp, 2)
        batch = []
        for name, k in (("x", 1), ("y", 2), ("xy", 3)):
            src, dst, rows = piece(place.chip(k), place.col)
            near, far = share(rows)
            start = pl.multiple_of(odd * far, ROWS)
            at = pl.ds(start, near)
            number = self.copies.start(src(at), dst(at), name)
            batch.append((k, number, piece))
        self.waiting.append(batch)

    def forward(self):
        place = self.copies.place
        odd = lax.rem(place.dp, 2)
        for k, number, piece in self.waiting.pop(0):
            self.copies.land(number)
            _, dst, rows = piece(place.col, place.chip(k))
            near, far = share(rows)
            at = pl.ds(pl.multiple_of(odd * near, ROWS), far)
            self.copies.start(dst(at), dst(at), "z")


def rows_of(ref, first, rows, lead=None, columns=None):
    def view(at):
        where = pl.ds(pl.multiple_of(first + at.start, ROWS), at.size)
        index = (where, columns if columns is not None else slice(None))
        return ref.at[index] if lead is None else ref.at[(lead,) + index]

    return view


def weight_pieces(geo, refs, outs):
    n_col, part, bw, tiles, wide = geo
    shared, span = n_col * bw, wide * LANES
    rec_in, rec_out, mlp_in, mlp_out = refs
    w_rec, w_out, w_in, w_down = outs

    def here(chip):
        return pl.multiple_of(chip * part, LANES)

    def blk(chip):
        return pl.multiple_of(chip * bw, LANES)

    def tile(chip):
        return pl.multiple_of(shared + lax.div(chip, 2) * LANES, LANES)

    def win(chip):
        return pl.multiple_of(window_tile(chip, tiles, n_col, wide) * LANES, LANES)

    def in_piece(ref, j, out, lead, source_at, size, column):
        def piece(dest, source):
            return (
                rows_of(ref, 0, part, j, pl.ds(pl.multiple_of(source_at(dest), LANES), size)),
                rows_of(out, here(source), part, lead, pl.ds(column, size)),
                part,
            )

        return piece

    def down_piece(ref, out, source_at, size, row):
        def piece(dest, source):
            return (
                rows_of(ref, source_at(dest), size),
                rows_of(out, row, size, None, pl.ds(here(source), part)),
                size,
            )

        return piece

    found = {}
    if rec_in is not None:
        found["rec_in"] = [
            in_piece(rec_in, 0, w_rec, None, blk, bw, 0),
            in_piece(rec_in, 0, w_rec, None, lambda chip: shared, bw, bw),
            in_piece(rec_in, 1, w_rec, None, blk, bw, 2 * bw),
            in_piece(rec_in, 1, w_rec, None, tile, LANES, 3 * bw),
        ]
    if rec_out is not None:
        found["rec_out"] = [
            down_piece(rec_out, w_out, blk, bw, 0),
            down_piece(rec_out, w_out, tile, LANES, bw),
        ]
    if mlp_in is not None:
        half = span // 2
        found["mlp_in"] = [
            in_piece(mlp_in, j, w_in, j, lambda chip, h=h: win(chip) + h * half, half, h * half)
            for j in range(2)
            for h in range(2)
        ]
    if mlp_out is not None:
        found["mlp_out"] = [down_piece(mlp_out, w_down, win, span, 0)]
    return found


def keep_own(copies, pieces, sems, first):
    col = copies.place.col
    for i, piece in enumerate(pieces):
        src, dst, rows = piece(col, col)
        copies.keep(src(pl.ds(0, rows)), dst(pl.ds(0, rows)), sems.at[first + i])


class Gather:
    def __init__(self, copies, mine, at):
        self.copies, self.at = copies, at
        place = copies.place
        row, col = place.row, place.col
        self.first = [
            copies.start(mine(half), at(row, col, half), name)
            for half in (0, 1)
            for name in ("x", "y")
        ]
        self.own = copies.start(mine(None), at(row, col, None), "core")

    def pass_on(self):
        copies, place = self.copies, self.copies.place
        row = place.row
        x, y = place.chip(1), place.chip(2)
        x0, y0, x1, y1 = self.first
        copies.land(x0)
        self.round0 = copies.start(self.at(row, x, 0), self.at(row, x, 0), "y")
        copies.land(y0, y1)
        self.round1 = copies.start(self.at(row, y, 1), self.at(row, y, 1), "x")
        self.core_y = copies.start(self.at(row, y, None), self.at(row, y, None), "core")
        copies.land(x1)
        self.core_x = copies.start(self.at(row, x, None), self.at(row, x, None), "core")

    def last(self):
        copies, place = self.copies, self.copies.place
        corner = self.at(place.row, place.chip(3), None)
        copies.land(self.round0, self.round1)
        self.core_xy = copies.start(corner, corner, "core")


def block_gather(copies, source, target, sem):
    rows, part = source.shape
    cut = rows // 2

    def at(row, col, half):
        first = row * rows + (0 if half is None else half * cut)
        size = rows if half is None else cut
        return target.at[
            pl.ds(pl.multiple_of(first, ROWS), size), pl.ds(pl.multiple_of(col * part, LANES), part)
        ]

    def mine(half):
        return source if half is None else source.at[pl.ds(half * cut, cut), :]

    place = copies.place
    copies.keep(source, at(place.row, place.col, None), sem)
    return Gather(copies, mine, at)


AROUND = ("x", "y", "xy", "core", "z")


def open_kernel(geo, tokens, rec_in, gains, x_all, w_rec, gains_all, send, recv, local):
    place = Place()
    place.meet(AROUND)
    copies = Copies(place, send, recv)
    pieces = weight_pieces(geo, (rec_in, None, None, None), (w_rec, None, None, None))["rec_in"]
    dealer = Dealer(copies)
    dealer.deal(pieces[0])
    dealer.deal(pieces[1])
    gather = block_gather(copies, tokens, x_all, local.at[0])
    dealer.deal(pieces[2])
    dealer.deal(pieces[3])
    mine = gains_all.at[place.col]
    for name in ("x", "y", "xy"):
        copies.start(gains, mine, name)
    copies.keep(gains, mine, local.at[5])
    keep_own(copies, pieces, local, 1)
    dealer.forward()
    dealer.forward()
    gather.pass_on()
    dealer.forward()
    dealer.forward()
    gather.last()
    copies.finish()
    for copy in copies.local:
        copy.wait()


def open_gather(tokens, rec_in, gains, geo):
    n_col, part, bw, tiles, wide = geo
    width = part * n_col
    return pl.pallas_call(
        functools.partial(open_kernel, geo),
        out_shape=(
            jax.ShapeDtypeStruct((2 * tokens.shape[0], width), low),
            jax.ShapeDtypeStruct((width, 3 * bw + LANES), low),
            jax.ShapeDtypeStruct((n_col,) + gains.shape, f32),
        ),
        in_specs=[anywhere] * 3,
        out_specs=(anywhere,) * 3,
        scratch_shapes=[
            pltpu.SemaphoreType.DMA((37,)),
            pltpu.SemaphoreType.DMA((37,)),
            pltpu.SemaphoreType.DMA((6,)),
        ],
        compiler_params=pltpu.CompilerParams(collective_id=1, has_side_effects=True),
        name="open_gather",
    )(tokens, rec_in, gains)


def slot_gather(copies, local_ref, buf, own):
    cut = own // 2
    n_col = buf.shape[0] // 2

    def at(row, col, half):
        slot = buf.at[row * n_col + col]
        return slot if half is None else slot.at[pl.ds(half * cut, cut), :]

    def mine(half):
        return local_ref if half is None else local_ref.at[pl.ds(half * cut, cut), :]

    return Gather(copies, mine, at)


def tanh_parts(x):
    k = 0.7978845608028654
    square = x * x
    t = jnp.tanh(k * x * (1.0 + 0.044715 * square))
    value = 0.5 * x * (1.0 + t)
    slope = 0.5 * (1.0 + t) + 0.5 * x * (1.0 - t * t) * k * (1.0 + 3 * 0.044715 * square)
    return value, slope


def glu_kernel(
    spare, n2, w_in, w_down, g_all, n2_all, hidden, d_glu, buf, wi, wd, g, hid, dgl, send, recv, local
):
    place = Place()
    place.meet(("x", "y", "core"))
    copies = Copies(place, send, recv)
    own, width = n2.shape
    n_col = buf.shape[0] // 2
    span = wd.shape[0]
    step = 256
    gather = slot_gather(copies, n2, buf, own)
    me = place.row * n_col + place.col
    loads = [
        copies.keep(n2, buf.at[me], local.at[0]),
        copies.keep(w_in, wi, local.at[1]),
        copies.keep(w_down, wd, local.at[2]),
        copies.keep(g_all, g, local.at[3]),
    ]
    for load in loads:
        load.wait()
    hide = spare(place.col)

    def work(chip):
        slots = (chip, n_col + chip)
        rows = [pl.ds(pl.multiple_of(s * own, ROWS), own) for s in slots]
        n2_here = jnp.concatenate([buf[s] for s in slots], axis=0)
        g_here = jnp.concatenate([g[r, :] for r in rows], axis=0)

        def columns(i, carry):
            at = pl.ds(pl.multiple_of(i * step, LANES), step)
            up_at = pl.ds(pl.multiple_of(span + i * step, LANES), step)
            gate = dot(n2_here, wi[0, :, at])
            up = dot(n2_here, wi[1, :, at])
            d_hid = dot(g_here, wd[at, :], ((1,), (1,)))
            lane = lax.broadcasted_iota(jnp.int32, gate.shape, 1) + i * step
            used = (lane >= LANES) | jnp.logical_not(hide)
            up = jnp.where(used, up, 0.0)
            d_hid = jnp.where(used, d_hid, 0.0)
            value, slope = tanh_parts(gate)
            h = (value * up).astype(low)
            dg = (d_hid * up * slope).astype(low)
            du = (d_hid * value).astype(low)
            for n, r in enumerate(rows):
                part = slice(n * own, (n + 1) * own)
                hid[r, at] = h[part]
                dgl[r, at] = dg[part]
                dgl[r, up_at] = du[part]
            return carry

        lax.fori_loop(0, span // step, columns, 0)

    copies.land(gather.own)
    work(place.col)
    gather.pass_on()
    copies.land(gather.core_y)
    work(place.chip(2))
    gather.last()
    copies.land(gather.core_x)
    work(place.chip(1))
    copies.land(gather.core_xy)
    out_n2 = copies.keep(buf, n2_all, local.at[4])
    work(place.chip(3))
    out_h = copies.keep(hid, hidden, local.at[5])
    out_d = copies.keep(dgl, d_glu, local.at[6])
    copies.finish()
    out_n2.wait()
    out_h.wait()
    out_d.wait()


def glu(n2, w_in, w_down, g_all, spare):
    own, width = n2.shape
    group = g_all.shape[0]
    span = w_down.shape[0]
    n_all, h, d = pl.pallas_call(
        functools.partial(glu_kernel, spare),
        out_shape=(
            jax.ShapeDtypeStruct((group // own, own, width), low),
            jax.ShapeDtypeStruct((group, span), low),
            jax.ShapeDtypeStruct((group, 2 * span), low),
        ),
        in_specs=[anywhere] * 4,
        out_specs=(anywhere,) * 3,
        scratch_shapes=[
            pltpu.VMEM((group // own, own, width), low),
            pltpu.VMEM(w_in.shape, low),
            pltpu.VMEM(w_down.shape, low),
            pltpu.VMEM((group, width), low),
            pltpu.VMEM((group, span), low),
            pltpu.VMEM((group, 2 * span), low),
            pltpu.SemaphoreType.DMA((10,)),
            pltpu.SemaphoreType.DMA((10,)),
            pltpu.SemaphoreType.DMA((7,)),
        ],
        compiler_params=pltpu.CompilerParams(
            collective_id=3, has_side_effects=True, vmem_limit_bytes=58 * MIB
        ),
        cost_estimate=pl.CostEstimate(
            flops=6 * group * width * span, bytes_accessed=60 * MIB, transcendentals=group * span
        ),
        name="glu",
    )(n2, w_in, w_down, g_all)
    return n_all.reshape(group, width), h, d


def branch_kernel(x, w, x_all, y, buf, wv, send, recv, local):
    place = Place()
    place.meet(("x", "y", "core"))
    copies = Copies(place, send, recv)
    own = x.shape[0]
    n_col = buf.shape[0] // 2
    gather = slot_gather(copies, x, buf, own)
    me = place.row * n_col + place.col
    load = copies.keep(w, wv, local.at[0])
    mine = copies.keep(x, buf.at[me], local.at[1])
    load.wait()
    mine.wait()

    def work(chip):
        slots = (chip, n_col + chip)
        value = dot(jnp.concatenate([buf[s] for s in slots], axis=0), wv[...], ((1,), (1,)))
        for n, s in enumerate(slots):
            y[pl.ds(pl.multiple_of(s * own, ROWS), own), :] = value[n * own : (n + 1) * own]

    copies.land(gather.own)
    work(place.col)
    gather.pass_on()
    copies.land(gather.core_y)
    work(place.chip(2))
    gather.last()
    copies.land(gather.core_x)
    work(place.chip(1))
    copies.land(gather.core_xy)
    out = copies.keep(buf, x_all, local.at[2])
    work(place.chip(3))
    copies.finish()
    out.wait()


def gather_branch(x, w):
    own, width = x.shape
    slots = 2 * lax.axis_size("col")
    x_all, y = pl.pallas_call(
        branch_kernel,
        out_shape=(
            jax.ShapeDtypeStruct((slots, own, width), low),
            jax.ShapeDtypeStruct((slots * own, w.shape[0]), f32),
        ),
        in_specs=[anywhere] * 2,
        out_specs=(anywhere, in_vmem),
        scratch_shapes=[
            pltpu.VMEM((slots, own, width), low),
            pltpu.VMEM(w.shape, low),
            pltpu.SemaphoreType.DMA((10,)),
            pltpu.SemaphoreType.DMA((10,)),
            pltpu.SemaphoreType.DMA((3,)),
        ],
        compiler_params=pltpu.CompilerParams(
            collective_id=4, has_side_effects=True, vmem_limit_bytes=48 * MIB
        ),
        name="gather_branch",
    )(x, w)
    return x_all.reshape(slots * own, width), y


def scatter_kernel(
    n_parts, across, act, w, out, actv, wv, other, mine, from_core, from_x, from_y, turn, send, recv, local
):
    place = Place()
    place.meet(("x", "y", "core"))
    copies = Copies(place, send, recv)
    own, width = out.shape
    cut = own // 2
    n_col = act.shape[0] // own // 2
    k = act.shape[1] // n_parts
    step = 256
    loads = [copies.keep(act, actv, local.at[0]), copies.keep(w, wv, local.at[1])]
    for load in loads:
        load.wait()
    top, bottom = pl.ds(0, cut), pl.ds(cut, cut)

    def work(j):
        chip = place.chip(j)
        slots = ((1 - place.row) * n_col + chip, place.row * n_col + chip)
        left = [
            jnp.concatenate(
                [
                    actv[pl.ds(pl.multiple_of(s * own, ROWS), own), n * k : (n + 1) * k]
                    for s in slots
                ],
                axis=0,
            )
            for n in range(n_parts)
        ]

        def columns(i, carry):
            at = pl.ds(pl.multiple_of(i * step, LANES), step)
            total = None
            for n in range(n_parts):
                if across:
                    right = wv[n, at, :] if n_parts > 1 else wv[at, :]
                    term = dot(left[n], right, ((1,), (1,)))
                else:
                    term = dot(left[n], wv[:, at])
                total = term if total is None else total + term
            other[j, :, at] = total[:own].astype(low)
            mine[j, :, at] = total[own:]
            return carry

        lax.fori_loop(0, width // step, columns, 0)
        return copies.start(other.at[j], from_core.at[j], "core")

    def add_core(j, number):
        copies.land(number)
        mine[j] = mine[j] + from_core[j].astype(f32)
        turn[j] = mine[j].astype(low)

    core3 = work(3)
    core1 = work(1)
    add_core(3, core3)
    x3 = copies.start(turn.at[3, top, :], from_x.at[0], "x")
    y3 = copies.start(turn.at[3, bottom, :], from_y.at[0], "y")
    core2 = work(2)
    add_core(1, core1)
    x1 = copies.start(turn.at[1, top, :], from_x.at[1], "x")
    core0 = work(0)
    add_core(2, core2)
    y2 = copies.start(turn.at[2, bottom, :], from_y.at[1], "y")
    copies.land(x3)
    turn[2, top, :] = (mine[2, top, :] + from_x[0].astype(f32)).astype(low)
    y_last = copies.start(turn.at[2, top, :], from_y.at[2], "y")
    copies.land(y3)
    turn[1, bottom, :] = (mine[1, bottom, :] + from_y[0].astype(f32)).astype(low)
    x_last = copies.start(turn.at[1, bottom, :], from_x.at[2], "x")
    add_core(0, core0)
    copies.land(x1, y2, y_last, x_last)
    out[top, :] = mine[0, top, :] + from_x[1].astype(f32) + from_y[2].astype(f32)
    out[bottom, :] = mine[0, bottom, :] + from_y[1].astype(f32) + from_x[2].astype(f32)
    copies.finish()


def multiply_scatter(act, w, across, number, name):
    n_parts = w.shape[0] if w.ndim == 3 else 1
    group = act.shape[0]
    slots = 2 * lax.axis_size("col")
    own = group // slots
    width = w.shape[-2] if across else w.shape[-1]
    return pl.pallas_call(
        functools.partial(scatter_kernel, n_parts, across),
        out_shape=jax.ShapeDtypeStruct((own, width), f32),
        in_specs=[anywhere] * 2,
        out_specs=in_vmem,
        scratch_shapes=[
            pltpu.VMEM(act.shape, low),
            pltpu.VMEM(w.shape, low),
            pltpu.VMEM((4, own, width), low),
            pltpu.VMEM((4, own, width), f32),
            pltpu.VMEM((4, own, width), low),
            pltpu.VMEM((3, own // 2, width), low),
            pltpu.VMEM((3, own // 2, width), low),
            pltpu.VMEM((4, own, width), low),
            pltpu.SemaphoreType.DMA((10,)),
            pltpu.SemaphoreType.DMA((10,)),
            pltpu.SemaphoreType.DMA((2,)),
        ],
        compiler_params=pltpu.CompilerParams(
            collective_id=number, has_side_effects=True, vmem_limit_bytes=58 * MIB
        ),
        cost_estimate=pl.CostEstimate(
            flops=2 * group * width * act.shape[1], bytes_accessed=40 * MIB, transcendentals=0
        ),
        name=name,
    )(act, w)


def sums_kernel(far, split, mixed, gate_part, sums_out, chans_out, gates_out, got, acc, ch, send, recv, local):
    place = Place()
    steps = [f"d{d}" for d in far if d & (d - 1) == 0]
    place.meet(("core", "x", "y") + tuple(f"d{d}" for d in far))
    copies = Copies(place, send, recv)
    dp, col = place.dp, place.col
    own_gates = gates_out.at[col]
    stay = copies.keep(gate_part, own_gates.at[dp], local)
    parts = [copies.start(gate_part, own_gates.at[dp], f"d{d}") for d in far]
    acc[0] = mixed[...]
    n = 0
    for name in steps:
        copies.land(copies.start(acc.at[n], got.at[n], name))
        acc[n + 1] = acc[n] + got[n]
        n += 1
    stay.wait()
    copies.land(*parts)
    half = gates_out.shape[1] // 2
    halves = (pl.ds(0, half), pl.ds(half, half))

    def gate_view(chip, h):
        return gates_out.at[chip, halves[h]]

    direct = {
        (name, h): copies.start(gate_view(col, h), gate_view(col, h), name)
        for h in (0, 1)
        for name in ("x", "y")
    }
    ch[col] = acc[n][:, :split]
    x_ch = copies.start(ch.at[col], ch.at[col], "x")
    rest = slice(split, None)
    for name in ("core", "x", "y"):
        number = copies.start(acc.at[n, :, rest], got.at[n, :, rest], name)
        if name == "y":
            copies.land(x_ch)
            pair = pl.ds(lax.div(col, 2) * 2, 2)
            y_ch = copies.start(ch.at[pair], ch.at[pair], "y")
        copies.land(number)
        acc[n + 1, :, rest] = acc[n, :, rest] + got[n, :, rest]
        n += 1
    copies.land(direct["x", 0])
    far_x = gate_view(place.chip(1), 0)
    copies.start(far_x, far_x, "y")
    copies.land(direct["y", 1])
    far_y = gate_view(place.chip(2), 1)
    copies.start(far_y, far_y, "x")
    sums_out[...] = acc[n, :, rest]
    copies.land(y_ch)
    chans_out[...] = ch[...]
    copies.finish()


def sum_everywhere(mixed, split, gate_part, n_dp, n_col):
    far = tuple(range(1, n_dp))
    stages = len([d for d in far if d & (d - 1) == 0]) + 3
    count = 2 * len(far) + stages + 8
    rows, columns = mixed.shape
    return pl.pallas_call(
        functools.partial(sums_kernel, far, split),
        out_shape=(
            jax.ShapeDtypeStruct((rows, columns - split), f32),
            jax.ShapeDtypeStruct((n_col, rows, split), f32),
            jax.ShapeDtypeStruct((n_col, n_dp) + gate_part.shape, gate_part.dtype),
        ),
        in_specs=[in_vmem, anywhere],
        out_specs=(in_vmem, in_vmem, anywhere),
        scratch_shapes=[
            pltpu.VMEM((stages, rows, columns), f32),
            pltpu.VMEM((stages + 1, rows, columns), f32),
            pltpu.VMEM((n_col, rows, split), f32),
            pltpu.SemaphoreType.DMA((count,)),
            pltpu.SemaphoreType.DMA((count,)),
            pltpu.SemaphoreType.DMA,
        ],
        compiler_params=pltpu.CompilerParams(collective_id=5, has_side_effects=True),
        name="small_sums",
    )(mixed, gate_part)


def one_less_exp(z):
    series = 1.0 + z / 6.0
    for n in (5.0, 4.0, 3.0, 2.0):
        series = 1.0 + z / n * series
    return jnp.where(z > -0.1, -z * series, 1.0 - jnp.exp(z))


def scan_tile(a, u, reverse):
    rows = a.shape[0]
    index = lax.broadcasted_iota(jnp.int32, a.shape, 0)
    by = 1
    while by < rows:
        turn = rows - by if reverse else by
        inside = index < rows - by if reverse else index >= by
        u = u + a * jnp.where(inside, pltpu.roll(u, turn, 0), 0.0)
        a = a * jnp.where(inside, pltpu.roll(a, turn, 0), 1.0)
        by *= 2
    return a, u


def forward_kernel(
    geo,
    x_all,
    w_rec,
    gain,
    gates_blk,
    gates_tile,
    bias,
    soft,
    conv_w,
    conv_b,
    places,
    cotangent,
    rec_out,
    mlp_in,
    mlp_out,
    n1_out,
    x_out,
    y_out,
    pre_out,
    c_out,
    state_out,
    branch_out,
    first_out,
    g_all,
    w_out,
    w_in,
    w_down,
    xv,
    wv,
    before,
    xb,
    yv,
    prev,
    cv,
    hv,
    pv,
    bv,
    carry,
    first,
    send,
    recv,
    local,
):
    place = Place()
    place.meet(AROUND + ("next", "prev"))
    copies = Copies(place, send, recv)
    n_col, part, bw, tiles, wide = geo
    chans = bw + LANES
    group, width = xv.shape
    tile = 256
    n_tiles = group // tile
    loads = [copies.keep(x_all, xv, local.at[0]), copies.keep(w_rec, wv, local.at[1])]
    halo = copies.start(x_all.at[pl.ds(group - ROWS, ROWS), :], before, "next")
    found = weight_pieces(geo, (None, rec_out, mlp_in, mlp_out), (None, w_out, w_in, w_down))
    pieces = found["rec_out"] + found["mlp_in"] + found["mlp_out"]
    dealer = Dealer(copies)
    dealer.deal(pieces[0])
    dealer.deal(pieces[1])
    dealer.deal(pieces[2])
    dealer.deal(pieces[3])
    keep_own(copies, pieces, local, 2)
    for load in loads:
        load.wait()
    high_tile = place.col >= 2
    idle_tile = lax.rem(place.col, 2) == 1

    def normed(x):
        x = x.astype(f32)
        scale = lax.rsqrt(jnp.sum(x * x, axis=-1, keepdims=True) / width + epsilon)
        return (x * scale * gain[...]).astype(low)

    copies.land(halo)
    xb[0:8, :] = dot(normed(before[...]), wv[:, : 2 * bw])[ROWS - 8 :]
    carry[0:1] = jnp.zeros_like(carry[0:1])
    carry[1:2] = jnp.ones_like(carry[1:2])

    def work(i, unused):
        r0 = pl.multiple_of(i * tile, tile)
        rows = pl.ds(r0, tile)
        n1 = normed(xv[rows, :])
        xv[rows, :] = n1
        both = dot(n1, wv[...])
        xb[pl.ds(pl.multiple_of(r0 + 8, 8), tile), :] = both[:, : 2 * bw]
        yv[rows, :] = both[:, 2 * bw :]
        spot = places[rows, :]
        reach = xb[pl.ds(r0, tile + 8), :]
        conv = []
        for lane in range(2 * bw // LANES):
            at = slice(lane * LANES, (lane + 1) * LANES)
            near = reach[:, at]
            total = conv_b[0:1, at] + conv_w[0:1, at] * near[8:]
            for t in range(1, conv_w.shape[0]):
                lagged = pltpu.roll(near, t, 0)[8:]
                total = total + jnp.where(spot >= t, conv_w[t : t + 1, at] * lagged, 0.0)
            conv.append(total.astype(low))
        c = jnp.concatenate(conv, axis=1)
        cv[rows, :] = c
        pre = [
            jnp.concatenate([dot(c[:, :bw], gates_blk[j]), dot(c[:, bw:], gates_tile[j])], axis=1)
            + bias[j : j + 1, :]
            for j in range(2)
        ]
        prev[rows, :chans] = pre[0]
        prev[rows, chans:] = pre[1]
        reset = spot == 0
        for lane in range(chans // LANES):
            at = slice(lane * LANES, (lane + 1) * LANES)
            if lane * LANES < bw:
                own_c = conv[lane].astype(f32)
            else:
                own_c = jnp.where(high_tile, conv[lane + 1].astype(f32), conv[lane].astype(f32))
            log_a = -8.0 * jax.nn.sigmoid(pre[1][:, at]) * soft[0:1, at]
            a = jnp.where(reset, 0.0, jnp.exp(log_a))
            m = jnp.where(reset, 1.0, jnp.sqrt(one_less_exp(2.0 * log_a)))
            u = own_c * jax.nn.sigmoid(pre[0][:, at]) * m
            a, u = scan_tile(a, u, False)
            h = u + a * carry[0:1, at]
            p = a * carry[1:2, at]
            hv[rows, at] = h
            pv[rows, at] = p
            carry[0:1, at] = h[tile - 1 :]
            carry[1:2, at] = p[tile - 1 :]
        return unused

    third = n_tiles // 3
    lax.fori_loop(0, third, work, 0)
    dealer.forward()
    dealer.forward()
    dealer.deal(pieces[4])
    dealer.forward()
    lax.fori_loop(third, 2 * third, work, 0)
    dealer.forward()
    gather = block_gather(copies, cotangent, g_all, local.at[9])
    dealer.deal(pieces[5])
    lax.fori_loop(2 * third, n_tiles, work, 0)
    state_in = copies.start(hv.at[pl.ds(group - 8, 8), :], first, "next")
    outs = [
        copies.keep(src, dst, local.at[10 + i])
        for i, (src, dst) in enumerate(
            ((xv, n1_out), (xb, x_out), (yv, y_out), (prev, pre_out), (cv, c_out))
        )
    ]
    dealer.forward()
    dealer.deal(pieces[6])
    copies.land(state_in)
    copies.leave(state_in)
    before_all = first[7:8, :]

    def finish(i, unused):
        rows = pl.ds(pl.multiple_of(i * tile, tile), tile)
        for lane in range(chans // LANES):
            at = slice(lane * LANES, (lane + 1) * LANES)
            state = hv[rows, at] + pv[rows, at] * before_all[:, at]
            hv[rows, at] = state
            value, _ = tanh_parts(yv[rows, at])
            b = state * value
            if lane * LANES >= bw:
                b = jnp.where(idle_tile, 0.0, b)
            bv[rows, at] = b.astype(low)
        return unused

    lax.fori_loop(0, n_tiles, finish, 0)
    outs += [
        copies.keep(hv, state_out, local.at[15]),
        copies.keep(bv, branch_out, local.at[16]),
        copies.keep(first, first_out, local.at[17]),
    ]
    dealer.forward()
    gather.pass_on()
    gather.last()
    dealer.forward()
    copies.finish()
    for copy in copies.local:
        if not any(copy is load for load in loads):
            copy.wait()


def rec_forward(x_all, w_rec, params, places, cotangent, rec_out, mlp_in, mlp_out, geo):
    n_col, part, bw, tiles, wide = geo
    width, span, chans = part * n_col, wide * LANES, bw + LANES
    group = x_all.shape[0]

    def of(shape, dtype):
        return jax.ShapeDtypeStruct(shape, dtype)

    kept = [
        ((group, width), low),
        ((group + 8, 2 * bw), f32),
        ((group, chans), f32),
        ((group, 2 * chans), f32),
        ((group, 2 * bw), low),
        ((group, chans), f32),
        ((group, chans), low),
        ((8, chans), f32),
    ]
    dealt = [((group, width), low), ((chans, width), low), ((2, width, span), low), ((span, width), low)]
    copy_count = 1 + 6 * 7 + 10 + 1
    return pl.pallas_call(
        functools.partial(forward_kernel, geo),
        out_shape=tuple(of(*s) for s in kept + dealt),
        in_specs=[anywhere] * 2 + [in_vmem] * 8 + [anywhere] * 4,
        out_specs=(anywhere,) * 12,
        scratch_shapes=[
            pltpu.VMEM((group, width), low),
            pltpu.VMEM(w_rec.shape, low),
            pltpu.VMEM((ROWS, width), low),
            pltpu.VMEM((group + 8, 2 * bw), f32),
            pltpu.VMEM((group, chans), f32),
            pltpu.VMEM((group, 2 * chans), f32),
            pltpu.VMEM((group, 2 * bw), low),
            pltpu.VMEM((group, chans), f32),
            pltpu.VMEM((group, chans), f32),
            pltpu.VMEM((group, chans), low),
            pltpu.VMEM((8, chans), f32),
            pltpu.VMEM((8, chans), f32),
            pltpu.SemaphoreType.DMA((copy_count,)),
            pltpu.SemaphoreType.DMA((copy_count,)),
            pltpu.SemaphoreType.DMA((18,)),
        ],
        compiler_params=pltpu.CompilerParams(
            collective_id=2, has_side_effects=True, vmem_limit_bytes=58 * MIB
        ),
        name="rec_forward",
    )(x_all, w_rec, *params, places, cotangent, rec_out, mlp_in, mlp_out)


def scan_kernel(reverse, a_ref, u_ref, h_ref, p_ref, carry):
    step = pl.program_id(0)
    rows = a_ref.shape[0]

    @pl.when(step == 0)
    def _():
        carry[0:1] = jnp.zeros_like(carry[0:1])
        carry[1:2] = jnp.ones_like(carry[1:2])

    for lane in range(a_ref.shape[1] // LANES):
        at = slice(lane * LANES, (lane + 1) * LANES)
        a = a_ref[:, at]
        u = u_ref[:, at]
        index = lax.broadcasted_iota(jnp.int32, a.shape, 0)
        by = 1
        while by < rows:
            turn = rows - by if reverse else by
            inside = index < rows - by if reverse else index >= by
            a_far = jnp.where(inside, pltpu.roll(a, turn, 0), 1.0)
            u_far = jnp.where(inside, pltpu.roll(u, turn, 0), 0.0)
            u = u + a * u_far
            a = a * a_far
            by *= 2
        h = u + a * carry[0:1, at]
        p = a * carry[1:2, at]
        h_ref[:, at] = h
        p_ref[:, at] = p
        edge = 0 if reverse else rows - 1
        carry[0:1, at] = h[edge : edge + 1]
        carry[1:2, at] = p[edge : edge + 1]


def scan_rows(decay, inject, reverse, rows=256):
    length, channels = decay.shape
    steps = length // rows
    block = pl.BlockSpec((rows, channels), lambda i: (steps - 1 - i if reverse else i, 0))
    shape = jax.ShapeDtypeStruct(decay.shape, f32)
    return pl.pallas_call(
        functools.partial(scan_kernel, reverse),
        grid=(steps,),
        out_shape=(shape, shape),
        in_specs=[block, block],
        out_specs=(block, block),
        scratch_shapes=[pltpu.VMEM((8, channels), f32)],
        name="scan_back" if reverse else "scan",
    )(decay, inject)


def outer_kernel(n_dp, first_steps, left1, right1, left2, right2, out_ref):
    def multiply(left, right):
        total = dot(left[...], right[...], ((0,), (0,)))
        rows = total.shape[0] // n_dp
        for k in range(n_dp):
            out_ref[k, 0] = total[k * rows : (k + 1) * rows].astype(out_ref.dtype)

    j = pl.program_id(1)

    @pl.when(j < first_steps)
    def _():
        multiply(left1, right1)

    @pl.when(j >= first_steps)
    def _():
        multiply(left2, right2)


def outer_pair(left1, right1, left2, right2, n_dp, n_col, columns, name):
    length, width = left1.shape
    part = width // n_col
    steps1, steps2 = right1.shape[1] // columns, right2.shape[1] // columns
    count = (steps1 + steps2) * columns
    left_block = pl.BlockSpec((length, part), lambda i, j: (0, i))
    return pl.pallas_call(
        functools.partial(outer_kernel, n_dp, steps1),
        grid=(n_col, steps1 + steps2),
        out_shape=jax.ShapeDtypeStruct((n_dp, n_col, part // n_dp, count), low),
        in_specs=[
            left_block,
            pl.BlockSpec((length, columns), lambda i, j: (0, jnp.minimum(j, steps1 - 1))),
            left_block,
            pl.BlockSpec((length, columns), lambda i, j: (0, jnp.maximum(j - steps1, 0))),
        ],
        out_specs=pl.BlockSpec((n_dp, 1, part // n_dp, columns), lambda i, j: (0, i, 0, j)),
        compiler_params=pltpu.CompilerParams(vmem_limit_bytes=48 * MIB),
        cost_estimate=pl.CostEstimate(
            flops=2 * length * width * count,
            bytes_accessed=2 * (2 * length * width + length * count + width * count),
            transcendentals=0,
        ),
        name=name,
    )(left1, right1, left2, right2)


def dot(a, b, dims=((1,), (0,))):
    return lax.dot_general(a, b, (dims, ((), ())), preferred_element_type=f32)


def neighbour(x, axis, by):
    length = lax.axis_size(axis)
    pairs = [(i, i + by) for i in range(length) if 0 <= i + by < length]
    return lax.ppermute(x, axis, pairs)


def places_of(rows, lengths):
    ends = jnp.cumsum(lengths)
    starts = ends - lengths
    inside = (rows[:, None] >= starts[None, :]) & (rows[:, None] < ends[None, :])
    return rows - jnp.sum(jnp.where(inside, starts[None, :], 0), axis=1)


def lru_coeffs(pre_in, pre_rate, inputs, decay, reset):
    input_gate = jax.nn.sigmoid(pre_in)
    rate_gate = jax.nn.sigmoid(pre_rate)
    log_decay = -8.0 * rate_gate * jax.nn.softplus(decay)
    decay_factor = jnp.where(reset, 0.0, jnp.exp(log_decay))
    scaling = jnp.where(reset, 1.0, jnp.sqrt(-jnp.expm1(2.0 * log_decay)))
    return (decay_factor, inputs * input_gate * scaling)


def body(
    tokens,
    cotangent,
    rec_in,
    rec_out,
    gates,
    gate_bias,
    decay,
    conv_w,
    conv_b,
    gains,
    mlp_in,
    mlp_out,
    lengths,
    order,
):
    n_dp, n_row, n_col = (lax.axis_size(a) for a in ("dp", "row", "col"))
    dp, row, col = (lax.axis_index(a) for a in ("dp", "row", "col"))
    given, part = tokens.shape
    own = given // n_col
    group = given * n_row
    width = part * n_col
    taps = conv_w.shape[0]
    blocks, bw = gates.shape[1], gates.shape[2]
    half = rec_out.shape[0]
    hidden_half = mlp_out.shape[0]
    tiles = hidden_half // LANES
    wide = -(-tiles // n_col)
    span = wide * LANES
    shared = n_col * bw
    chans = bw + LANES

    geo = (n_col, part, bw, tiles, wide)
    x_all, w_rec, gains_all = open_gather(tokens, rec_in, gains, geo)
    gains_all = gains_all.transpose(1, 0, 2).reshape(gains.shape[0], width)
    w_x, w_y = w_rec[:, : 2 * bw], w_rec[:, 2 * bw :]

    def own_rows(x):
        return lax.dynamic_slice_in_dim(x, (row * n_col + col) * own, own, axis=0)

    def home_rows(x):
        dealt = lax.all_to_all(x.reshape(own, n_col, part).transpose(1, 0, 2), "col", 0, 0)
        return dealt.reshape(given, part)

    tile_at = shared + (col // 2) * LANES
    tile_owner = col % 2 == 0

    def own_channels(x):
        blk = lax.dynamic_slice_in_dim(x, col * bw, bw, axis=-1)
        tile = lax.dynamic_slice_in_dim(x, tile_at, LANES, axis=-1)
        return jnp.concatenate([blk, tile], axis=-1)

    def block_channels(x):
        blk = lax.dynamic_slice_in_dim(x, col * bw, bw, axis=-1)
        return jnp.concatenate([blk, x[..., shared:]], axis=-1)

    bias = own_channels(gate_bias)
    decay_o = own_channels(decay)
    conv_w_c = block_channels(conv_w)
    conv_b_c = block_channels(conv_b)
    conv_w_o = own_channels(conv_w)
    gates_blk = lax.dynamic_index_in_dim(gates, col, axis=1, keepdims=False)
    gates_five = gates[:, n_col]
    gates_tile = lax.dynamic_slice_in_dim(gates_five, (col // 2) * LANES, LANES, axis=2)
    gates_rows = lax.dynamic_slice_in_dim(gates_five, (col // 2) * LANES, LANES, axis=1)
    channel_ok = (jnp.arange(chans) < bw) | tile_owner

    base = dp * group
    places_ext = places_of(base + jnp.arange(group + taps - 1, dtype=jnp.int32), lengths)
    places = places_ext[:group]
    reset = (places == 0)[:, None]

    n1, x_rows, y_branch, pre_both, conv_low, state, branch, first, g_all, w_out, w_in, w_down = rec_forward(
        x_all,
        w_rec,
        (
            gains_all[0:1],
            gates_blk,
            gates_tile,
            bias,
            jax.nn.softplus(decay_o)[None, :],
            conv_w_c,
            conv_b_c[None, :],
        ),
        jnp.broadcast_to(places[:, None], (group, LANES)),
        cotangent,
        rec_out,
        mlp_in,
        mlp_out,
        geo,
    )
    inputs = own_rows(x_all).astype(f32)
    upstream = own_rows(g_all).astype(f32)
    sumsq_one = jnp.sum(inputs * inputs, axis=-1, keepdims=True)
    scale_one = lax.rsqrt(sumsq_one / width + epsilon)
    x_ext = x_rows[8 - (taps - 1) :]
    conv_blk, conv_five = conv_low[:, :bw], conv_low[:, bw:]
    conv_o = jnp.concatenate(
        [conv_blk, lax.dynamic_slice_in_dim(conv_five, (col // 2) * LANES, LANES, axis=1)], axis=1
    ).astype(f32)
    pre = [pre_both[:, :chans], pre_both[:, chans:]]
    factor, _ = lru_coeffs(pre[0], pre[1], conv_o, decay_o, reset)
    state_in = first[7:]
    out_one = multiply_scatter(branch, w_out, False, 6, "out_one")
    resid = inputs + out_one
    sumsq_two = jnp.sum(resid * resid, axis=-1, keepdims=True)
    scale_two = lax.rsqrt(sumsq_two / width + epsilon)
    normed_two = (resid * scale_two * gains_all[1]).astype(low)

    def spare(at):
        return spare_window(at, tiles, n_col, wide)

    n2, hidden, d_glu = glu(normed_two, w_in, w_down, g_all, spare)
    g_mlp = outer_pair(n2, d_glu, g_all, hidden, n_dp, n_col, 512, "outer_mlp")
    d_glu, hidden, g_mlp = lax.optimization_barrier((d_glu, hidden, g_mlp))
    sum_mlp = lax.psum_scatter(g_mlp, "dp", scatter_dimension=0)
    d_normed_two = multiply_scatter(d_glu, w_in, True, 7, "d_normed_two")
    gained_two = gains_all[1] * d_normed_two
    inner_two = jnp.sum(gained_two * resid, axis=-1, keepdims=True)
    grad_gain_two = jnp.sum(d_normed_two * resid * scale_two, axis=0)
    d_resid = upstream + scale_two * gained_two - resid * scale_two**3 * (inner_two / width)
    d_out, d_branch = gather_branch(d_resid.astype(low), w_out)

    d_branch = jnp.where(channel_ok, d_branch, 0.0)
    _, mix_back = jax.vjp(lambda state_v, gate_v: state_v * gelu(gate_v), state, y_branch)
    d_state, d_y = mix_back(d_branch)
    message, until = scan_rows(factor, factor * d_state, True)
    message_in = neighbour(message[:8], "dp", -1)[:1]
    message = message + until * message_in
    grad_state = d_state + jnp.concatenate([message[1:], message_in], axis=0)
    state_prev = jnp.concatenate([state_in, state[:-1]], axis=0)
    _, coef_back = jax.vjp(
        lambda a, b, c, d: lru_coeffs(a, b, c, d, reset), pre[0], pre[1], conv_o, decay_o
    )
    d_pre_in, d_pre_rate, d_conv, g_decay = coef_back((grad_state * state_prev, grad_state))
    d_pre = [d_pre_in.astype(low), d_pre_rate.astype(low)]
    tiles_here = jnp.concatenate([d[:, bw:] for d in d_pre], axis=1)
    tiles_there = lax.ppermute(tiles_here, "col", [(i, i ^ 2) for i in range(n_col)])
    low_half = col // 2 == 0
    d_conv_parts = []
    d_five = []
    for j in range(2):
        here = d_pre[j][:, bw:]
        there = tiles_there[:, j * LANES : (j + 1) * LANES]
        d_five.append(
            jnp.where(
                low_half,
                jnp.concatenate([here, there], axis=1),
                jnp.concatenate([there, here], axis=1),
            )
        )
        d_conv_parts.append(
            jnp.concatenate(
                [
                    dot(d_pre[j][:, :bw], gates_blk[j], ((1,), (1,))),
                    dot(d_five[j], gates_rows[j], ((1,), (1,))),
                ],
                axis=1,
            )
        )
    d_conv = d_conv + d_conv_parts[0] + d_conv_parts[1]
    g_gates = jnp.stack(
        [
            jnp.concatenate(
                [
                    dot(conv_blk, d_pre[j][:, :bw], ((0,), (0,))),
                    dot(conv_five, d_pre[j][:, bw:], ((0,), (0,))),
                ],
                axis=1,
            )
            for j in range(2)
        ]
    )
    g_bias = [jnp.sum(d.astype(f32), axis=0) for d in d_pre]
    later = neighbour(d_conv[:8], "dp", -1)[: taps - 1]
    d_ext = jnp.concatenate([d_conv, later], axis=0)
    x_own = jnp.concatenate(
        [x_ext[:, :bw], lax.dynamic_slice_in_dim(x_ext, bw + (col // 2) * LANES, LANES, axis=1)],
        axis=1,
    )
    d_x = jnp.zeros_like(d_conv)
    g_taps = []
    for t in range(taps):
        ahead = d_ext[t : t + group]
        valid = (places_ext[t : t + group] >= t)[:, None]
        d_x = d_x + jnp.where(valid, conv_w_o[t][None, :] * ahead, 0.0)
        lagged = x_own[taps - 1 - t : taps - 1 - t + group]
        g_taps.append(jnp.sum(jnp.where((places >= t)[:, None], d_conv * lagged, 0.0), axis=0))
    g_conv_b = jnp.sum(d_conv, axis=0)
    d_x_low = jnp.where(channel_ok, d_x, 0.0).astype(low)
    d_y_low = jnp.where(channel_ok, d_y, 0.0).astype(low)
    d_rec = jnp.concatenate([d_x_low, d_y_low], axis=1)
    w_x_own = jnp.concatenate(
        [w_x[:, :bw], lax.dynamic_slice_in_dim(w_x, bw + (col // 2) * LANES, LANES, axis=1)], axis=1
    )
    w_back = jnp.concatenate([w_x_own, w_y], axis=1)
    g_rec = outer_pair(n1, d_rec, d_out, branch, n_dp, n_col, chans, "outer_rec")
    g_rec, d_rec = lax.optimization_barrier((g_rec, d_rec))
    d_normed_one = multiply_scatter(d_rec, w_back, True, 9, "d_normed_one")
    g_rec, g_gates, sum_mlp, d_normed_one, hidden = lax.optimization_barrier(
        (g_rec, g_gates, sum_mlp, d_normed_one, hidden)
    )
    gate_sums = lax.psum_scatter(
        g_gates.astype(low).reshape(n_dp, 2 * bw // n_dp, chans), "dp", scatter_dimension=0
    )
    g_rec, gate_sums = lax.optimization_barrier((g_rec, gate_sums))
    sum_rec = lax.psum_scatter(g_rec, "dp", scatter_dimension=0)
    out_two = multiply_scatter(hidden, w_down, False, 8, "out_two")
    result = (resid + out_two).astype(low)
    gained_one = gains_all[0] * d_normed_one
    inner_one = jnp.sum(gained_one * inputs, axis=-1, keepdims=True)
    grad_gain_one = jnp.sum(d_normed_one * inputs * scale_one, axis=0)
    d_input = d_resid + scale_one * gained_one - inputs * scale_one**3 * (inner_one / width)

    result = home_rows(result)
    grad_input = home_rows(d_input.astype(low))

    def windows(got, first):
        return [
            got[c][..., first + (LANES if c > n_col - 1 - (wide * n_col - tiles) else 0) : first + span]
            for c in range(n_col)
        ]

    def channels_of(got, first):
        return [got[c][..., first : first + bw] for c in range(n_col)] + [
            got[c][..., first + bw : first + chans] for c in range(0, n_col, 2)
        ]

    dealt = lax.all_to_all(sum_mlp, "col", 0, 0)
    grad_mlp_in = jnp.stack(
        [jnp.concatenate(windows(dealt[..., j * span : (j + 1) * span], 0), axis=-1) for j in range(2)]
    ).astype(f32)
    grad_mlp_out = jnp.concatenate(windows(dealt[..., 2 * span :], 0), axis=-1).astype(f32).T
    recs = lax.all_to_all(sum_rec, "col", 0, 0)
    grad_rec_in = jnp.stack(
        [jnp.concatenate(channels_of(recs, j * chans), axis=-1) for j in range(2)]
    ).astype(f32)
    grad_rec_out = jnp.concatenate(channels_of(recs, 2 * chans), axis=-1).astype(f32).T

    small = jnp.where(channel_ok, jnp.stack(g_bias + [g_decay] + g_taps + [g_conv_b]), 0.0)
    square_sums = jnp.stack(
        [jnp.sum(sumsq_one), jnp.sum(out_one * out_one), jnp.sum(sumsq_two), jnp.sum(out_two * out_two)]
    )
    lines = small.shape[0]
    gain_sums = jnp.stack([grad_gain_one, grad_gain_two]).reshape(lines, 2 * width // lines)
    stat_block = jnp.pad(square_sums[None, :], ((0, lines - 1), (0, LANES - 4)))
    mixed = jnp.concatenate([small, gain_sums, stat_block], axis=1)
    sums, chan_sums, gate_parts = sum_everywhere(mixed, chans, gate_sums, n_dp, n_col)
    mine = jnp.concatenate(channels_of(chan_sums, 0), axis=-1)
    gain_rows = sums[:, : 2 * width // lines].reshape(2, width)
    grad_gains = lax.dynamic_slice_in_dim(gain_rows, col * part, part, axis=1)
    stats = jnp.sqrt(sums[0, 2 * width // lines :][:4] / (n_dp * group * width))
    gate_parts = gate_parts.reshape(n_col, 2, bw, chans).astype(f32)
    five = jnp.concatenate([gate_parts[c, :, :, bw:] for c in range(0, n_col, 2)], axis=-1)
    grad_gates = jnp.stack([gate_parts[c, :, :, :bw] for c in range(n_col)] + [five], axis=1)
    return (
        result,
        grad_input,
        grad_rec_in,
        grad_rec_out,
        grad_gates,
        mine[0:2],
        mine[2],
        mine[3 : 3 + taps],
        mine[3 + taps],
        grad_gains,
        grad_mlp_in,
        grad_mlp_out,
        stats,
    )


def solution(mesh):
    placed = (
        P(("dp", "row"), "col"),
        P(("dp", "row"), "col"),
        P(None, "col", "row"),
        P("row", "col"),
        P(None, "row", None, None),
        P(None, "row"),
        P("row"),
        P(None, "row"),
        P("row"),
        P(None, "col"),
        P(None, "col", "row"),
        P("row", "col"),
        P(),
        P(),
    )
    return jax.shard_map(
        body,
        mesh=mesh,
        in_specs=placed,
        out_specs=(
            P(("dp", "row"), "col"),
            P(("dp", "row"), "col"),
            P(None, ("col", "dp"), "row"),
            P("row", ("col", "dp")),
            P(None, "row", None, None),
            P(None, "row"),
            P("row"),
            P(None, "row"),
            P("row"),
            P(None, "col"),
            P(None, ("col", "dp"), "row"),
            P("row", ("col", "dp")),
            P(),
        ),
        check_vma=False,
    )
```

time: 1580 us -> 922 us (0.58)
  waiting for transfers between devices: 817 us -> 66.4 us
  Pallas kernels: 350 us -> 675 us
  matrix products: 153 us -> 4.86 us
  blocking collectives: 54.1 us -> 0 us
  other arithmetic: 87.7 us -> 67.6 us
    reduce_scatter x8 -> x3, waiting for transfers between devices: 514 us -> 20.6 us  [the longest x1 20.6 us: body(): lax.psum_scatter(g_gates.astype(low).reshape(n_dp, 2 * bw // n_dp, chans)...]
    pallas_call x5 -> x11, Pallas kernels: 335 us -> 668 us  [the longest x4 197 us: multiply_scatter(): pl.pallas_call(functools.partial(scatter_kernel, n_parts, across), out_sh...]
    dot_general x25 -> x8, matrix products: 153 us -> 4.86 us  [dot(): return lax.dot_general(a, b, (dims, ((), ())), preferred_element_type=f32)]
    all_gather x5 -> x0, waiting for transfers between devices: 116 us -> none  [the longest x4 116 us: gather_rows(): return lax.all_gather(local, ('row', 'col'), axis=0, tiled=True)]
    psum x2 -> x0, waiting for transfers between devices: 112 us -> none  [the longest x1 112 us: body(): sums = lax.psum(rows_all, ('dp', 'row', 'col'))]
    all_to_all x4 -> x2, waiting for transfers between devices: 48.4 us -> 10.2 us  [the longest x1 10.2 us: body(): recs = lax.all_to_all(sum_rec, 'col', 0, 0)]
    all_to_all x2 -> x0, blocking collectives: 38 us -> none  [the longest x1 22.2 us: own_rows(): dealt = lax.all_to_all(x.reshape(n_col, own, part), 'col', 0, 0)]
    all_gather x1 -> x0, blocking collectives: 16.1 us -> none  [body(): gains_all = lax.all_gather(gains, 'col', axis=1, tiled=True)]
  transfers between devices with their start and end apart: 26 -> 10, of which waited for: 20 -> 6; matrix products, arithmetic and copies ran while one was open for 9% -> 11% of each run, Pallas kernels for 21% -> 31%
where the time goes in v2:
time: 922 us; the launch traced here: 910 us
  Pallas kernels  675 us (73%)
  other arithmetic  67.6 us (7%)
  waiting for transfers between devices  66.4 us (7%)
  local copies, waits for them, and re-layouts  59.3 us (6%)
  starting transfers between devices  21 us (2%)
  between operations  15.5 us (2%)
    pallas_call x4, Pallas kernels, multiply_scatter(): pl.pallas_call(functools.partial(scatter_kernel, n_parts, across), out_sh...  197 us
    pallas_call x1, Pallas kernels, rec_forward(): pl.pallas_call(functools.partial(forward_kernel, geo), out_shape=tuple((o...  181 us
    pallas_call x1, Pallas kernels, open_gather(): pl.pallas_call(functools.partial(open_kernel, geo), out_shape=(jax.ShapeD...  70.4 us
    pallas_call x2, Pallas kernels, outer_pair(): pl.pallas_call(functools.partial(outer_kernel, n_dp, steps1), grid=(n_col...  63.4 us
    pallas_call x1, Pallas kernels, sum_everywhere(): pl.pallas_call(functools.partial(sums_kernel, far, split), out_shape=(jax...  62.3 us
    pallas_call x1, Pallas kernels, glu(): pl.pallas_call(functools.partial(glu_kernel, spare), out_shape=(jax.Shape...  54.1 us
    pallas_call x1, Pallas kernels, gather_branch(): pl.pallas_call(branch_kernel, out_shape=(jax.ShapeDtypeStruct((slots, own...  39.7 us
    reduce_scatter x1, waiting for transfers between devices, body(): lax.psum_scatter(g_gates.astype(low).reshape(n_dp, 2 * bw // n_dp, chans)...  20.6 us
  transfers between devices with their start and end apart: 10, of which 6 were waited for; matrix products, arithmetic and copies ran while one was open for 11% of the time, Pallas kernels for 31%

profile of v2, /device:TPU:0, one launch (start us, length us, event | category | flops | bytes accessed | tf_op | source)
XLA Modules:
  0.0 910.0 jit_solution(16220037820971358769)
XLA Ops:
  12.0 70.4 %open_gather.1 = (bf16[1536,2560]{1,0:T(8,128)(2,1)}, bf16[2560,896]{1,0:T(8,128)(2,1)}, f32[4,2,640]{2,1,0:T(2,128)}) custom-call(bf16[768,640]{1,0:T(8,128)(2,1)} %tokens.1, bf16[2,640,1280]{2,1,0:T(8,128)(2,1)} %rec_in.1, f32[2,640]{1,0:T(2,128)} %gains.1), custom_call_target="tpu_custom_call" | custom-call | tf_op jit(solution)/shard_map/open_gather/pallas_call | solution.py:302
  91.1 181.1 %rec_forward.1 = (bf16[1536,2560]{1,0:T(8,128)(2,1)}, f32[1544,512]{1,0:T(8,128)}, f32[1536,384]{1,0:T(8,128)}, f32[1536,768]{1,0:T(8,128)}, bf16[1536,512]{1,0:...) custom-call(bf16[1536,2560]{1,0:T(8,128)(2,1)} %get-tuple-element.50, ...), custom_call_target="tpu_custom_call" | custom-call | tf_op jit(solution)/shard_map/rec_forward/pallas_call | solution.py:916
  272.2 43.8 %out_one.1 = f32[192,2560]{1,0:T(8,128)} custom-call(bf16[1536,384]{1,0:T(8,128)(2,1)} %get-tuple-element.53.act.right2, bf16[384,2560]{1,0:T(8,128)(2,1)} %get-tuple-element.54.w), custom_call_target="tpu_custom_call" | custom-call | flops 3019898880 | bytes 41943040 | tf_op jit(solution)/shard_map/out_one/pallas_call | solution.py:591
  321.0 54.1 %glu.1 = (bf16[8,192,2560]{2,1,0:T(8,128)(2,1)}, bf16[1536,1024]{1,0:T(8,128)(2,1)}, bf16[1536,2048]{1,0:T(8,128)(2,1)}) custom-call(bf16[192,2560]{1,0:T(8,128)(2,1)} %multiply_convert_fusion.n2, bf16[2,2560,1024]{2,1,0:T(8,128)(2,1)} %get-tuple-element.57.w_in.w, bf16[1024,2560]{1,0:T(8,128)(2,1)} %get-tuple-element.58.w_down.w, ...), custom_call_target="tpu_custom_call" | custom-call | flops 24159191040 | bytes 62914560 | tf_op jit(solution)/shard_map/glu/pallas_call | solution.py:418
  377.1 41.6 %outer_mlp.1 = bf16[4,4,160,3072]{3,2,1,0:T(8,128)(2,1)} custom-call(bf16[1536,2560]{1,0:T(8,128)(2,1)} %bitcast.170, bf16[1536,2048]{1,0:T(8,128)(2,1)} %get-tuple-element.62.right1.act, bf16[1536,2560]{1,0:T(8,128)(2,1)} %get-tuple-element.56.g_all.left2, bf16[1536,1024]{1,0:T(8,128)(2,1)S(1)} %copy-done.5), custom_call_target="tpu_custom_call" | custom-call | flops 24159191040 | bytes 40894464 | tf_op jit(solution)/shard_map/outer_mlp/pallas_call | solution.py:1017
  419.5 58.9 %d_normed_two.1 = f32[192,2560]{1,0:T(8,128)} custom-call(bf16[1536,2048]{1,0:T(8,128)(2,1)} %get-tuple-element.62.right1.act, bf16[2,2560,1024]{2,1,0:T(8,128)(2,1)} %get-tuple-element.57.w_in.w), custom_call_target="tpu_custom_call" | custom-call | flops 16106127360 | bytes 41943040 | tf_op jit(solution)/shard_map/d_normed_two/pallas_call | solution.py:591
  485.9 39.7 %gather_branch.1 = (bf16[8,192,2560]{2,1,0:T(8,128)(2,1)}, f32[1536,384]{1,0:T(8,128)S(1)}) custom-call(bf16[192,2560]{1,0:T(8,128)(2,1)S(1)} %get-tuple-element.119.x, bf16[384,2560]{1,0:T(8,128)(2,1)S(1)} %copy-done.3), custom_call_target="tpu_custom_call" | custom-call | tf_op jit(solution)/shard_map/gather_branch/pallas_call | solution.py:486
  526.9 5.2 fusion.115
  532.2 7.5 scan_back.1
  551.4 4.0 slice.441
  572.4 8.5 convert_reduce_fusion.1
  588.6 14.0 %collective-permute-done.1 = bf16[1536,256]{1,0:T(8,128)(2,1)S(1)} collective-permute-done((bf16[1536,256]{1,0:T(8,128)(2,1)S(1)}, bf16[1536,256]{1,0:T(8,128)(2,1)S(1)}, u32[]{:S(2)}, u32[]{:S(2)}) %collective-permute-start.1) | collective-permute-done | bytes 786464 | tf_op jit(solution)/shard_map/ppermute | solution.py:1201
  604.7 4.2 fusion.44
  611.2 5.1 collective-permute-done.2
  621.5 21.9 %outer_rec.1 = bf16[4,4,160,1152]{3,2,1,0:T(8,128)(2,1)} custom-call(bf16[1536,2560]{1,0:T(8,128)(2,1)} %get-tuple-element.55.left1, bf16[1536,768]{1,0:T(8,128)(2,1)S(1)} %pad_maximum_fusion.3.right1.act, bf16[1536,2560]{1,0:T(8,128)(2,1)} %bitcast.169, bf16[1536,384]{1,0:T(8,128)(2,1)S(1)} %copy-done.4), custom_call_target="tpu_custom_call" | custom-call | flops 9059696640 | bytes 25165824 | tf_op jit(solution)/shard_map/outer_rec/pallas_call | solution.py:1017
  643.3 46.5 %d_normed_one.1 = f32[192,2560]{1,0:T(8,128)} custom-call(bf16[1536,768]{1,0:T(8,128)(2,1)} %copy-done.2, bf16[2560,768]{1,0:T(8,128)(2,1)} %pad_maximum_fusion.w), custom_call_target="tpu_custom_call" | custom-call | flops 6039797760 | bytes 41943040 | tf_op jit(solution)/shard_map/d_normed_one/pallas_call | solution.py:591
  690.8 20.6 %reduce-scatter.6.cloned.1.call-done = bf16[1,128,384]{2,1,0:T(8,128)(2,1)} async-done(((bf16[4,128,384]{2,1,0:T(8,128)(2,1)}), bf16[1,128,384]{2,1,0:T(8,128)(2,1)}) %reduce-scatter.6.cloned.1.call-update) | async-done | bytes 98320 | tf_op jit(solution)/shard_map/reduce_scatter | solution.py:1266
  712.4 47.7 %out_two.1 = f32[192,2560]{1,0:T(8,128)} custom-call(bf16[1536,1024]{1,0:T(8,128)(2,1)} %get-tuple-element.76.right2.act, bf16[1024,2560]{1,0:T(8,128)(2,1)} %get-tuple-element.58.w_down.w), custom_call_target="tpu_custom_call" | custom-call | flops 8053063680 | bytes 41943040 | tf_op jit(solution)/shard_map/out_two/pallas_call | solution.py:591
  763.8 4.0 all-to-all-start
  773.7 6.6 all-to-all-done
  787.3 9.9 %all-to-all-done.1 = bf16[4,192,640]{2,1,0:T(8,128)(2,1)S(1)} async-done(((bf16[4,192,640]{2,1,0:T(8,128)(2,1)}), bf16[4,192,640]{2,1,0:T(8,128)(2,1)S(1)}, u32[]{:S(2)}, u32[]{:S(2)}) %all-to-all-start.1) | async-done | bytes 983072 | tf_op jit(solution)/shard_map/all_to_all | solution.py:1105
  798.1 4.9 all-to-all-start.3
  803.0 62.3 %small_sums.1 = (f32[8,768]{1,0:T(8,128)}, f32[4,8,384]{2,1,0:T(8,128)}, bf16[4,4,128,384]{3,2,1,0:T(8,128)(2,1)}) custom-call(f32[8,1152]{1,0:T(8,128)} %select_maximum_fusion.mixed, bf16[128,384]{1,0:T(8,128)(2,1)} %bitcast.162), custom_call_target="tpu_custom_call" | custom-call | tf_op jit(solution)/shard_map/small_sums/pallas_call | solution.py:676
  888.3 10.2 %all-to-all-done.2 = bf16[4,160,1152]{2,1,0:T(8,128)(2,1)S(1)} async-done(((bf16[4,160,1152]{2,1,0:T(8,128)(2,1)}), bf16[4,160,1152]{2,1,0:T(8,128)(2,1)S(1)}, u32[]{:S(2)}, u32[]{:S(2)}) %all-to-all-start.2) | async-done | bytes 1474592 | tf_op jit(solution)/shard_map/all_to_all | solution.py:1297
  (277 shorter events, 122.2 us)
Async XLA Ops:
  7.2 682.6 %reduce-scatter.4.cloned.1.call-start = ((), (), s32[]{:S(2)}) async-start(), calls=%async_computation.7 | async-start | bytes 19660800 | tf_op jit(solution)/shard_map/reduce_scatter | solution.py:1179
  8.0 80.6 %copy-start.57 = (f32[1,128]{1,0:T(1,128)}, f32[1,128]{1,0:T(1,128)S(1)}, u32[]{:S(2)}) copy-start(f32[1,128]{1,0:T(1,128)S(1)} %dynamic-slice_bitcast_fusion.10) | copy-start | bytes 1540
  8.8 516.8 %copy-start.35 = (f32[256]{0:T(256)}, f32[256]{0:T(256)S(1)}, u32[]{:S(2)}) copy-start(f32[256]{0:T(256)S(1)} %dynamic_slice.58) | copy-start | bytes 3076
  319.2 162.7 %copy-start.6 = (f32[192,2560]{1,0:T(8,128)}, f32[192,2560]{1,0:T(8,128)S(1)}, u32[]{:S(2)}) copy-start(f32[192,2560]{1,0:T(8,128)S(1)} %get-tuple-element.122) | copy-start | bytes 5898244
  418.7 292.7 %reduce-scatter.6.cloned.1.call-start = ((), (), s32[]{:S(2)}) async-start(), calls=%async_computation.8 | async-start | bytes 491520 | tf_op jit(solution)/shard_map/reduce_scatter | solution.py:1266
  478.4 48.5 %slice-start = ((s8[4718592]{0:T(1024)(128)(4,1)}), s8[4194304]{0:T(1024)(128)(4,1)S(1)}, s32[]{:S(2)}) async-start(s8[4718592]{0:T(1024)(128)(4,1)} %bitcast.145), calls=%async_computation.10 | async-start | bytes 8388608
  481.9 45.0 %slice-start.1 = ((s8[4718592]{0:T(1024)(128)(4,1)}), s8[524288]{0:T(1024)(128)(4,1)S(1)}, s32[]{:S(2)}) async-start(s8[4718592]{0:T(1024)(128)(4,1)} %bitcast.145), calls=%async_computation.11 | async-start | bytes 1048576
  481.9 45.0 %copy-start.20 = (f32[1536,384]{1,0:T(8,128)S(1)}, f32[1536,384]{1,0:T(8,128)}, u32[]{:S(2)}) copy-start(f32[1536,384]{1,0:T(8,128)} %get-tuple-element.64) | copy-start | bytes 7077892
  485.8 41.1 %copy-start.8 = (f32[1536,384]{1,0:T(8,128)S(1)}, f32[1536,384]{1,0:T(8,128)}, u32[]{:S(2)}) copy-start(f32[1536,384]{1,0:T(8,128)} %get-tuple-element.70) | copy-start | bytes 7077892
  540.9 27.6 %collective-permute-start = (f32[8,384]{1,0:T(8,128)}, f32[8,384]{1,0:T(8,128)}, u32[]{:S(2)}, u32[]{:S(2)}) collective-permute-start(f32[8,384]{1,0:T(8,128)} %slice.386), channel_id=1, source_target_pairs={{8,0},{16,8},{24,16},{9,1},{17,9},{25,17},{10,2},{18,10},{26,18},{... | collective-permute-start | bytes 36872 | tf_op jit(solution)/shard_map/ppermute | solution.py:1045
  582.5 20.1 %collective-permute-start.1 = (bf16[1536,256]{1,0:T(8,128)(2,1)S(1)}, bf16[1536,256]{1,0:T(8,128)(2,1)S(1)}, u32[]{:S(2)}, u32[]{:S(2)}) collective-permute-start(bf16[1536,256]{1,0:T(8,128)(2,1)S(1)} %pad_maximum_fusion.6), channel_id=1, source_target_pairs={{0,2},{1,3},{2,0},{3,1},{4,6},{5,7},{6,4},{7,5},{8,10},{9,11},{10,... | collective-permute-start | bytes 2359304 | tf_op jit(solution)/shard_map/ppermute | solution.py:1201
  587.3 15.4 %copy-start.27 = (bf16[2,1,256,256]{3,2,1,0:T(8,128)(2,1)S(1)}, bf16[2,1,256,256]{3,2,1,0:T(8,128)(2,1)}, u32[]{:S(2)}) copy-start(bf16[2,1,256,256]{3,2,1,0:T(8,128)(2,1)} %copy-done.26) | copy-start | bytes 786436
  604.7 11.7 %copy-start.40 = (pred[1536]{0:T(1024)(128)(4,1)S(1)}, pred[1536]{0:T(1024)(128)(4,1)}, u32[]{:S(2)}) copy-start(pred[1536]{0:T(1024)(128)(4,1)} %get-tuple-element.181) | copy-start | bytes 4612
  604.7 11.7 %copy-start.41 = (pred[1536]{0:T(1024)(128)(4,1)S(1)}, pred[1536]{0:T(1024)(128)(4,1)}, u32[]{:S(2)}) copy-start(pred[1536]{0:T(1024)(128)(4,1)} %get-tuple-element.187) | copy-start | bytes 4612
  608.9 7.4 collective-permute-start.2
  620.1 23.3 %copy-start.2 = (bf16[1536,768]{1,0:T(8,128)(2,1)}, bf16[1536,768]{1,0:T(8,128)(2,1)S(1)}, u32[]{:S(2)}) copy-start(bf16[1536,768]{1,0:T(8,128)(2,1)S(1)} %pad_maximum_fusion.3.right1.act) | copy-start | bytes 7077892
  643.3 46.5 %copy-start.22 = (bf16[2,256,384]{1,2,0:T(8,128)(2,1)S(1)}, bf16[2,256,384]{1,2,0:T(8,128)(2,1)}, u32[]{:S(2)}) copy-start(bf16[2,256,384]{1,2,0:T(8,128)(2,1)} %pad_maximum_fusion.8) | copy-start | bytes 1179652
  690.8 188.3 %reduce-scatter.8.cloned.1.call-start = ((), (), s32[]{:S(2)}) async-start(), calls=%async_computation.9 | async-start | bytes 7372800 | tf_op jit(solution)/shard_map/reduce_scatter | solution.py:1270
  712.4 47.7 %copy-start.7 = (f32[192,2560]{1,0:T(8,128)S(1)}, f32[192,2560]{1,0:T(8,128)}, u32[]{:S(2)}) copy-start(f32[192,2560]{1,0:T(8,128)} %copy-done.6) | copy-start | bytes 5898244
  763.8 16.5 %all-to-all-start = ((bf16[4,192,640]{2,1,0:T(8,128)(2,1)}), bf16[4,192,640]{2,1,0:T(8,128)(2,1)S(1)}, u32[]{:S(2)}, u32[]{:S(2)}) async-start(bf16[4,192,640]{2,1,0:T(8,128)(2,1)} %bitcast.154), calls=%async_computation.1 | async-start | bytes 1966080 | tf_op jit(solution)/shard_map/all_to_all | solution.py:1105
  780.4 16.8 %copy-start.15 = (bf16[4,192,640]{2,1,0:T(8,128)(2,1)}, bf16[4,192,640]{2,1,0:T(8,128)(2,1)S(1)}, u32[]{:S(2)}) copy-start(bf16[4,192,640]{2,1,0:T(8,128)(2,1)S(1)} %all-to-all-done) | copy-start | bytes 2949124
  780.4 16.8 %all-to-all-start.1 = ((bf16[4,192,640]{2,1,0:T(8,128)(2,1)}), bf16[4,192,640]{2,1,0:T(8,128)(2,1)S(1)}, u32[]{:S(2)}, u32[]{:S(2)}) async-start(bf16[4,192,640]{2,1,0:T(8,128)(2,1)} %bitcast.139), calls=%async_computation.2 | async-start | bytes 1966080 | tf_op jit(solution)/shard_map/all_to_all | solution.py:1105
  798.1 75.7 %all-to-all-start.3 = ((bf16[4,160,3072]{2,1,0:T(8,128)(2,1)}), bf16[4,160,3072]{2,1,0:T(8,128)(2,1)}, u32[]{:S(2)}, u32[]{:S(2)}) async-start(bf16[4,160,3072]{2,1,0:T(8,128)(2,1)} %bitcast.151), calls=%async_computation.6 | async-start | bytes 7864320 | tf_op jit(solution)/shard_map/all_to_all | solution.py:1292
  879.1 19.4 %all-to-all-start.2 = ((bf16[4,160,1152]{2,1,0:T(8,128)(2,1)}), bf16[4,160,1152]{2,1,0:T(8,128)(2,1)S(1)}, u32[]{:S(2)}, u32[]{:S(2)}) async-start(bf16[4,160,1152]{2,1,0:T(8,128)(2,1)} %bitcast.158), calls=%async_computation.5 | async-start | bytes 2949120 | tf_op jit(solution)/shard_map/all_to_all | solution.py:1297
  (49 other events, 164.2 us)
Sparse Core Ops, SparseCore 0:
  418.8 263.5 reduce-scatter.3
  690.9 20.4 reduce-scatter.5
  713.8 109.7 reduce-scatter.7

commit v3 on v2

--- a/solution.py
+++ b/solution.py
@@ -16,10 +16,6 @@
 f32 = jnp.float32
 anywhere = pl.BlockSpec(memory_space=pl.ANY)
 in_vmem = pl.BlockSpec(memory_space=pltpu.VMEM)
-
-
-def gelu(values):
-    return jax.nn.gelu(values, approximate=True)
 
 
 def window_tile(col, tiles, n_col, wide):
@@ -103,7 +99,7 @@
 
 
 def share(rows):
-    far = rows * 9 // 20 // ROWS * ROWS
+    far = rows * 2 // 5 // ROWS * ROWS
     return rows - far, far
 
 
@@ -204,7 +200,11 @@
             for h in range(2)
         ]
     if mlp_out is not None:
-        found["mlp_out"] = [down_piece(mlp_out, w_down, win, span, 0)]
+        half = span // 2
+        found["mlp_out"] = [
+            down_piece(mlp_out, w_down, lambda chip, h=h: win(chip) + h * half, half, h * half)
+            for h in range(2)
+        ]
     return found
 
 
@@ -446,78 +446,25 @@
     return n_all.reshape(group, width), h, d
 
 
-def branch_kernel(x, w, x_all, y, buf, wv, send, recv, local):
+def scatter_kernel(shape, finish, n_more, n_outs, homes, act, w, *refs):
+    n_parts, across, own, width = shape
+    more, refs = refs[:n_more], refs[n_more:]
+    outs, refs = refs[:n_outs], refs[n_outs:]
+    actv, wv, other, mine, from_core, from_x, from_y, turn, fin, back, send, recv, local, home_sem = refs[:14]
+    held = refs[14:]
     place = Place()
-    place.meet(("x", "y", "core"))
+    place.meet(("x", "y", "xy", "core") if homes else ("x", "y", "core"))
     copies = Copies(place, send, recv)
-    own = x.shape[0]
-    n_col = buf.shape[0] // 2
-    gather = slot_gather(copies, x, buf, own)
-    me = place.row * n_col + place.col
-    load = copies.keep(w, wv, local.at[0])
-    mine = copies.keep(x, buf.at[me], local.at[1])
-    load.wait()
-    mine.wait()
-
-    def work(chip):
-        slots = (chip, n_col + chip)
-        value = dot(jnp.concatenate([buf[s] for s in slots], axis=0), wv[...], ((1,), (1,)))
-        for n, s in enumerate(slots):
-            y[pl.ds(pl.multiple_of(s * own, ROWS), own), :] = value[n * own : (n + 1) * own]
-
-    copies.land(gather.own)
-    work(place.col)
-    gather.pass_on()
-    copies.land(gather.core_y)
-    work(place.chip(2))
-    gather.last()
-    copies.land(gather.core_x)
-    work(place.chip(1))
-    copies.land(gather.core_xy)
-    out = copies.keep(buf, x_all, local.at[2])
-    work(place.chip(3))
-    copies.finish()
-    out.wait()
-
-
-def gather_branch(x, w):
-    own, width = x.shape
-    slots = 2 * lax.axis_size("col")
-    x_all, y = pl.pallas_call(
-        branch_kernel,
-        out_shape=(
-            jax.ShapeDtypeStruct((slots, own, width), low),
-            jax.ShapeDtypeStruct((slots * own, w.shape[0]), f32),
-        ),
-        in_specs=[anywhere] * 2,
-        out_specs=(anywhere, in_vmem),
-        scratch_shapes=[
-            pltpu.VMEM((slots, own, width), low),
-            pltpu.VMEM(w.shape, low),
-            pltpu.SemaphoreType.DMA((10,)),
-            pltpu.SemaphoreType.DMA((10,)),
-            pltpu.SemaphoreType.DMA((3,)),
-        ],
-        compiler_params=pltpu.CompilerParams(
-            collective_id=4, has_side_effects=True, vmem_limit_bytes=48 * MIB
-        ),
-        name="gather_branch",
-    )(x, w)
-    return x_all.reshape(slots * own, width), y
-
-
-def scatter_kernel(
-    n_parts, across, act, w, out, actv, wv, other, mine, from_core, from_x, from_y, turn, send, recv, local
-):
-    place = Place()
-    place.meet(("x", "y", "core"))
-    copies = Copies(place, send, recv)
-    own, width = out.shape
     cut = own // 2
     n_col = act.shape[0] // own // 2
     k = act.shape[1] // n_parts
     step = 256
     loads = [copies.keep(act, actv, local.at[0]), copies.keep(w, wv, local.at[1])]
+    my_rows = pl.ds(pl.multiple_of((place.row * n_col + place.col) * own, ROWS), own)
+    extra = []
+    for i, (ref, buf) in enumerate(zip(more, held)):
+        src = ref.at[my_rows, :] if ref.shape[0] > own else ref
+        extra.append(copies.keep(src, buf, local.at[2 + i]))
     for load in loads:
         load.wait()
     top, bottom = pl.ds(0, cut), pl.ds(cut, cut)
@@ -577,22 +524,50 @@
     x_last = copies.start(turn.at[1, bottom, :], from_x.at[2], "x")
     add_core(0, core0)
     copies.land(x1, y2, y_last, x_last)
-    out[top, :] = mine[0, top, :] + from_x[1].astype(f32) + from_y[2].astype(f32)
-    out[bottom, :] = mine[0, bottom, :] + from_y[1].astype(f32) + from_x[2].astype(f32)
+    fin[top, :] = mine[0, top, :] + from_x[1].astype(f32) + from_y[2].astype(f32)
+    fin[bottom, :] = mine[0, bottom, :] + from_y[1].astype(f32) + from_x[2].astype(f32)
+    for load in extra:
+        load.wait()
+    for ref in outs[(1 if homes else 0) :]:
+        if ref.shape[0] == 8:
+            ref[...] = jnp.zeros_like(ref)
+    rows_at_once = 64
+
+    def rows_done(i, carry):
+        rows = pl.ds(pl.multiple_of(i * rows_at_once, rows_at_once), rows_at_once)
+        finish(rows, fin, held, back, outs[(1 if homes else 0) :])
+        return carry
+
+    lax.fori_loop(0, own // rows_at_once, rows_done, 0)
+    if homes:
+        home = outs[0]
+        part = width // n_col
+
+        def columns_of(chip):
+            return back.at[:, pl.ds(pl.multiple_of(chip * part, LANES), part)]
+
+        spot = home.at[pl.ds(pl.multiple_of(place.col * own, ROWS), own), :]
+        for name, j in (("xy", 3), ("x", 1), ("y", 2)):
+            copies.start(columns_of(place.chip(j)), spot, name)
+        stay = copies.keep(columns_of(place.col), spot, home_sem)
+        stay.wait()
     copies.finish()
 
 
-def multiply_scatter(act, w, across, number, name):
+def multiply_scatter(act, w, across, number, name, finish, more, outs, homes):
     n_parts = w.shape[0] if w.ndim == 3 else 1
     group = act.shape[0]
-    slots = 2 * lax.axis_size("col")
-    own = group // slots
+    n_col = lax.axis_size("col")
+    own = group // (2 * n_col)
     width = w.shape[-2] if across else w.shape[-1]
+    held = [((own, r.shape[1]) if r.shape[0] > own else r.shape, r.dtype) for r in more]
     return pl.pallas_call(
-        functools.partial(scatter_kernel, n_parts, across),
-        out_shape=jax.ShapeDtypeStruct((own, width), f32),
-        in_specs=[anywhere] * 2,
-        out_specs=in_vmem,
+        functools.partial(
+            scatter_kernel, (n_parts, across, own, width), finish, len(more), len(outs), homes
+        ),
+        out_shape=tuple(jax.ShapeDtypeStruct(*s) for s in outs),
+        in_specs=[anywhere] * (2 + len(more)),
+        out_specs=tuple(anywhere if homes and i == 0 else in_vmem for i in range(len(outs))),
         scratch_shapes=[
             pltpu.VMEM(act.shape, low),
             pltpu.VMEM(w.shape, low),
@@ -602,28 +577,142 @@
             pltpu.VMEM((3, own // 2, width), low),
             pltpu.VMEM((3, own // 2, width), low),
             pltpu.VMEM((4, own, width), low),
-            pltpu.SemaphoreType.DMA((10,)),
-            pltpu.SemaphoreType.DMA((10,)),
-            pltpu.SemaphoreType.DMA((2,)),
-        ],
+            pltpu.VMEM((own, width), f32),
+            pltpu.VMEM((own, width), low),
+            pltpu.SemaphoreType.DMA((13,)),
+            pltpu.SemaphoreType.DMA((13,)),
+            pltpu.SemaphoreType.DMA((2 + len(more),)),
+            pltpu.SemaphoreType.DMA,
+        ]
+        + [pltpu.VMEM(*h) for h in held],
         compiler_params=pltpu.CompilerParams(
-            collective_id=number, has_side_effects=True, vmem_limit_bytes=58 * MIB
+            collective_id=number, has_side_effects=True, vmem_limit_bytes=60 * MIB
         ),
         cost_estimate=pl.CostEstimate(
             flops=2 * group * width * act.shape[1], bytes_accessed=40 * MIB, transcendentals=0
         ),
         name=name,
-    )(act, w)
-
-
-def sums_kernel(far, split, mixed, gate_part, sums_out, chans_out, gates_out, got, acc, ch, send, recv, local):
+    )(act, w, *more)
+
+
+def square_sum(ref, row, x):
+    ref[row : row + 1, :] += jnp.broadcast_to(jnp.sum(x * x, keepdims=True), (1, LANES))
+
+
+def norm_scale(x):
+    return lax.rsqrt(jnp.mean(x * x, axis=-1, keepdims=True) + epsilon)
+
+
+def after_out_one(rows, fin, held, back, outs):
+    x, gain = held
+    resid_out, n2_out, squares = outs
+    out_one = fin[rows, :]
+    resid = x[rows, :].astype(f32) + out_one
+    resid_out[rows, :] = resid
+    n2_out[rows, :] = (resid * norm_scale(resid) * gain[1:2, :]).astype(low)
+    square_sum(squares, 0, out_one)
+    square_sum(squares, 1, resid)
+
+
+def norm_back(d_normed, x, gain, grad_gain):
+    scale = norm_scale(x)
+    gained = gain * d_normed
+    inner = jnp.mean(gained * x, axis=-1, keepdims=True)
+    grad_gain[0:1, :] += jnp.sum(d_normed * x * scale, axis=0, keepdims=True)
+    return scale * gained - x * (scale * scale * scale * inner)
+
+
+def after_normed_two(rows, fin, held, back, outs):
+    resid, upstream, gain = held
+    d_resid_out, d_out, grad_gain = outs
+    d_resid = upstream[rows, :].astype(f32) + norm_back(
+        fin[rows, :], resid[rows, :], gain[1:2, :], grad_gain
+    )
+    d_resid_out[rows, :] = d_resid
+    d_out[rows, :] = d_resid.astype(low)
+
+
+def after_normed_one(rows, fin, held, back, outs):
+    x, d_resid, gain = held
+    grad_gain, squares = outs
+    x_here = x[rows, :].astype(f32)
+    passed = norm_back(fin[rows, :], x_here, gain[0:1, :], grad_gain)
+    back[rows, :] = (d_resid[rows, :] + passed).astype(low)
+    square_sum(squares, 0, x_here)
+
+
+def after_out_two(rows, fin, held, back, outs):
+    (resid,) = held
+    (squares,) = outs
+    out_two = fin[rows, :]
+    back[rows, :] = (resid[rows, :] + out_two).astype(low)
+    square_sum(squares, 0, out_two)
+
+
+def start_deal(copies, source, target):
+    col = copies.place.col
+    for name, j in (("xy", 3), ("x", 1), ("y", 2)):
+        copies.start(source.at[copies.place.chip(j)], target.at[col], name)
+
+
+def deal_kernel(source, target, send, recv, local):
+    place = Place()
+    place.meet(("x", "y", "xy"))
+    copies = Copies(place, send, recv)
+    start_deal(copies, source, target)
+    stay = copies.keep(source.at[place.col], target.at[place.col], local)
+    copies.finish()
+    stay.wait()
+
+
+def deal_back(x, number, name):
+    return pl.pallas_call(
+        deal_kernel,
+        out_shape=jax.ShapeDtypeStruct(x.shape, x.dtype),
+        in_specs=[anywhere],
+        out_specs=anywhere,
+        scratch_shapes=[
+            pltpu.SemaphoreType.DMA((3,)),
+            pltpu.SemaphoreType.DMA((3,)),
+            pltpu.SemaphoreType.DMA,
+        ],
+        compiler_params=pltpu.CompilerParams(collective_id=number, has_side_effects=True),
+        name=name,
+    )(x)
+
+
+def sums_kernel(
+    far,
+    split,
+    mixed,
+    gate_part,
+    grads_a,
+    grads_b,
+    sums_out,
+    chans_out,
+    gates_out,
+    out_a,
+    out_b,
+    got,
+    acc,
+    ch,
+    send,
+    recv,
+    local,
+):
     place = Place()
     steps = [f"d{d}" for d in far if d & (d - 1) == 0]
-    place.meet(("core", "x", "y") + tuple(f"d{d}" for d in far))
+    place.meet(("core", "x", "y", "xy") + tuple(f"d{d}" for d in far))
     copies = Copies(place, send, recv)
     dp, col = place.dp, place.col
+    start_deal(copies, grads_a, out_a)
+    start_deal(copies, grads_b, out_b)
+    keeps = [
+        copies.keep(grads_a.at[col], out_a.at[col], local.at[1]),
+        copies.keep(grads_b.at[col], out_b.at[col], local.at[2]),
+    ]
     own_gates = gates_out.at[col]
-    stay = copies.keep(gate_part, own_gates.at[dp], local)
+    stay = copies.keep(gate_part, own_gates.at[dp], local.at[0])
     parts = [copies.start(gate_part, own_gates.at[dp], f"d{d}") for d in far]
     acc[0] = mixed[...]
     n = 0
@@ -666,12 +755,14 @@
     copies.land(y_ch)
     chans_out[...] = ch[...]
     copies.finish()
-
-
-def sum_everywhere(mixed, split, gate_part, n_dp, n_col):
+    for copy in keeps:
+        copy.wait()
+
+
+def sum_everywhere(mixed, split, gate_part, grads_a, grads_b, n_dp, n_col):
     far = tuple(range(1, n_dp))
     stages = len([d for d in far if d & (d - 1) == 0]) + 3
-    count = 2 * len(far) + stages + 8
+    count = 2 * len(far) + stages + 14
     rows, columns = mixed.shape
     return pl.pallas_call(
         functools.partial(sums_kernel, far, split),
@@ -679,20 +770,22 @@
             jax.ShapeDtypeStruct((rows, columns - split), f32),
             jax.ShapeDtypeStruct((n_col, rows, split), f32),
             jax.ShapeDtypeStruct((n_col, n_dp) + gate_part.shape, gate_part.dtype),
+            jax.ShapeDtypeStruct(grads_a.shape, grads_a.dtype),
+            jax.ShapeDtypeStruct(grads_b.shape, grads_b.dtype),
         ),
-        in_specs=[in_vmem, anywhere],
-        out_specs=(in_vmem, in_vmem, anywhere),
+        in_specs=[in_vmem] + [anywhere] * 3,
+        out_specs=(in_vmem, in_vmem) + (anywhere,) * 3,
         scratch_shapes=[
             pltpu.VMEM((stages, rows, columns), f32),
             pltpu.VMEM((stages + 1, rows, columns), f32),
             pltpu.VMEM((n_col, rows, split), f32),
             pltpu.SemaphoreType.DMA((count,)),
             pltpu.SemaphoreType.DMA((count,)),
-            pltpu.SemaphoreType.DMA,
+            pltpu.SemaphoreType.DMA((3,)),
         ],
         compiler_params=pltpu.CompilerParams(collective_id=5, has_side_effects=True),
         name="small_sums",
-    )(mixed, gate_part)
+    )(mixed, gate_part, grads_a, grads_b)
 
 
 def one_less_exp(z):
@@ -772,10 +865,8 @@
     found = weight_pieces(geo, (None, rec_out, mlp_in, mlp_out), (None, w_out, w_in, w_down))
     pieces = found["rec_out"] + found["mlp_in"] + found["mlp_out"]
     dealer = Dealer(copies)
-    dealer.deal(pieces[0])
-    dealer.deal(pieces[1])
-    dealer.deal(pieces[2])
-    dealer.deal(pieces[3])
+    for piece in pieces[:5]:
+        dealer.deal(piece)
     keep_own(copies, pieces, local, 2)
     for load in loads:
         load.wait()
@@ -844,13 +935,14 @@
     lax.fori_loop(0, third, work, 0)
     dealer.forward()
     dealer.forward()
-    dealer.deal(pieces[4])
+    dealer.deal(pieces[5])
     dealer.forward()
     lax.fori_loop(third, 2 * third, work, 0)
     dealer.forward()
-    gather = block_gather(copies, cotangent, g_all, local.at[9])
-    dealer.deal(pieces[5])
+    dealer.deal(pieces[6])
     lax.fori_loop(2 * third, n_tiles, work, 0)
+    dealer.forward()
+    dealer.deal(pieces[7])
     state_in = copies.start(hv.at[pl.ds(group - 8, 8), :], first, "next")
     outs = [
         copies.keep(src, dst, local.at[10 + i])
@@ -858,8 +950,6 @@
             ((xv, n1_out), (xb, x_out), (yv, y_out), (prev, pre_out), (cv, c_out))
         )
     ]
-    dealer.forward()
-    dealer.deal(pieces[6])
     copies.land(state_in)
     copies.leave(state_in)
     before_all = first[7:8, :]
@@ -884,9 +974,11 @@
         copies.keep(first, first_out, local.at[17]),
     ]
     dealer.forward()
+    gather = block_gather(copies, cotangent, g_all, local.at[18])
+    dealer.forward()
+    dealer.forward()
     gather.pass_on()
     gather.last()
-    dealer.forward()
     copies.finish()
     for copy in copies.local:
         if not any(copy is load for load in loads):
@@ -912,7 +1004,7 @@
         ((8, chans), f32),
     ]
     dealt = [((group, width), low), ((chans, width), low), ((2, width, span), low), ((span, width), low)]
-    copy_count = 1 + 6 * 7 + 10 + 1
+    copy_count = 1 + 6 * 8 + 10 + 1
     return pl.pallas_call(
         functools.partial(forward_kernel, geo),
         out_shape=tuple(of(*s) for s in kept + dealt),
@@ -933,7 +1025,7 @@
             pltpu.VMEM((8, chans), f32),
             pltpu.SemaphoreType.DMA((copy_count,)),
             pltpu.SemaphoreType.DMA((copy_count,)),
-            pltpu.SemaphoreType.DMA((18,)),
+            pltpu.SemaphoreType.DMA((19,)),
         ],
         compiler_params=pltpu.CompilerParams(
             collective_id=2, has_side_effects=True, vmem_limit_bytes=58 * MIB
@@ -942,52 +1034,302 @@
     )(x_all, w_rec, *params, places, cotangent, rec_out, mlp_in, mlp_out)
 
 
-def scan_kernel(reverse, a_ref, u_ref, h_ref, p_ref, carry):
-    step = pl.program_id(0)
-    rows = a_ref.shape[0]
-
-    @pl.when(step == 0)
-    def _():
-        carry[0:1] = jnp.zeros_like(carry[0:1])
-        carry[1:2] = jnp.ones_like(carry[1:2])
-
-    for lane in range(a_ref.shape[1] // LANES):
-        at = slice(lane * LANES, (lane + 1) * LANES)
-        a = a_ref[:, at]
-        u = u_ref[:, at]
-        index = lax.broadcasted_iota(jnp.int32, a.shape, 0)
-        by = 1
-        while by < rows:
-            turn = rows - by if reverse else by
-            inside = index < rows - by if reverse else index >= by
-            a_far = jnp.where(inside, pltpu.roll(a, turn, 0), 1.0)
-            u_far = jnp.where(inside, pltpu.roll(u, turn, 0), 0.0)
-            u = u + a * u_far
-            a = a * a_far
-            by *= 2
-        h = u + a * carry[0:1, at]
-        p = a * carry[1:2, at]
-        h_ref[:, at] = h
-        p_ref[:, at] = p
-        edge = 0 if reverse else rows - 1
-        carry[0:1, at] = h[edge : edge + 1]
-        carry[1:2, at] = p[edge : edge + 1]
-
-
-def scan_rows(decay, inject, reverse, rows=256):
-    length, channels = decay.shape
-    steps = length // rows
-    block = pl.BlockSpec((rows, channels), lambda i: (steps - 1 - i if reverse else i, 0))
-    shape = jax.ShapeDtypeStruct(decay.shape, f32)
-    return pl.pallas_call(
-        functools.partial(scan_kernel, reverse),
-        grid=(steps,),
-        out_shape=(shape, shape),
-        in_specs=[block, block],
-        out_specs=(block, block),
-        scratch_shapes=[pltpu.VMEM((8, channels), f32)],
-        name="scan_back" if reverse else "scan",
-    )(decay, inject)
+def backward_kernel(
+    geo,
+    d_out,
+    w_out,
+    y_in,
+    state_in,
+    first_in,
+    pre_in,
+    c_in,
+    x_in,
+    gates_blk,
+    gates_rows,
+    soft,
+    conv_w,
+    places,
+    d_all,
+    d_rec_out,
+    gate_out,
+    sums,
+    buf,
+    wv,
+    dbv,
+    yv,
+    hs,
+    prev,
+    cv,
+    xb,
+    ghv,
+    qv,
+    dpv,
+    there,
+    dcv,
+    drv,
+    gg,
+    glo,
+    gfar,
+    carry,
+    message,
+    send,
+    recv,
+    local,
+):
+    place = Place()
+    n_dp = glo.shape[0]
+    far = [f"d{d}" for d in range(1, n_dp)]
+    place.meet(["x", "y", "core", "next", "prev"] + far)
+    copies = Copies(place, send, recv)
+    n_col, part, bw, tiles, wide = geo
+    chans = bw + LANES
+    own = d_out.shape[0]
+    group = yv.shape[0]
+    tile = 256
+    n_tiles = group // tile
+    lanes = [slice(k * LANES, (k + 1) * LANES) for k in range(chans // LANES)]
+    gather = slot_gather(copies, d_out, buf, own)
+    me = place.row * n_col + place.col
+    load = copies.keep(w_out, wv, local.at[0])
+    mine = copies.keep(d_out, buf.at[me], local.at[1])
+    loads = [
+        copies.keep(src, dst, local.at[2 + i])
+        for i, (src, dst) in enumerate(
+            (
+                (y_in, yv),
+                (state_in, hs.at[pl.ds(8, group), :]),
+                (first_in, hs.at[pl.ds(0, 8), :]),
+                (pre_in, prev),
+                (c_in, cv),
+                (x_in, xb),
+            )
+        )
+    ]
+    load.wait()
+    mine.wait()
+    high_tile = place.col >= 2
+    idle_tile = lax.rem(place.col, 2) == 1
+
+    def work(chip):
+        slots = (chip, n_col + chip)
+        value = dot(jnp.concatenate([buf[s] for s in slots], axis=0), wv[...], ((1,), (1,)))
+        for n, s in enumerate(slots):
+            rows = pl.ds(pl.multiple_of(s * own, ROWS), own)
+            dbv[rows, :] = value[n * own : (n + 1) * own]
+
+    copies.land(gather.own)
+    work(place.col)
+    gather.pass_on()
+    copies.land(gather.core_y)
+    work(place.chip(2))
+    gather.last()
+    copies.land(gather.core_x)
+    work(place.chip(1))
+    copies.land(gather.core_xy)
+    out = copies.keep(buf, d_all, local.at[8])
+    work(place.chip(3))
+    for each in loads:
+        each.wait()
+
+    def coeffs(rows, at, spot):
+        rate = jax.nn.sigmoid(prev[rows, slice(chans + at.start, chans + at.stop)])
+        log_a = -8.0 * rate * soft[0:1, at]
+        return rate, log_a, jnp.where(spot == 0, 0.0, jnp.exp(log_a))
+
+    carry[0:1] = jnp.zeros_like(carry[0:1])
+    carry[1:2] = jnp.ones_like(carry[1:2])
+
+    def scan_back(k, unused):
+        r0 = pl.multiple_of((n_tiles - 1 - k) * tile, tile)
+        rows = pl.ds(r0, tile)
+        spot = places[rows, :]
+        last = lax.broadcasted_iota(jnp.int32, spot.shape, 0) == tile - 1
+        for at in lanes:
+            d_branch = dbv[rows, at]
+            if at.start >= bw:
+                d_branch = jnp.where(idle_tile, 0.0, d_branch)
+            value, slope = tanh_parts(yv[rows, at])
+            state = hs[pl.ds(pl.multiple_of(r0 + 8, 8), tile), at]
+            d_state = d_branch * value
+            drv[rows, slice(chans + at.start, chans + at.stop)] = (d_branch * state * slope).astype(low)
+            _, _, a = coeffs(rows, at, spot)
+            a, u = scan_tile(a, a * d_state, True)
+            m = u + a * carry[0:1, at]
+            q = a * carry[1:2, at]
+            ghv[rows, at] = d_state + jnp.where(last, carry[0:1, at], pltpu.roll(m, tile - 1, 0))
+            qv[rows, at] = jnp.where(last, carry[1:2, at], pltpu.roll(q, tile - 1, 0))
+            carry[0:1, at] = m[0:1]
+            carry[1:2, at] = q[0:1]
+        return unused
+
+    lax.fori_loop(0, n_tiles, scan_back, 0)
+    arriving = copies.start(carry, message, "prev")
+    copies.land(arriving)
+    sums[...] = jnp.zeros_like(sums)
+    gg[...] = jnp.zeros_like(gg)
+
+    def through_gates(k, unused):
+        r0 = pl.multiple_of(k * tile, tile)
+        rows = pl.ds(r0, tile)
+        spot = places[rows, :]
+        reset = spot == 0
+        for n, at in enumerate(lanes):
+            g = ghv[rows, at] + qv[rows, at] * message[0:1, at]
+            before = pltpu.roll(hs[pl.ds(r0, tile + 8), at], 1, 0)[8:]
+            if at.start < bw:
+                c = cv[rows, at].astype(f32)
+            else:
+                c = jnp.where(
+                    high_tile,
+                    cv[rows, slice(at.start + LANES, at.stop + LANES)].astype(f32),
+                    cv[rows, at].astype(f32),
+                )
+            gate = jax.nn.sigmoid(prev[rows, at])
+            rate, log_a, a = coeffs(rows, at, spot)
+            m = jnp.where(reset, 1.0, jnp.sqrt(one_less_exp(2.0 * log_a)))
+            gated = gate * m
+            d_log = jnp.where(reset, 0.0, g * before * a - g * c * gate * a * a / m)
+            d_pre_in = (g * c * gated * (1.0 - gate)).astype(low)
+            d_pre_rate = (d_log * (-8.0 * soft[0:1, at]) * rate * (1.0 - rate)).astype(low)
+            dpv[rows, at] = d_pre_in
+            dpv[rows, slice(chans + at.start, chans + at.stop)] = d_pre_rate
+            dcv[rows, at] = g * gated
+            sums[0:1, at] += jnp.sum(d_pre_in.astype(f32), axis=0, keepdims=True)
+            sums[1:2, at] += jnp.sum(d_pre_rate.astype(f32), axis=0, keepdims=True)
+            sums[2:3, at] += jnp.sum(d_log * (-8.0 * rate), axis=0, keepdims=True)
+        return unused
+
+    swaps = []
+    for h in range(2):
+        lax.fori_loop(h * n_tiles // 2, (h + 1) * n_tiles // 2, through_gates, 0)
+        rows = pl.ds(h * group // 2, group // 2)
+        for j in range(2):
+            swaps.append(
+                copies.start(
+                    dpv.at[rows, pl.ds(j * chans + bw, LANES)],
+                    there.at[rows, pl.ds(j * LANES, LANES)],
+                    "y",
+                )
+            )
+
+    def through_blocks(k, unused):
+        rows = pl.ds(pl.multiple_of(k * tile, tile), tile)
+        c = cv[rows, :]
+        d_blk = dcv[rows, :bw]
+        d_tile = dcv[rows, bw:]
+        for j in range(2):
+            p_blk = dpv[rows, slice(j * chans, j * chans + bw)]
+            here = dpv[rows, slice(j * chans + bw, (j + 1) * chans)]
+            far = there[rows, slice(j * LANES, (j + 1) * LANES)]
+            five = jnp.concatenate(
+                [jnp.where(high_tile, far, here), jnp.where(high_tile, here, far)], axis=1
+            )
+            d_blk = d_blk + dot(p_blk, gates_blk[j], ((1,), (1,)))
+            d_tile = d_tile + dot(five, gates_rows[j], ((1,), (1,)))
+            gg[j, :, :bw] += dot(c[:, :bw], p_blk, ((0,), (0,)))
+            gg[j, :, bw:] += dot(c[:, bw:], here, ((0,), (0,)))
+        dcv[rows, :bw] = d_blk
+        dcv[rows, bw:] = d_tile
+        return unused
+
+    copies.land(swaps[0], swaps[1])
+    lax.fori_loop(0, 1, through_blocks, 0)
+    later = copies.start(dcv.at[pl.ds(0, 8), :], dcv.at[pl.ds(group, 8), :], "prev")
+    lax.fori_loop(1, n_tiles // 2, through_blocks, 0)
+    copies.land(swaps[2], swaps[3])
+    lax.fori_loop(n_tiles // 2, n_tiles, through_blocks, 0)
+    part_rows = gate_out.shape[0]
+    for p in range(n_dp):
+        j, first_row = divmod(p * part_rows, bw)
+        glo[p] = gg[j, first_row : first_row + part_rows].astype(low)
+    parts = [
+        copies.start(glo.at[jnp.bitwise_xor(place.dp, d + 1)], gfar.at[d], name)
+        for d, name in enumerate(far)
+    ]
+    copies.land(later)
+
+    def through_conv(k, unused):
+        r0 = pl.multiple_of(k * tile, tile)
+        rows = pl.ds(r0, tile)
+        ext = pl.ds(r0, tile + 8)
+        spot = places[ext, :]
+        for at in lanes:
+            reach = dcv[ext, at]
+            if at.start < bw:
+                x = xb[ext, at]
+            else:
+                x = jnp.where(high_tile, xb[ext, slice(at.start + LANES, at.stop + LANES)], xb[ext, at])
+            d_c = reach[:tile]
+            d_x = conv_w[0:1, at] * d_c
+            sums[3:4, at] += jnp.sum(d_c * x[8:], axis=0, keepdims=True)
+            for t in range(1, conv_w.shape[0]):
+                term = jnp.where(spot >= t, conv_w[t : t + 1, at] * reach, 0.0)
+                d_x = d_x + pltpu.roll(term, tile + 8 - t, 0)[:tile]
+                lagged = pltpu.roll(x, t, 0)[8:]
+                here = jnp.where(spot[:tile] >= t, d_c * lagged, 0.0)
+                sums[3 + t : 4 + t, at] += jnp.sum(here, axis=0, keepdims=True)
+            sums[7:8, at] += jnp.sum(d_c, axis=0, keepdims=True)
+            drv[rows, at] = d_x.astype(low)
+        return unused
+
+    lax.fori_loop(0, n_tiles, through_conv, 0)
+    out_rec = copies.keep(drv, d_rec_out, local.at[9])
+    copies.land(*parts)
+    total = glo[place.dp].astype(f32)
+    for d in range(n_dp - 1):
+        total = total + gfar[d].astype(f32)
+    gate_out[...] = total.astype(low)
+    copies.finish()
+    out.wait()
+    out_rec.wait()
+
+
+def rec_backward(d_out, w_out, kept, gates_blk, gates_rows, soft, conv_w, places, geo, n_dp):
+    n_col, part, bw, tiles, wide = geo
+    own, width = d_out.shape
+    slots = 2 * n_col
+    group, chans = slots * own, bw + LANES
+    part_rows = 2 * bw // n_dp
+    d_all, d_rec, gate_grads, sums = pl.pallas_call(
+        functools.partial(backward_kernel, geo),
+        out_shape=(
+            jax.ShapeDtypeStruct((slots, own, width), low),
+            jax.ShapeDtypeStruct((group, 2 * chans), low),
+            jax.ShapeDtypeStruct((part_rows, chans), low),
+            jax.ShapeDtypeStruct((8, chans), f32),
+        ),
+        in_specs=[anywhere] * 8 + [in_vmem] * 5,
+        out_specs=(anywhere, anywhere, in_vmem, in_vmem),
+        scratch_shapes=[
+            pltpu.VMEM((slots, own, width), low),
+            pltpu.VMEM(w_out.shape, low),
+            pltpu.VMEM((group, chans), f32),
+            pltpu.VMEM((group, chans), f32),
+            pltpu.VMEM((group + 8, chans), f32),
+            pltpu.VMEM((group, 2 * chans), f32),
+            pltpu.VMEM((group, 2 * bw), low),
+            pltpu.VMEM((group + 8, 2 * bw), f32),
+            pltpu.VMEM((group, chans), f32),
+            pltpu.VMEM((group, chans), f32),
+            pltpu.VMEM((group, 2 * chans), low),
+            pltpu.VMEM((group, 2 * LANES), low),
+            pltpu.VMEM((group + 8, chans), f32),
+            pltpu.VMEM((group, 2 * chans), low),
+            pltpu.VMEM((2, bw, chans), f32),
+            pltpu.VMEM((n_dp, part_rows, chans), low),
+            pltpu.VMEM((n_dp - 1, part_rows, chans), low),
+            pltpu.VMEM((8, chans), f32),
+            pltpu.VMEM((8, chans), f32),
+            pltpu.SemaphoreType.DMA((15 + n_dp,)),
+            pltpu.SemaphoreType.DMA((15 + n_dp,)),
+            pltpu.SemaphoreType.DMA((10,)),
+        ],
+        compiler_params=pltpu.CompilerParams(
+            collective_id=4, has_side_effects=True, vmem_limit_bytes=60 * MIB
+        ),
+        name="rec_backward",
+    )(d_out, w_out, *kept, gates_blk, gates_rows, soft, conv_w, places)
+    return d_all.reshape(group, width), d_rec, gate_grads, sums
 
 
 def outer_kernel(n_dp, first_steps, left1, right1, left2, right2, out_ref):
@@ -1006,6 +1348,36 @@
     @pl.when(j >= first_steps)
     def _():
         multiply(left2, right2)
+
+
+def outer_one_kernel(n_dp, left, right, out_ref):
+    total = dot(left[...], right[...], ((0,), (0,)))
+    rows = total.shape[0] // n_dp
+    for k in range(n_dp):
+        out_ref[k, 0] = total[k * rows : (k + 1) * rows].astype(out_ref.dtype)
+
+
+def outer(left, right, n_dp, n_col, columns, name):
+    length, width = left.shape
+    part = width // n_col
+    count = right.shape[1]
+    return pl.pallas_call(
+        functools.partial(outer_one_kernel, n_dp),
+        grid=(n_col, count // columns),
+        out_shape=jax.ShapeDtypeStruct((n_dp, n_col, part // n_dp, count), low),
+        in_specs=[
+            pl.BlockSpec((length, part), lambda i, j: (0, i)),
+            pl.BlockSpec((length, columns), lambda i, j: (0, j)),
+        ],
+        out_specs=pl.BlockSpec((n_dp, 1, part // n_dp, columns), lambda i, j: (0, i, 0, j)),
+        compiler_params=pltpu.CompilerParams(vmem_limit_bytes=48 * MIB),
+        cost_estimate=pl.CostEstimate(
+            flops=2 * length * width * count,
+            bytes_accessed=2 * (length * width + length * count + width * count),
+            transcendentals=0,
+        ),
+        name=name,
+    )(left, right)
 
 
 def outer_pair(left1, right1, left2, right2, n_dp, n_col, columns, name):
@@ -1039,26 +1411,12 @@
     return lax.dot_general(a, b, (dims, ((), ())), preferred_element_type=f32)
 
 
-def neighbour(x, axis, by):
-    length = lax.axis_size(axis)
-    pairs = [(i, i + by) for i in range(length) if 0 <= i + by < length]
-    return lax.ppermute(x, axis, pairs)
-
-
 def places_of(rows, lengths):
     ends = jnp.cumsum(lengths)
     starts = ends - lengths
     inside = (rows[:, None] >= starts[None, :]) & (rows[:, None] < ends[None, :])
-    return rows - jnp.sum(jnp.where(inside, starts[None, :], 0), axis=1)
-
-
-def lru_coeffs(pre_in, pre_rate, inputs, decay, reset):
-    input_gate = jax.nn.sigmoid(pre_in)
-    rate_gate = jax.nn.sigmoid(pre_rate)
-    log_decay = -8.0 * rate_gate * jax.nn.softplus(decay)
-    decay_factor = jnp.where(reset, 0.0, jnp.exp(log_decay))
-    scaling = jnp.where(reset, 1.0, jnp.sqrt(-jnp.expm1(2.0 * log_decay)))
-    return (decay_factor, inputs * input_gate * scaling)
+    places = rows - jnp.sum(jnp.where(inside, starts[None, :], 0), axis=1)
+    return jnp.where(jnp.any(inside, axis=1), places, 0)
 
 
 def body(
@@ -1098,15 +1456,7 @@
     gains_all = gains_all.transpose(1, 0, 2).reshape(gains.shape[0], width)
     w_x, w_y = w_rec[:, : 2 * bw], w_rec[:, 2 * bw :]
 
-    def own_rows(x):
-        return lax.dynamic_slice_in_dim(x, (row * n_col + col) * own, own, axis=0)
-
-    def home_rows(x):
-        dealt = lax.all_to_all(x.reshape(own, n_col, part).transpose(1, 0, 2), "col", 0, 0)
-        return dealt.reshape(given, part)
-
     tile_at = shared + (col // 2) * LANES
-    tile_owner = col % 2 == 0
 
     def own_channels(x):
         blk = lax.dynamic_slice_in_dim(x, col * bw, bw, axis=-1)
@@ -1126,12 +1476,11 @@
     gates_five = gates[:, n_col]
     gates_tile = lax.dynamic_slice_in_dim(gates_five, (col // 2) * LANES, LANES, axis=2)
     gates_rows = lax.dynamic_slice_in_dim(gates_five, (col // 2) * LANES, LANES, axis=1)
-    channel_ok = (jnp.arange(chans) < bw) | tile_owner
 
     base = dp * group
-    places_ext = places_of(base + jnp.arange(group + taps - 1, dtype=jnp.int32), lengths)
-    places = places_ext[:group]
-    reset = (places == 0)[:, None]
+    places = places_of(base + jnp.arange(group + 8, dtype=jnp.int32), lengths)
+    places = jnp.broadcast_to(places[:, None], (group + 8, LANES))
+    soft = jax.nn.softplus(decay_o)[None, :]
 
     n1, x_rows, y_branch, pre_both, conv_low, state, branch, first, g_all, w_out, w_in, w_down = rec_forward(
         x_all,
@@ -1141,142 +1490,81 @@
             gates_blk,
             gates_tile,
             bias,
-            jax.nn.softplus(decay_o)[None, :],
+            soft,
             conv_w_c,
             conv_b_c[None, :],
         ),
-        jnp.broadcast_to(places[:, None], (group, LANES)),
+        places,
         cotangent,
         rec_out,
         mlp_in,
         mlp_out,
         geo,
     )
-    inputs = own_rows(x_all).astype(f32)
-    upstream = own_rows(g_all).astype(f32)
-    sumsq_one = jnp.sum(inputs * inputs, axis=-1, keepdims=True)
-    scale_one = lax.rsqrt(sumsq_one / width + epsilon)
-    x_ext = x_rows[8 - (taps - 1) :]
-    conv_blk, conv_five = conv_low[:, :bw], conv_low[:, bw:]
-    conv_o = jnp.concatenate(
-        [conv_blk, lax.dynamic_slice_in_dim(conv_five, (col // 2) * LANES, LANES, axis=1)], axis=1
-    ).astype(f32)
-    pre = [pre_both[:, :chans], pre_both[:, chans:]]
-    factor, _ = lru_coeffs(pre[0], pre[1], conv_o, decay_o, reset)
-    state_in = first[7:]
-    out_one = multiply_scatter(branch, w_out, False, 6, "out_one")
-    resid = inputs + out_one
-    sumsq_two = jnp.sum(resid * resid, axis=-1, keepdims=True)
-    scale_two = lax.rsqrt(sumsq_two / width + epsilon)
-    normed_two = (resid * scale_two * gains_all[1]).astype(low)
+    rows_f, rows_b = ((own, width), f32), ((own, width), low)
+    line, squares, home = ((8, width), f32), ((8, LANES), f32), ((given, part), low)
+    resid, normed_two, squares_one = multiply_scatter(
+        branch, w_out, False, 6, "out_one", after_out_one, (x_all, gains_all), (rows_f, rows_b, squares), False
+    )
 
     def spare(at):
         return spare_window(at, tiles, n_col, wide)
 
     n2, hidden, d_glu = glu(normed_two, w_in, w_down, g_all, spare)
-    g_mlp = outer_pair(n2, d_glu, g_all, hidden, n_dp, n_col, 512, "outer_mlp")
-    d_glu, hidden, g_mlp = lax.optimization_barrier((d_glu, hidden, g_mlp))
-    sum_mlp = lax.psum_scatter(g_mlp, "dp", scatter_dimension=0)
-    d_normed_two = multiply_scatter(d_glu, w_in, True, 7, "d_normed_two")
-    gained_two = gains_all[1] * d_normed_two
-    inner_two = jnp.sum(gained_two * resid, axis=-1, keepdims=True)
-    grad_gain_two = jnp.sum(d_normed_two * resid * scale_two, axis=0)
-    d_resid = upstream + scale_two * gained_two - resid * scale_two**3 * (inner_two / width)
-    d_out, d_branch = gather_branch(d_resid.astype(low), w_out)
-
-    d_branch = jnp.where(channel_ok, d_branch, 0.0)
-    _, mix_back = jax.vjp(lambda state_v, gate_v: state_v * gelu(gate_v), state, y_branch)
-    d_state, d_y = mix_back(d_branch)
-    message, until = scan_rows(factor, factor * d_state, True)
-    message_in = neighbour(message[:8], "dp", -1)[:1]
-    message = message + until * message_in
-    grad_state = d_state + jnp.concatenate([message[1:], message_in], axis=0)
-    state_prev = jnp.concatenate([state_in, state[:-1]], axis=0)
-    _, coef_back = jax.vjp(
-        lambda a, b, c, d: lru_coeffs(a, b, c, d, reset), pre[0], pre[1], conv_o, decay_o
+    g_down = outer(g_all, hidden, n_dp, n_col, 512, "outer_down")
+    d_glu, hidden, g_down = lax.optimization_barrier((d_glu, hidden, g_down))
+    sum_down = lax.psum_scatter(g_down, "dp", scatter_dimension=0)
+    g_in = outer(n2, d_glu, n_dp, n_col, 512, "outer_in")
+    d_glu, g_in = lax.optimization_barrier((d_glu, g_in))
+    d_resid, d_out, gain_two = multiply_scatter(
+        d_glu,
+        w_in,
+        True,
+        7,
+        "d_normed_two",
+        after_normed_two,
+        (resid, g_all, gains_all),
+        (rows_f, rows_b, line),
+        False,
     )
-    d_pre_in, d_pre_rate, d_conv, g_decay = coef_back((grad_state * state_prev, grad_state))
-    d_pre = [d_pre_in.astype(low), d_pre_rate.astype(low)]
-    tiles_here = jnp.concatenate([d[:, bw:] for d in d_pre], axis=1)
-    tiles_there = lax.ppermute(tiles_here, "col", [(i, i ^ 2) for i in range(n_col)])
-    low_half = col // 2 == 0
-    d_conv_parts = []
-    d_five = []
-    for j in range(2):
-        here = d_pre[j][:, bw:]
-        there = tiles_there[:, j * LANES : (j + 1) * LANES]
-        d_five.append(
-            jnp.where(
-                low_half,
-                jnp.concatenate([here, there], axis=1),
-                jnp.concatenate([there, here], axis=1),
-            )
-        )
-        d_conv_parts.append(
-            jnp.concatenate(
-                [
-                    dot(d_pre[j][:, :bw], gates_blk[j], ((1,), (1,))),
-                    dot(d_five[j], gates_rows[j], ((1,), (1,))),
-                ],
-                axis=1,
-            )
-        )
-    d_conv = d_conv + d_conv_parts[0] + d_conv_parts[1]
-    g_gates = jnp.stack(
-        [
-            jnp.concatenate(
-                [
-                    dot(conv_blk, d_pre[j][:, :bw], ((0,), (0,))),
-                    dot(conv_five, d_pre[j][:, bw:], ((0,), (0,))),
-                ],
-                axis=1,
-            )
-            for j in range(2)
-        ]
+    g_in, sum_down, d_out = lax.optimization_barrier((g_in, sum_down, d_out))
+    sum_in = lax.psum_scatter(g_in, "dp", scatter_dimension=0)
+
+    d_out_all, d_rec, gate_sums, small = rec_backward(
+        d_out,
+        w_out,
+        (y_branch, state, first, pre_both, conv_low, x_rows),
+        gates_blk,
+        gates_rows,
+        soft,
+        conv_w_o,
+        places,
+        geo,
+        n_dp,
     )
-    g_bias = [jnp.sum(d.astype(f32), axis=0) for d in d_pre]
-    later = neighbour(d_conv[:8], "dp", -1)[: taps - 1]
-    d_ext = jnp.concatenate([d_conv, later], axis=0)
-    x_own = jnp.concatenate(
-        [x_ext[:, :bw], lax.dynamic_slice_in_dim(x_ext, bw + (col // 2) * LANES, LANES, axis=1)],
-        axis=1,
-    )
-    d_x = jnp.zeros_like(d_conv)
-    g_taps = []
-    for t in range(taps):
-        ahead = d_ext[t : t + group]
-        valid = (places_ext[t : t + group] >= t)[:, None]
-        d_x = d_x + jnp.where(valid, conv_w_o[t][None, :] * ahead, 0.0)
-        lagged = x_own[taps - 1 - t : taps - 1 - t + group]
-        g_taps.append(jnp.sum(jnp.where((places >= t)[:, None], d_conv * lagged, 0.0), axis=0))
-    g_conv_b = jnp.sum(d_conv, axis=0)
-    d_x_low = jnp.where(channel_ok, d_x, 0.0).astype(low)
-    d_y_low = jnp.where(channel_ok, d_y, 0.0).astype(low)
-    d_rec = jnp.concatenate([d_x_low, d_y_low], axis=1)
+    small = small.at[2].multiply(jax.nn.sigmoid(decay_o))
     w_x_own = jnp.concatenate(
         [w_x[:, :bw], lax.dynamic_slice_in_dim(w_x, bw + (col // 2) * LANES, LANES, axis=1)], axis=1
     )
     w_back = jnp.concatenate([w_x_own, w_y], axis=1)
-    g_rec = outer_pair(n1, d_rec, d_out, branch, n_dp, n_col, chans, "outer_rec")
+    g_rec = outer_pair(n1, d_rec, d_out_all, branch, n_dp, n_col, chans, "outer_rec")
     g_rec, d_rec = lax.optimization_barrier((g_rec, d_rec))
-    d_normed_one = multiply_scatter(d_rec, w_back, True, 9, "d_normed_one")
-    g_rec, g_gates, sum_mlp, d_normed_one, hidden = lax.optimization_barrier(
-        (g_rec, g_gates, sum_mlp, d_normed_one, hidden)
+    grad_input, gain_one, squares_x = multiply_scatter(
+        d_rec,
+        w_back,
+        True,
+        9,
+        "d_normed_one",
+        after_normed_one,
+        (x_all, d_resid, gains_all),
+        (home, line, squares),
+        True,
     )
-    gate_sums = lax.psum_scatter(
-        g_gates.astype(low).reshape(n_dp, 2 * bw // n_dp, chans), "dp", scatter_dimension=0
+    g_rec, sum_in, grad_input, hidden = lax.optimization_barrier((g_rec, sum_in, grad_input, hidden))
+    sum_rec = lax.psum_scatter(g_rec, "dp", scatter_dimension=0)
+    result, squares_two = multiply_scatter(
+        hidden, w_down, False, 8, "out_two", after_out_two, (resid,), (home, squares), True
     )
-    g_rec, gate_sums = lax.optimization_barrier((g_rec, gate_sums))
-    sum_rec = lax.psum_scatter(g_rec, "dp", scatter_dimension=0)
-    out_two = multiply_scatter(hidden, w_down, False, 8, "out_two")
-    result = (resid + out_two).astype(low)
-    gained_one = gains_all[0] * d_normed_one
-    inner_one = jnp.sum(gained_one * inputs, axis=-1, keepdims=True)
-    grad_gain_one = jnp.sum(d_normed_one * inputs * scale_one, axis=0)
-    d_input = d_resid + scale_one * gained_one - inputs * scale_one**3 * (inner_one / width)
-
-    result = home_rows(result)
-    grad_input = home_rows(d_input.astype(low))
 
     def windows(got, first):
         return [
@@ -1289,26 +1577,24 @@
             got[c][..., first + bw : first + chans] for c in range(0, n_col, 2)
         ]
 
-    dealt = lax.all_to_all(sum_mlp, "col", 0, 0)
+    square_sums = jnp.stack([squares_x[0, 0], squares_one[0, 0], squares_one[1, 0], squares_two[0, 0]])
+    lines = small.shape[0]
+    gain_sums = jnp.concatenate([gain_one[:1], gain_two[:1]]).reshape(lines, 2 * width // lines)
+    stat_block = jnp.pad(square_sums[None, :], ((0, lines - 1), (0, LANES - 4)))
+    mixed = jnp.concatenate([small, gain_sums, stat_block], axis=1)
+    sums, chan_sums, gate_parts, into, down = sum_everywhere(
+        mixed, chans, gate_sums, sum_in, sum_down, n_dp, n_col
+    )
+    sum_rec, into = lax.optimization_barrier((sum_rec, into))
+    recs = deal_back(sum_rec, 10, "deal_rec")
     grad_mlp_in = jnp.stack(
-        [jnp.concatenate(windows(dealt[..., j * span : (j + 1) * span], 0), axis=-1) for j in range(2)]
+        [jnp.concatenate(windows(into[..., j * span : (j + 1) * span], 0), axis=-1) for j in range(2)]
     ).astype(f32)
-    grad_mlp_out = jnp.concatenate(windows(dealt[..., 2 * span :], 0), axis=-1).astype(f32).T
-    recs = lax.all_to_all(sum_rec, "col", 0, 0)
+    grad_mlp_out = jnp.concatenate(windows(down, 0), axis=-1).astype(f32).T
     grad_rec_in = jnp.stack(
         [jnp.concatenate(channels_of(recs, j * chans), axis=-1) for j in range(2)]
     ).astype(f32)
     grad_rec_out = jnp.concatenate(channels_of(recs, 2 * chans), axis=-1).astype(f32).T
-
-    small = jnp.where(channel_ok, jnp.stack(g_bias + [g_decay] + g_taps + [g_conv_b]), 0.0)
-    square_sums = jnp.stack(
-        [jnp.sum(sumsq_one), jnp.sum(out_one * out_one), jnp.sum(sumsq_two), jnp.sum(out_two * out_two)]
-    )
-    lines = small.shape[0]
-    gain_sums = jnp.stack([grad_gain_one, grad_gain_two]).reshape(lines, 2 * width // lines)
-    stat_block = jnp.pad(square_sums[None, :], ((0, lines - 1), (0, LANES - 4)))
-    mixed = jnp.concatenate([small, gain_sums, stat_block], axis=1)
-    sums, chan_sums, gate_parts = sum_everywhere(mixed, chans, gate_sums, n_dp, n_col)
     mine = jnp.concatenate(channels_of(chan_sums, 0), axis=-1)
     gain_rows = sums[:, : 2 * width // lines].reshape(2, width)
     grad_gains = lax.dynamic_slice_in_dim(gain_rows, col * part, part, axis=1)

time: 922 us -> 856 us (0.928)
  Pallas kernels: 675 us -> 772 us
  waiting for transfers between devices: 66.4 us -> 4.81 us
  other arithmetic: 67.6 us -> 18 us
  local copies, waits for them, and re-layouts: 59.3 us -> 38.1 us
  starting transfers between devices: 21 us -> 0.12 us
    pallas_call x6 -> x8, Pallas kernels: 244 us -> 382 us  [the longest x4 231 us: multiply_scatter(): pl.pallas_call(functools.partial(scatter_kernel, (n_parts, across, own, w...]
    pallas_call x2 -> x1, Pallas kernels: 63.4 us -> 21.6 us  [outer_pair(): pl.pallas_call(functools.partial(outer_kernel, n_dp, steps1), grid=(n_col...]
    all_to_all x4 -> x0, waiting for transfers between devices: 26.7 us -> none  [the longest x2 16.5 us: home_rows(): lax.all_to_all(x.reshape(own, n_col, part).transpose(1, 0, 2), 'col', 0, 0)]
    reduce_sum x8 -> x1, other arithmetic: 26.7 us -> 0.1 us  [places_of(): places = rows - jnp.sum(jnp.where(inside, starts[None, :], 0), axis=1)]
    ppermute x3 -> x0, waiting for transfers between devices: 19.1 us -> none  [the longest x1 14 us: body(): lax.ppermute(tiles_here, 'col', [(i, i ^ 2) for i in range(n_col)])]
    all_to_all x4 -> x0, starting transfers between devices: 15.9 us -> none  [the longest x2 7.48 us: home_rows(): lax.all_to_all(x.reshape(own, n_col, part).transpose(1, 0, 2), 'col', 0, 0)]
    reduce_scatter x2, waiting for transfers between devices: 20.6 us -> 4.76 us  [the longest x1 4.74 us: body(): sum_down = lax.psum_scatter(g_down, 'dp', scatter_dimension=0)]
    pallas_call x1, Pallas kernels: 62.3 us -> 72.9 us  [sum_everywhere(): pl.pallas_call(functools.partial(sums_kernel, far, split), out_shape=(jax...]
  transfers between devices with their start and end apart: 10 -> 3, of which waited for: 6 -> 1; matrix products, arithmetic and copies ran while one was open for 11% -> 4% of each run, Pallas kernels for 31% -> 47%
where the time goes in v3:
time: 856 us; the launch traced here: 848 us
  Pallas kernels  772 us (90%)
  local copies, waits for them, and re-layouts  38.1 us (4%)
  other arithmetic  18 us (2%)
  between operations  14.4 us (2%)
    pallas_call x4, Pallas kernels, multiply_scatter(): pl.pallas_call(functools.partial(scatter_kernel, (n_parts, across, own, w...  231 us
    pallas_call x1, Pallas kernels, rec_forward(): pl.pallas_call(functools.partial(forward_kernel, geo), out_shape=tuple((o...  171 us
    pallas_call x1, Pallas kernels, rec_backward(): pl.pallas_call(functools.partial(backward_kernel, geo), out_shape=(jax.Sh...  92.9 us
    pallas_call x1, Pallas kernels, sum_everywhere(): pl.pallas_call(functools.partial(sums_kernel, far, split), out_shape=(jax...  72.9 us
    pallas_call x1, Pallas kernels, open_gather(): pl.pallas_call(functools.partial(open_kernel, geo), out_shape=(jax.ShapeD...  70.4 us
    pallas_call x1, Pallas kernels, glu(): pl.pallas_call(functools.partial(glu_kernel, spare), out_shape=(jax.Shape...  54.4 us
    pallas_call x2, Pallas kernels, outer(): pl.pallas_call(functools.partial(outer_one_kernel, n_dp), grid=(n_col, co...  42 us
    pallas_call x1, Pallas kernels, outer_pair(): pl.pallas_call(functools.partial(outer_kernel, n_dp, steps1), grid=(n_col...  21.6 us
  transfers between devices with their start and end apart: 3, of which 1 were waited for; matrix products, arithmetic and copies ran while one was open for 4% of the time, Pallas kernels for 47%

profile of v3, /device:TPU:0, one launch (start us, length us, event | category | flops | bytes accessed | tf_op | source)
XLA Modules:
  0.0 847.8 jit_solution(934065589416641271)
XLA Ops:
  12.1 70.4 %open_gather.1 = (bf16[1536,2560]{1,0:T(8,128)(2,1)}, bf16[2560,896]{1,0:T(8,128)(2,1)}, f32[4,2,640]{2,1,0:T(2,128)}) custom-call(bf16[768,640]{1,0:T(8,128)(2,1)} %tokens.1, bf16[2,640,1280]{2,1,0:T(8,128)(2,1)} %rec_in.1, f32[2,640]{1,0:T(2,128)} %gains.1), custom_call_target="tpu_custom_call" | custom-call | tf_op jit(solution)/shard_map/open_gather/pallas_call | solution.py:302
  86.1 1.8 fusion.6
  89.7 171.1 %rec_forward.1 = (bf16[1536,2560]{1,0:T(8,128)(2,1)}, f32[1544,512]{1,0:T(8,128)}, f32[1536,384]{1,0:T(8,128)}, f32[1536,768]{1,0:T(8,128)}, bf16[1536,512]{1,0:...) custom-call(bf16[1536,2560]{1,0:T(8,128)(2,1)} %get-tuple-element.79, ...), custom_call_target="tpu_custom_call" | custom-call | tf_op jit(solution)/shard_map/rec_forward/pallas_call | solution.py:1008
  260.9 52.0 %out_one.1 = (f32[192,2560]{1,0:T(8,128)}, bf16[192,2560]{1,0:T(8,128)(2,1)}, f32[8,128]{1,0:T(8,128)}) custom-call(bf16[1536,384]{1,0:T(8,128)(2,1)} %get-tuple-element.83.act.right2, bf16[384,2560]{1,0:T(8,128)(2,1)} %get-tuple-element.84.w.w_out, bf16[1536,2560]{1,0:T(8,128)(2,1)} %get-tuple-element.79.x_all.refs_0_, f32[2,2560]{1,0:T(2,128)} %bitcast.125), custom_call_target="tpu_custom_call" | custom-call | flops 3019898880 | bytes 41943040 | tf_op jit(solution)/shard_map/out_one/pallas_call | solution.py:564
  312.9 54.4 %glu.1 = (bf16[8,192,2560]{2,1,0:T(8,128)(2,1)}, bf16[1536,1024]{1,0:T(8,128)(2,1)}, bf16[1536,2048]{1,0:T(8,128)(2,1)}) custom-call(bf16[192,2560]{1,0:T(8,128)(2,1)} %get-tuple-element.85.n2, bf16[2,2560,1024]{2,1,0:T(8,128)(2,1)} %get-tuple-element.86.w_in.w, bf16[1024,2560]{1,0:T(8,128)(2,1)} %get-tuple-element.87.w_down.w, ...), custom_call_target="tpu_custom_call" | custom-call | flops 24159191040 | bytes 62914560 | tf_op jit(solution)/shard_map/glu/pallas_call | solution.py:418
  367.3 1.9 copy-done.4
  369.2 13.9 %outer_down.1 = bf16[4,4,160,1024]{3,2,1,0:T(8,128)(2,1)} custom-call(bf16[1536,2560]{1,0:T(8,128)(2,1)} %get-tuple-element.88.g_all.left.refs_1_, bf16[1536,1024]{1,0:T(8,128)(2,1)S(1)} %copy-done.4), custom_call_target="tpu_custom_call" | custom-call | flops 8053063680 | bytes 16252928 | tf_op jit(solution)/shard_map/outer_down/pallas_call | solution.py:1364
  383.2 28.1 %outer_in.1 = bf16[4,4,160,2048]{3,2,1,0:T(8,128)(2,1)} custom-call(bf16[1536,2560]{1,0:T(8,128)(2,1)} %bitcast.130, bf16[1536,2048]{1,0:T(8,128)(2,1)} %get-tuple-element.95.right.act), custom_call_target="tpu_custom_call" | custom-call | flops 16106127360 | bytes 24641536 | tf_op jit(solution)/shard_map/outer_in/pallas_call | solution.py:1364
  411.3 59.1 %d_normed_two.1 = (f32[192,2560]{1,0:T(8,128)}, bf16[192,2560]{1,0:T(8,128)(2,1)}, f32[8,2560]{1,0:T(8,128)}) custom-call(bf16[1536,2048]{1,0:T(8,128)(2,1)} %get-tuple-element.95.right.act, bf16[2,2560,1024]{2,1,0:T(8,128)(2,1)} %get-tuple-element.86.w_in.w, f32[192,2560]{1,0:T(8,128)} %get-tuple-element.96.refs_0_, ...), custom_call_target="tpu_custom_call" | custom-call | flops 16106127360 | bytes 41943040 | tf_op jit(solution)/shard_map/d_normed_two/pallas_call | solution.py:564
  470.5 4.7 reduce-scatter.4.cloned.1.call-done
  476.7 1.7 slice.282
  478.4 3.4 slice.281
  485.1 2.5 pad_maximum_fusion.w
  487.6 92.9 %rec_backward.1 = (bf16[8,192,2560]{2,1,0:T(8,128)(2,1)}, bf16[1536,768]{1,0:T(8,128)(2,1)}, bf16[128,384]{1,0:T(8,128)(2,1)}, f32[8,384]{1,0:T(8,128)}) custom-call(bf16[192,2560]{1,0:T(8,128)(2,1)} %get-tuple-element.98.d_out, bf16[384,2560]{1,0:T(8,128)(2,1)} %get-tuple-element.84.w.w_out, f32[1536,384]{1,0:T(8,128)} %get-tuple-element.99.y_in, ...), custom_call_target="tpu_custom_call" | custom-call | tf_op jit(solution)/shard_map/rec_backward/pallas_call | solution.py:1293
  580.6 1.7 copy-done.2
  582.2 21.6 %outer_rec.1 = bf16[4,4,160,1152]{3,2,1,0:T(8,128)(2,1)} custom-call(bf16[1536,2560]{1,0:T(8,128)(2,1)} %get-tuple-element.82.left1, bf16[1536,768]{1,0:T(8,128)(2,1)S(1)} %copy-done.2, bf16[1536,2560]{1,0:T(8,128)(2,1)} %bitcast.129, bf16[1536,384]{1,0:T(8,128)(2,1)S(1)} %copy-done.3), custom_call_target="tpu_custom_call" | custom-call | flops 9059696640 | bytes 25165824 | tf_op jit(solution)/shard_map/outer_rec/pallas_call | solution.py:1389
  603.8 59.8 %d_normed_one.1 = (bf16[768,640]{1,0:T(8,128)(2,1)}, f32[8,2560]{1,0:T(8,128)}, f32[8,128]{1,0:T(8,128)}) custom-call(bf16[1536,768]{1,0:T(8,128)(2,1)} %get-tuple-element.109.right1.act, bf16[2560,768]{1,0:T(8,128)(2,1)} %pad_maximum_fusion.w, bf16[1536,2560]{1,0:T(8,128)(2,1)} %get-tuple-element.79.x_all.refs_0_, f32[192,2560]{1,0:T(8,128)} %get-tuple-element.110.refs_1_, ...), custom_call_target="tpu_custom_call" | custom-call | flops 6039797760 | bytes 41943040 | tf_op jit(solution)/shard_map/d_normed_one/pallas_call | solution.py:564
  668.1 60.0 %out_two.1 = (bf16[768,640]{1,0:T(8,128)(2,1)}, f32[8,128]{1,0:T(8,128)}) custom-call(bf16[1536,1024]{1,0:T(8,128)(2,1)} %get-tuple-element.113.right.act, bf16[1024,2560]{1,0:T(8,128)(2,1)} %get-tuple-element.87.w_down.w, f32[192,2560]{1,0:T(8,128)} %get-tuple-element.96.refs_0_), custom_call_target="tpu_custom_call" | custom-call | flops 8053063680 | bytes 41943040 | tf_op jit(solution)/shard_map/out_two/pallas_call | solution.py:564
  729.3 2.7 maximum_bitcast_fusion.3
  732.6 72.9 %small_sums.1 = (f32[8,768]{1,0:T(8,128)}, f32[4,8,384]{2,1,0:T(8,128)}, bf16[4,4,128,384]{3,2,1,0:T(8,128)(2,1)}, bf16[4,160,2048]{2,1,0:T(8,128)(2,1)}, bf16[4,160,1024]{2,1,0:T(8,128)(2,1)}) custom-call(f32[8,1152]{1,0:T(8,128)} %select_maximum_fusion.mixed, bf16[128,384]{1,0:T(8,128)(2,1)} %get-tuple-element.123.gate_part, ...), custom_call_target="tpu_custom_call" | custom-call | tf_op jit(solution)/shard_map/small_sums/pallas_call | solution.py:767
  813.0 1.6 convert_bitcast_fusion
  814.6 16.0 %deal_rec.1 = bf16[4,160,1152]{2,1,0:T(8,128)(2,1)} custom-call(bf16[4,160,1152]{2,1,0:T(8,128)(2,1)} %bitcast.116), custom_call_target="tpu_custom_call" | custom-call | tf_op jit(solution)/shard_map/deal_rec/pallas_call | solution.py:669
  830.6 1.4 slice_bitcast_fusion.4
  836.0 2.6 maximum_convert_fusion
  (108 shorter events, 35.0 us)
Async XLA Ops:
  7.2 0.9 copy-start
  7.2 468.0 %reduce-scatter.4.cloned.1.call-start = ((), (), s32[]{:S(2)}) async-start(), calls=%async_computation.3 | async-start | bytes 6553600 | tf_op jit(solution)/shard_map/reduce_scatter | solution.py:1516
  8.0 78.1 %copy-start.11 = (f32[1,128]{1,0:T(1,128)}, f32[1,128]{1,0:T(1,128)S(1)}, u32[]{:S(2)}) copy-start(f32[1,128]{1,0:T(1,128)S(1)} %dynamic-slice_bitcast_fusion.3) | copy-start | bytes 1540
  367.3 1.9 copy-start.4
  383.2 280.5 %reduce-scatter.6.cloned.1.call-start = ((), (), s32[]{:S(2)}) async-start(), calls=%async_computation.4 | async-start | bytes 13107200 | tf_op jit(solution)/shard_map/reduce_scatter | solution.py:1531
  475.2 339.3 %reduce-scatter.8.cloned.1.call-start = ((), (), s32[]{:S(2)}) async-start(), calls=%async_computation.5 | async-start | bytes 7372800 | tf_op jit(solution)/shard_map/reduce_scatter | solution.py:1564
  487.6 92.9 %copy-start.3 = (bf16[1536,384]{1,0:T(8,128)(2,1)S(1)}, bf16[1536,384]{1,0:T(8,128)(2,1)}, u32[]{:S(2)}) copy-start(bf16[1536,384]{1,0:T(8,128)(2,1)} %get-tuple-element.83.act.right2) | copy-start | bytes 3538948
  580.6 1.7 copy-start.2
  663.7 4.3 copy-start.10
  663.7 4.3 copy-start.12
  805.5 5.6 copy-start.6
  811.6 19.0 %copy-start.9 = (f32[2,5,256,256]{3,2,1,0:T(8,128)}, f32[2,5,256,256]{3,2,1,0:T(8,128)S(1)}, u32[]{:S(2)}) copy-start(f32[2,5,256,256]{3,2,1,0:T(8,128)S(1)} %fusion.4) | copy-start | bytes 7864324
  832.0 2.0 copy-start.5
  836.0 2.6 copy-start.8
  836.0 5.1 copy-start.1
  838.6 1.6 copy-start.7
Sparse Core Ops, SparseCore 0:
  383.3 91.8 reduce-scatter.3
  477.6 185.3 reduce-scatter.5
  665.3 116.1 reduce-scatter.7

commit v4 on v3

--- a/solution.py
+++ b/solution.py
@@ -45,6 +45,8 @@
             return {"dp": lax.rem(self.dp + (1 if name == "next" else n_dp - 1), n_dp)}
         if name[0] == "d":
             return {"dp": jnp.bitwise_xor(self.dp, int(name[1:]))}
+        if name[0] == "c":
+            return {"row": 1 - self.row, "col": self.chip({"x": 1, "y": 2, "xy": 3}[name[1:]])}
         return {"col": self.chip({"x": 1, "y": 2, "xy": 3}[name])}
 
     def meet(self, names):
@@ -98,14 +100,14 @@
         self.leave(*range(len(self.made)))
 
 
-def share(rows):
-    far = rows * 2 // 5 // ROWS * ROWS
+def share(rows, far_part):
+    far = rows * far_part // 20 // ROWS * ROWS
     return rows - far, far
 
 
 class Dealer:
-    def __init__(self, copies):
-        self.copies = copies
+    def __init__(self, copies, far_part):
+        self.copies, self.far_part = copies, far_part
         self.waiting = []
 
     def deal(self, piece):
@@ -114,7 +116,7 @@
         batch = []
         for name, k in (("x", 1), ("y", 2), ("xy", 3)):
             src, dst, rows = piece(place.chip(k), place.col)
-            near, far = share(rows)
+            near, far = share(rows, self.far_part)
             start = pl.multiple_of(odd * far, ROWS)
             at = pl.ds(start, near)
             number = self.copies.start(src(at), dst(at), name)
@@ -127,7 +129,7 @@
         for k, number, piece in self.waiting.pop(0):
             self.copies.land(number)
             _, dst, rows = piece(place.col, place.chip(k))
-            near, far = share(rows)
+            near, far = share(rows, self.far_part)
             at = pl.ds(pl.multiple_of(odd * near, ROWS), far)
             self.copies.start(dst(at), dst(at), "z")
 
@@ -208,11 +210,37 @@
     return found
 
 
-def keep_own(copies, pieces, sems, first):
-    col = copies.place.col
-    for i, piece in enumerate(pieces):
-        src, dst, rows = piece(col, col)
-        copies.keep(src(pl.ds(0, rows)), dst(pl.ds(0, rows)), sems.at[first + i])
+def own_pieces(place, pieces):
+    pairs = []
+    for piece in pieces:
+        src, dst, rows = piece(place.col, place.col)
+        pairs.append((src(pl.ds(0, rows)), dst(pl.ds(0, rows))))
+    return pairs
+
+
+class Stay:
+    def __init__(self, pairs, bufs, sems):
+        self.pairs, self.bufs, self.sems = pairs, bufs, sems
+        self.loads = [
+            pltpu.make_async_copy(src, buf, sems.at[i])
+            for i, ((src, _), buf) in enumerate(zip(pairs, bufs))
+        ]
+        for load in self.loads:
+            load.start()
+
+    def turn(self):
+        for load in self.loads:
+            load.wait()
+        self.stores = [
+            pltpu.make_async_copy(buf, dst, self.sems.at[i])
+            for i, ((_, dst), buf) in enumerate(zip(self.pairs, self.bufs))
+        ]
+        for store in self.stores:
+            store.start()
+
+    def finish(self):
+        for store in self.stores:
+            store.wait()
 
 
 class Gather:
@@ -226,65 +254,76 @@
             for name in ("x", "y")
         ]
         self.own = copies.start(mine(None), at(row, col, None), "core")
+        self.rounds = []
+
+    def pass_half(self, half):
+        copies, place = self.copies, self.copies.place
+        views = [self.at(place.row, place.chip(k), half) for k in (1, 2)]
+        x, y = self.first[2 * half], self.first[2 * half + 1]
+        if half == 0:
+            copies.land(x)
+            round_ = copies.start(views[0], views[0], "y")
+            core_x = copies.start(views[0], views[0], "core")
+            copies.land(y)
+            core_y = copies.start(views[1], views[1], "core")
+        else:
+            copies.land(y)
+            round_ = copies.start(views[1], views[1], "x")
+            core_y = copies.start(views[1], views[1], "core")
+            copies.land(x)
+            core_x = copies.start(views[0], views[0], "core")
+        self.rounds.append(round_)
+        return core_x, core_y
 
     def pass_on(self):
-        copies, place = self.copies, self.copies.place
-        row = place.row
-        x, y = place.chip(1), place.chip(2)
-        x0, y0, x1, y1 = self.first
-        copies.land(x0)
-        self.round0 = copies.start(self.at(row, x, 0), self.at(row, x, 0), "y")
-        copies.land(y0, y1)
-        self.round1 = copies.start(self.at(row, y, 1), self.at(row, y, 1), "x")
-        self.core_y = copies.start(self.at(row, y, None), self.at(row, y, None), "core")
-        copies.land(x1)
-        self.core_x = copies.start(self.at(row, x, None), self.at(row, x, None), "core")
+        return self.pass_half(0) + self.pass_half(1)
 
     def last(self):
         copies, place = self.copies, self.copies.place
         corner = self.at(place.row, place.chip(3), None)
-        copies.land(self.round0, self.round1)
-        self.core_xy = copies.start(corner, corner, "core")
-
-
-def block_gather(copies, source, target, sem):
+        copies.land(*self.rounds)
+        return copies.start(corner, corner, "core")
+
+
+def block_view(source, target, row, col, half):
     rows, part = source.shape
     cut = rows // 2
-
-    def at(row, col, half):
-        first = row * rows + (0 if half is None else half * cut)
-        size = rows if half is None else cut
-        return target.at[
-            pl.ds(pl.multiple_of(first, ROWS), size), pl.ds(pl.multiple_of(col * part, LANES), part)
-        ]
+    first = row * rows + (0 if half is None else half * cut)
+    size = rows if half is None else cut
+    return target.at[
+        pl.ds(pl.multiple_of(first, ROWS), size), pl.ds(pl.multiple_of(col * part, LANES), part)
+    ]
+
+
+def block_gather(copies, source, target):
+    cut = source.shape[0] // 2
 
     def mine(half):
         return source if half is None else source.at[pl.ds(half * cut, cut), :]
 
-    place = copies.place
-    copies.keep(source, at(place.row, place.col, None), sem)
-    return Gather(copies, mine, at)
+    return Gather(copies, mine, functools.partial(block_view, source, target))
 
 
 AROUND = ("x", "y", "xy", "core", "z")
 
 
-def open_kernel(geo, tokens, rec_in, gains, x_all, w_rec, gains_all, send, recv, local):
+def open_kernel(geo, tokens, rec_in, gains, x_all, w_rec, gains_all, send, recv, local, *bufs):
     place = Place()
     place.meet(AROUND)
     copies = Copies(place, send, recv)
     pieces = weight_pieces(geo, (rec_in, None, None, None), (w_rec, None, None, None))["rec_in"]
-    dealer = Dealer(copies)
+    dealer = Dealer(copies, 10)
     dealer.deal(pieces[0])
     dealer.deal(pieces[1])
-    gather = block_gather(copies, tokens, x_all, local.at[0])
+    gather = block_gather(copies, tokens, x_all)
+    own_block = (tokens, block_view(tokens, x_all, place.row, place.col, None))
     dealer.deal(pieces[2])
     dealer.deal(pieces[3])
     mine = gains_all.at[place.col]
     for name in ("x", "y", "xy"):
         copies.start(gains, mine, name)
-    copies.keep(gains, mine, local.at[5])
-    keep_own(copies, pieces, local, 1)
+    stay = Stay([own_block] + own_pieces(place, pieces) + [(gains, mine)], bufs, local)
+    stay.turn()
     dealer.forward()
     dealer.forward()
     gather.pass_on()
@@ -292,8 +331,7 @@
     dealer.forward()
     gather.last()
     copies.finish()
-    for copy in copies.local:
-        copy.wait()
+    stay.finish()
 
 
 def open_gather(tokens, rec_in, gains, geo):
@@ -309,9 +347,15 @@
         in_specs=[anywhere] * 3,
         out_specs=(anywhere,) * 3,
         scratch_shapes=[
-            pltpu.SemaphoreType.DMA((37,)),
-            pltpu.SemaphoreType.DMA((37,)),
+            pltpu.SemaphoreType.DMA((39,)),
+            pltpu.SemaphoreType.DMA((39,)),
             pltpu.SemaphoreType.DMA((6,)),
+            pltpu.VMEM(tokens.shape, low),
+            pltpu.VMEM((part, bw), low),
+            pltpu.VMEM((part, bw), low),
+            pltpu.VMEM((part, bw), low),
+            pltpu.VMEM((part, LANES), low),
+            pltpu.VMEM(gains.shape, f32),
         ],
         compiler_params=pltpu.CompilerParams(collective_id=1, has_side_effects=True),
         name="open_gather",
@@ -363,10 +407,11 @@
         load.wait()
     hide = spare(place.col)
 
-    def work(chip):
-        slots = (chip, n_col + chip)
-        rows = [pl.ds(pl.multiple_of(s * own, ROWS), own) for s in slots]
-        n2_here = jnp.concatenate([buf[s] for s in slots], axis=0)
+    n_steps = span // step
+
+    def work(slots, first, size, lo, hi):
+        rows = [pl.ds(pl.multiple_of(s * own + first, ROWS), size) for s in slots]
+        n2_here = jnp.concatenate([buf[s, first : first + size, :] for s in slots], axis=0)
         g_here = jnp.concatenate([g[r, :] for r in rows], axis=0)
 
         def columns(i, carry):
@@ -384,25 +429,33 @@
             dg = (d_hid * up * slope).astype(low)
             du = (d_hid * value).astype(low)
             for n, r in enumerate(rows):
-                part = slice(n * own, (n + 1) * own)
+                part = slice(n * size, (n + 1) * size)
                 hid[r, at] = h[part]
                 dgl[r, at] = dg[part]
                 dgl[r, up_at] = du[part]
             return carry
 
-        lax.fori_loop(0, span // step, columns, 0)
-
+        lax.fori_loop(lo, hi, columns, 0)
+
+    def both_cores(*chips):
+        return [s for chip in chips for s in (chip, n_col + chip)]
+
+    half = own // 2
+    near = both_cores(place.chip(1), place.chip(2))
     copies.land(gather.own)
-    work(place.col)
-    gather.pass_on()
-    copies.land(gather.core_y)
-    work(place.chip(2))
-    gather.last()
-    copies.land(gather.core_x)
-    work(place.chip(1))
-    copies.land(gather.core_xy)
+    work(both_cores(place.col), 0, own, 0, n_steps)
+    core0 = gather.pass_half(0)
+    copies.land(*core0)
+    work(near, 0, half, 0, n_steps // 2)
+    core1 = gather.pass_half(1)
+    work(near, 0, half, n_steps // 2, n_steps)
+    copies.land(*core1)
+    work(near, half, half, 0, n_steps // 2)
+    corner = gather.last()
+    work(near, half, half, n_steps // 2, n_steps)
+    copies.land(corner)
     out_n2 = copies.keep(buf, n2_all, local.at[4])
-    work(place.chip(3))
+    work(both_cores(place.chip(3)), 0, own, 0, n_steps)
     out_h = copies.keep(hid, hidden, local.at[5])
     out_d = copies.keep(dgl, d_glu, local.at[6])
     copies.finish()
@@ -431,8 +484,8 @@
             pltpu.VMEM((group, width), low),
             pltpu.VMEM((group, span), low),
             pltpu.VMEM((group, 2 * span), low),
-            pltpu.SemaphoreType.DMA((10,)),
-            pltpu.SemaphoreType.DMA((10,)),
+            pltpu.SemaphoreType.DMA((12,)),
+            pltpu.SemaphoreType.DMA((12,)),
             pltpu.SemaphoreType.DMA((7,)),
         ],
         compiler_params=pltpu.CompilerParams(
@@ -655,14 +708,15 @@
         copies.start(source.at[copies.place.chip(j)], target.at[col], name)
 
 
-def deal_kernel(source, target, send, recv, local):
+def deal_kernel(source, target, send, recv, local, buf):
     place = Place()
     place.meet(("x", "y", "xy"))
     copies = Copies(place, send, recv)
     start_deal(copies, source, target)
-    stay = copies.keep(source.at[place.col], target.at[place.col], local)
+    stay = Stay([(source.at[place.col], target.at[place.col])], [buf], local)
+    stay.turn()
     copies.finish()
-    stay.wait()
+    stay.finish()
 
 
 def deal_back(x, number, name):
@@ -674,55 +728,66 @@
         scratch_shapes=[
             pltpu.SemaphoreType.DMA((3,)),
             pltpu.SemaphoreType.DMA((3,)),
-            pltpu.SemaphoreType.DMA,
+            pltpu.SemaphoreType.DMA((1,)),
+            pltpu.VMEM(x.shape[1:], x.dtype),
         ],
-        compiler_params=pltpu.CompilerParams(collective_id=number, has_side_effects=True),
+        compiler_params=pltpu.CompilerParams(
+            collective_id=number, has_side_effects=True, vmem_limit_bytes=16 * MIB
+        ),
         name=name,
     )(x)
 
 
+PLANE = ("x", "y", "xy", "core", "cx", "cy", "cxy")
+
+
 def sums_kernel(
-    far,
+    n_dp,
     split,
     mixed,
     gate_part,
-    grads_a,
-    grads_b,
+    grads,
     sums_out,
     chans_out,
     gates_out,
-    out_a,
-    out_b,
+    grads_out,
     got,
-    acc,
+    total,
     ch,
+    shared,
     send,
     recv,
     local,
+    *bufs,
 ):
     place = Place()
-    steps = [f"d{d}" for d in far if d & (d - 1) == 0]
-    place.meet(("core", "x", "y", "xy") + tuple(f"d{d}" for d in far))
+    far = [f"d{d}" for d in range(1, n_dp)]
+    place.meet(list(PLANE) + far)
     copies = Copies(place, send, recv)
     dp, col = place.dp, place.col
-    start_deal(copies, grads_a, out_a)
-    start_deal(copies, grads_b, out_b)
-    keeps = [
-        copies.keep(grads_a.at[col], out_a.at[col], local.at[1]),
-        copies.keep(grads_b.at[col], out_b.at[col], local.at[2]),
+    own_gates = gates_out.at[col]
+    parts = [copies.start(gate_part, own_gates.at[dp], name) for name in far]
+    planes = [copies.start(mixed, got.at[i], name) for i, name in enumerate(far)]
+    start_deal(copies, grads, grads_out)
+    stay = Stay(
+        [(gate_part, own_gates.at[dp]), (grads.at[col], grads_out.at[col])], bufs, local
+    )
+    stay.turn()
+    copies.land(*planes)
+    value = mixed[...]
+    for i in range(n_dp - 1):
+        value = value + got[i]
+    total[...] = value
+    ch[col] = value[:, :split]
+    for name in ("x", "y", "xy"):
+        copies.start(ch.at[col], ch.at[col], name)
+    rest = slice(split, None)
+    others = [
+        copies.start(total.at[:, rest], shared.at[i], name) for i, name in enumerate(PLANE)
     ]
-    own_gates = gates_out.at[col]
-    stay = copies.keep(gate_part, own_gates.at[dp], local.at[0])
-    parts = [copies.start(gate_part, own_gates.at[dp], f"d{d}") for d in far]
-    acc[0] = mixed[...]
-    n = 0
-    for name in steps:
-        copies.land(copies.start(acc.at[n], got.at[n], name))
-        acc[n + 1] = acc[n] + got[n]
-        n += 1
-    stay.wait()
+    stay.finish()
     copies.land(*parts)
-    half = gates_out.shape[1] // 2
+    half = n_dp // 2
     halves = (pl.ds(0, half), pl.ds(half, half))
 
     def gate_view(chip, h):
@@ -733,59 +798,51 @@
         for h in (0, 1)
         for name in ("x", "y")
     }
-    ch[col] = acc[n][:, :split]
-    x_ch = copies.start(ch.at[col], ch.at[col], "x")
-    rest = slice(split, None)
-    for name in ("core", "x", "y"):
-        number = copies.start(acc.at[n, :, rest], got.at[n, :, rest], name)
-        if name == "y":
-            copies.land(x_ch)
-            pair = pl.ds(lax.div(col, 2) * 2, 2)
-            y_ch = copies.start(ch.at[pair], ch.at[pair], "y")
-        copies.land(number)
-        acc[n + 1, :, rest] = acc[n, :, rest] + got[n, :, rest]
-        n += 1
+    copies.land(*others)
+    value = total[:, rest]
+    for i in range(len(PLANE)):
+        value = value + shared[i]
+    sums_out[...] = value
     copies.land(direct["x", 0])
     far_x = gate_view(place.chip(1), 0)
     copies.start(far_x, far_x, "y")
     copies.land(direct["y", 1])
     far_y = gate_view(place.chip(2), 1)
     copies.start(far_y, far_y, "x")
-    sums_out[...] = acc[n, :, rest]
-    copies.land(y_ch)
+    copies.finish()
     chans_out[...] = ch[...]
-    copies.finish()
-    for copy in keeps:
-        copy.wait()
-
-
-def sum_everywhere(mixed, split, gate_part, grads_a, grads_b, n_dp, n_col):
-    far = tuple(range(1, n_dp))
-    stages = len([d for d in far if d & (d - 1) == 0]) + 3
-    count = 2 * len(far) + stages + 14
+
+
+def sum_everywhere(mixed, split, gate_part, grads, n_dp, n_col):
+    count = 2 * n_dp + 20
     rows, columns = mixed.shape
+    rest = columns - split
     return pl.pallas_call(
-        functools.partial(sums_kernel, far, split),
+        functools.partial(sums_kernel, n_dp, split),
         out_shape=(
-            jax.ShapeDtypeStruct((rows, columns - split), f32),
+            jax.ShapeDtypeStruct((rows, rest), f32),
             jax.ShapeDtypeStruct((n_col, rows, split), f32),
             jax.ShapeDtypeStruct((n_col, n_dp) + gate_part.shape, gate_part.dtype),
-            jax.ShapeDtypeStruct(grads_a.shape, grads_a.dtype),
-            jax.ShapeDtypeStruct(grads_b.shape, grads_b.dtype),
+            jax.ShapeDtypeStruct(grads.shape, grads.dtype),
         ),
-        in_specs=[in_vmem] + [anywhere] * 3,
-        out_specs=(in_vmem, in_vmem) + (anywhere,) * 3,
+        in_specs=[in_vmem] + [anywhere] * 2,
+        out_specs=(in_vmem, in_vmem) + (anywhere,) * 2,
         scratch_shapes=[
-            pltpu.VMEM((stages, rows, columns), f32),
-            pltpu.VMEM((stages + 1, rows, columns), f32),
+            pltpu.VMEM((n_dp - 1, rows, columns), f32),
+            pltpu.VMEM((rows, columns), f32),
             pltpu.VMEM((n_col, rows, split), f32),
+            pltpu.VMEM((len(PLANE), rows, rest), f32),
             pltpu.SemaphoreType.DMA((count,)),
             pltpu.SemaphoreType.DMA((count,)),
-            pltpu.SemaphoreType.DMA((3,)),
+            pltpu.SemaphoreType.DMA((2,)),
+            pltpu.VMEM(gate_part.shape, gate_part.dtype),
+            pltpu.VMEM(grads.shape[1:], grads.dtype),
         ],
-        compiler_params=pltpu.CompilerParams(collective_id=5, has_side_effects=True),
+        compiler_params=pltpu.CompilerParams(
+            collective_id=5, has_side_effects=True, vmem_limit_bytes=24 * MIB
+        ),
         name="small_sums",
-    )(mixed, gate_part, grads_a, grads_b)
+    )(mixed, gate_part, grads)
 
 
 def one_less_exp(z):
@@ -851,6 +908,8 @@
     send,
     recv,
     local,
+    stay_sems,
+    *bufs,
 ):
     place = Place()
     place.meet(AROUND + ("next", "prev"))
@@ -864,12 +923,13 @@
     halo = copies.start(x_all.at[pl.ds(group - ROWS, ROWS), :], before, "next")
     found = weight_pieces(geo, (None, rec_out, mlp_in, mlp_out), (None, w_out, w_in, w_down))
     pieces = found["rec_out"] + found["mlp_in"] + found["mlp_out"]
-    dealer = Dealer(copies)
+    dealer = Dealer(copies, 9)
     for piece in pieces[:5]:
         dealer.deal(piece)
-    keep_own(copies, pieces, local, 2)
     for load in loads:
         load.wait()
+    own_block = (cotangent, block_view(cotangent, g_all, place.row, place.col, None))
+    stay = Stay([own_block] + own_pieces(place, pieces), bufs, stay_sems)
     high_tile = place.col >= 2
     idle_tile = lax.rem(place.col, 2) == 1
 
@@ -933,6 +993,7 @@
 
     third = n_tiles // 3
     lax.fori_loop(0, third, work, 0)
+    stay.turn()
     dealer.forward()
     dealer.forward()
     dealer.deal(pieces[5])
@@ -974,15 +1035,15 @@
         copies.keep(first, first_out, local.at[17]),
     ]
     dealer.forward()
-    gather = block_gather(copies, cotangent, g_all, local.at[18])
+    gather = block_gather(copies, cotangent, g_all)
     dealer.forward()
     dealer.forward()
     gather.pass_on()
     gather.last()
     copies.finish()
-    for copy in copies.local:
-        if not any(copy is load for load in loads):
-            copy.wait()
+    for copy in outs:
+        copy.wait()
+    stay.finish()
 
 
 def rec_forward(x_all, w_rec, params, places, cotangent, rec_out, mlp_in, mlp_out, geo):
@@ -1004,7 +1065,7 @@
         ((8, chans), f32),
     ]
     dealt = [((group, width), low), ((chans, width), low), ((2, width, span), low), ((span, width), low)]
-    copy_count = 1 + 6 * 8 + 10 + 1
+    copy_count = 1 + 6 * 8 + 12 + 1
     return pl.pallas_call(
         functools.partial(forward_kernel, geo),
         out_shape=tuple(of(*s) for s in kept + dealt),
@@ -1025,8 +1086,14 @@
             pltpu.VMEM((8, chans), f32),
             pltpu.SemaphoreType.DMA((copy_count,)),
             pltpu.SemaphoreType.DMA((copy_count,)),
-            pltpu.SemaphoreType.DMA((19,)),
-        ],
+            pltpu.SemaphoreType.DMA((18,)),
+            pltpu.SemaphoreType.DMA((9,)),
+            pltpu.VMEM(cotangent.shape, low),
+            pltpu.VMEM((bw, part), low),
+            pltpu.VMEM((LANES, part), low),
+        ]
+        + [pltpu.VMEM((part, span // 2), low)] * 4
+        + [pltpu.VMEM((span // 2, part), low)] * 2,
         compiler_params=pltpu.CompilerParams(
             collective_id=2, has_side_effects=True, vmem_limit_bytes=58 * MIB
         ),
@@ -1049,10 +1116,12 @@
     soft,
     conv_w,
     places,
+    down,
     d_all,
     d_rec_out,
     gate_out,
     sums,
+    down_out,
     buf,
     wv,
     dbv,
@@ -1072,14 +1141,16 @@
     gfar,
     carry,
     message,
+    down_buf,
     send,
     recv,
     local,
+    stay_sem,
 ):
     place = Place()
     n_dp = glo.shape[0]
     far = [f"d{d}" for d in range(1, n_dp)]
-    place.meet(["x", "y", "core", "next", "prev"] + far)
+    place.meet(["x", "y", "xy", "core", "next", "prev"] + far)
     copies = Copies(place, send, recv)
     n_col, part, bw, tiles, wide = geo
     chans = bw + LANES
@@ -1119,13 +1190,16 @@
 
     copies.land(gather.own)
     work(place.col)
-    gather.pass_on()
-    copies.land(gather.core_y)
+    x0, y0, x1, y1 = gather.pass_on()
+    start_deal(copies, down, down_out)
+    stay = Stay([(down.at[place.col], down_out.at[place.col])], [down_buf], stay_sem)
+    stay.turn()
+    copies.land(y0, y1)
     work(place.chip(2))
-    gather.last()
-    copies.land(gather.core_x)
+    corner = gather.last()
+    copies.land(x0, x1)
     work(place.chip(1))
-    copies.land(gather.core_xy)
+    copies.land(corner)
     out = copies.keep(buf, d_all, local.at[8])
     work(place.chip(3))
     for each in loads:
@@ -1282,24 +1356,26 @@
     copies.finish()
     out.wait()
     out_rec.wait()
-
-
-def rec_backward(d_out, w_out, kept, gates_blk, gates_rows, soft, conv_w, places, geo, n_dp):
+    stay.finish()
+
+
+def rec_backward(d_out, w_out, kept, gates_blk, gates_rows, soft, conv_w, places, down, geo, n_dp):
     n_col, part, bw, tiles, wide = geo
     own, width = d_out.shape
     slots = 2 * n_col
     group, chans = slots * own, bw + LANES
     part_rows = 2 * bw // n_dp
-    d_all, d_rec, gate_grads, sums = pl.pallas_call(
+    d_all, d_rec, gate_grads, sums, down_dealt = pl.pallas_call(
         functools.partial(backward_kernel, geo),
         out_shape=(
             jax.ShapeDtypeStruct((slots, own, width), low),
             jax.ShapeDtypeStruct((group, 2 * chans), low),
             jax.ShapeDtypeStruct((part_rows, chans), low),
             jax.ShapeDtypeStruct((8, chans), f32),
+            jax.ShapeDtypeStruct(down.shape, low),
         ),
-        in_specs=[anywhere] * 8 + [in_vmem] * 5,
-        out_specs=(anywhere, anywhere, in_vmem, in_vmem),
+        in_specs=[anywhere] * 8 + [in_vmem] * 5 + [anywhere],
+        out_specs=(anywhere, anywhere, in_vmem, in_vmem, anywhere),
         scratch_shapes=[
             pltpu.VMEM((slots, own, width), low),
             pltpu.VMEM(w_out.shape, low),
@@ -1320,16 +1396,18 @@
             pltpu.VMEM((n_dp - 1, part_rows, chans), low),
             pltpu.VMEM((8, chans), f32),
             pltpu.VMEM((8, chans), f32),
-            pltpu.SemaphoreType.DMA((15 + n_dp,)),
-            pltpu.SemaphoreType.DMA((15 + n_dp,)),
+            pltpu.VMEM(down.shape[1:], low),
+            pltpu.SemaphoreType.DMA((20 + n_dp,)),
+            pltpu.SemaphoreType.DMA((20 + n_dp,)),
             pltpu.SemaphoreType.DMA((10,)),
+            pltpu.SemaphoreType.DMA((1,)),
         ],
         compiler_params=pltpu.CompilerParams(
             collective_id=4, has_side_effects=True, vmem_limit_bytes=60 * MIB
         ),
         name="rec_backward",
-    )(d_out, w_out, *kept, gates_blk, gates_rows, soft, conv_w, places)
-    return d_all.reshape(group, width), d_rec, gate_grads, sums
+    )(d_out, w_out, *kept, gates_blk, gates_rows, soft, conv_w, places, down)
+    return d_all.reshape(group, width), d_rec, gate_grads, sums, down_dealt
 
 
 def outer_kernel(n_dp, first_steps, left1, right1, left2, right2, out_ref):
@@ -1530,7 +1608,7 @@
     g_in, sum_down, d_out = lax.optimization_barrier((g_in, sum_down, d_out))
     sum_in = lax.psum_scatter(g_in, "dp", scatter_dimension=0)
 
-    d_out_all, d_rec, gate_sums, small = rec_backward(
+    d_out_all, d_rec, gate_sums, small, down = rec_backward(
         d_out,
         w_out,
         (y_branch, state, first, pre_both, conv_low, x_rows),
@@ -1539,6 +1617,7 @@
         soft,
         conv_w_o,
         places,
+        sum_down,
         geo,
         n_dp,
     )
@@ -1582,8 +1661,8 @@
     gain_sums = jnp.concatenate([gain_one[:1], gain_two[:1]]).reshape(lines, 2 * width // lines)
     stat_block = jnp.pad(square_sums[None, :], ((0, lines - 1), (0, LANES - 4)))
     mixed = jnp.concatenate([small, gain_sums, stat_block], axis=1)
-    sums, chan_sums, gate_parts, into, down = sum_everywhere(
-        mixed, chans, gate_sums, sum_in, sum_down, n_dp, n_col
+    sums, chan_sums, gate_parts, into = sum_everywhere(
+        mixed, chans, gate_sums, sum_in, n_dp, n_col
     )
     sum_rec, into = lax.optimization_barrier((sum_rec, into))
     recs = deal_back(sum_rec, 10, "deal_rec")

time: 856 us -> 810 us (0.946)
  Pallas kernels: 772 us -> 722 us
    pallas_call x1, Pallas kernels: 72.9 us -> 50.1 us  [sum_everywhere(): pl.pallas_call(functools.partial(sums_kernel, n_dp, split), out_shape=(ja...]
    pallas_call x1, Pallas kernels: 171 us -> 150 us  [rec_forward(): pl.pallas_call(functools.partial(forward_kernel, geo), out_shape=tuple((o...]
  transfers between devices with their start and end apart: 3 -> 3, of which waited for: 1 -> 1; matrix products, arithmetic and copies ran while one was open for 4% -> 3% of each run, Pallas kernels for 47% -> 47%
where the time goes in v4:
time: 810 us; the launch traced here: 797 us
  Pallas kernels  722 us (89%)
  local copies, waits for them, and re-layouts  38.3 us (5%)
  other arithmetic  17.8 us (2%)
  between operations  14.7 us (2%)
    pallas_call x4, Pallas kernels, multiply_scatter(): pl.pallas_call(functools.partial(scatter_kernel, (n_parts, across, own, w...  227 us
    pallas_call x1, Pallas kernels, rec_forward(): pl.pallas_call(functools.partial(forward_kernel, geo), out_shape=tuple((o...  150 us
    pallas_call x1, Pallas kernels, rec_backward(): pl.pallas_call(functools.partial(backward_kernel, geo), out_shape=(jax.Sh...  96.1 us
    pallas_call x1, Pallas kernels, open_gather(): pl.pallas_call(functools.partial(open_kernel, geo), out_shape=(jax.ShapeD...  65.1 us
    pallas_call x1, Pallas kernels, glu(): pl.pallas_call(functools.partial(glu_kernel, spare), out_shape=(jax.Shape...  51.4 us
    pallas_call x1, Pallas kernels, sum_everywhere(): pl.pallas_call(functools.partial(sums_kernel, n_dp, split), out_shape=(ja...  50.1 us
    pallas_call x2, Pallas kernels, outer(): pl.pallas_call(functools.partial(outer_one_kernel, n_dp), grid=(n_col, co...  42.3 us
    pallas_call x1, Pallas kernels, outer_pair(): pl.pallas_call(functools.partial(outer_kernel, n_dp, steps1), grid=(n_col...  21.4 us
  transfers between devices with their start and end apart: 3, of which 1 were waited for; matrix products, arithmetic and copies ran while one was open for 3% of the time, Pallas kernels for 47%

profile of v4, /device:TPU:0, one launch (start us, length us, event | category | flops | bytes accessed | tf_op | source)
XLA Modules:
  0.0 797.4 jit_solution(5814831883001485963)
XLA Ops:
  12.1 65.1 %open_gather.1 = (bf16[1536,2560]{1,0:T(8,128)(2,1)}, bf16[2560,896]{1,0:T(8,128)(2,1)}, f32[4,2,640]{2,1,0:T(2,128)}) custom-call(bf16[768,640]{1,0:T(8,128)(2,1)} %tokens.1, bf16[2,640,1280]{2,1,0:T(8,128)(2,1)} %rec_in.1, f32[2,640]{1,0:T(2,128)} %gains.1), custom_call_target="tpu_custom_call" | custom-call | tf_op jit(solution)/shard_map/open_gather/pallas_call | solution.py:340
  80.8 1.8 fusion.6
  84.4 150.3 %rec_forward.1 = (bf16[1536,2560]{1,0:T(8,128)(2,1)}, f32[1544,512]{1,0:T(8,128)}, f32[1536,384]{1,0:T(8,128)}, f32[1536,768]{1,0:T(8,128)}, bf16[1536,512]{1,0:...) custom-call(bf16[1536,2560]{1,0:T(8,128)(2,1)} %get-tuple-element.79, ...), custom_call_target="tpu_custom_call" | custom-call | tf_op jit(solution)/shard_map/rec_forward/pallas_call | solution.py:1069
  234.7 45.6 %out_one.1 = (f32[192,2560]{1,0:T(8,128)}, bf16[192,2560]{1,0:T(8,128)(2,1)}, f32[8,128]{1,0:T(8,128)}) custom-call(bf16[1536,384]{1,0:T(8,128)(2,1)} %get-tuple-element.83.act.right2, bf16[384,2560]{1,0:T(8,128)(2,1)} %get-tuple-element.84.w.w_out, bf16[1536,2560]{1,0:T(8,128)(2,1)} %get-tuple-element.79.x_all.refs_0_, f32[2,2560]{1,0:T(2,128)} %bitcast.125), custom_call_target="tpu_custom_call" | custom-call | flops 3019898880 | bytes 41943040 | tf_op jit(solution)/shard_map/out_one/pallas_call | solution.py:617
  280.3 51.4 %glu.1 = (bf16[8,192,2560]{2,1,0:T(8,128)(2,1)}, bf16[1536,1024]{1,0:T(8,128)(2,1)}, bf16[1536,2048]{1,0:T(8,128)(2,1)}) custom-call(bf16[192,2560]{1,0:T(8,128)(2,1)} %get-tuple-element.85.n2, bf16[2,2560,1024]{2,1,0:T(8,128)(2,1)} %get-tuple-element.86.w_in.w, bf16[1024,2560]{1,0:T(8,128)(2,1)} %get-tuple-element.87.w_down.w, ...), custom_call_target="tpu_custom_call" | custom-call | flops 24159191040 | bytes 62914560 | tf_op jit(solution)/shard_map/glu/pallas_call | solution.py:471
  331.7 1.9 copy-done.10
  333.6 14.1 %outer_down.1 = bf16[4,4,160,1024]{3,2,1,0:T(8,128)(2,1)} custom-call(bf16[1536,2560]{1,0:T(8,128)(2,1)} %get-tuple-element.88.g_all.left.refs_1_, bf16[1536,1024]{1,0:T(8,128)(2,1)S(1)} %copy-done.10), custom_call_target="tpu_custom_call" | custom-call | flops 8053063680 | bytes 16252928 | tf_op jit(solution)/shard_map/outer_down/pallas_call | solution.py:1442
  347.8 28.2 %outer_in.1 = bf16[4,4,160,2048]{3,2,1,0:T(8,128)(2,1)} custom-call(bf16[1536,2560]{1,0:T(8,128)(2,1)} %bitcast.130, bf16[1536,2048]{1,0:T(8,128)(2,1)} %get-tuple-element.95.right.act), custom_call_target="tpu_custom_call" | custom-call | flops 16106127360 | bytes 24641536 | tf_op jit(solution)/shard_map/outer_in/pallas_call | solution.py:1442
  376.0 59.3 %d_normed_two.1 = (f32[192,2560]{1,0:T(8,128)}, bf16[192,2560]{1,0:T(8,128)(2,1)}, f32[8,2560]{1,0:T(8,128)}) custom-call(bf16[1536,2048]{1,0:T(8,128)(2,1)} %get-tuple-element.95.right.act, bf16[2,2560,1024]{2,1,0:T(8,128)(2,1)} %get-tuple-element.86.w_in.w, f32[192,2560]{1,0:T(8,128)} %get-tuple-element.96.refs_0_, ...), custom_call_target="tpu_custom_call" | custom-call | flops 16106127360 | bytes 41943040 | tf_op jit(solution)/shard_map/d_normed_two/pallas_call | solution.py:617
  435.3 4.5 reduce-scatter.4.cloned.1.call-done
  441.2 1.7 slice.282
  443.0 3.4 slice.281
  449.7 2.3 pad_maximum_fusion.w
  452.0 96.1 %rec_backward.1 = (bf16[8,192,2560]{2,1,0:T(8,128)(2,1)}, bf16[1536,768]{1,0:T(8,128)(2,1)}, bf16[128,384]{1,0:T(8,128)(2,1)}, f32[8,384]{1,0:T(8,128)}, bf16[4,160,1024]{2,1,0:T(8,128)(2,1)}) custom-call(bf16[192,2560]{1,0:T(8,128)(2,1)} %get-tuple-element.98.d_out, bf16[384,2560]{1,0:T(8,128)(2,1)} %get-tuple-element.84.w.w_out, ...), custom_call_target="tpu_custom_call" | custom-call | tf_op jit(solution)/shard_map/rec_backward/pallas_call | solution.py:1368
  548.2 1.7 copy-done.8
  549.8 21.4 %outer_rec.1 = bf16[4,4,160,1152]{3,2,1,0:T(8,128)(2,1)} custom-call(bf16[1536,2560]{1,0:T(8,128)(2,1)} %get-tuple-element.82.left1, bf16[1536,768]{1,0:T(8,128)(2,1)S(1)} %copy-done.8, bf16[1536,2560]{1,0:T(8,128)(2,1)} %bitcast.129, bf16[1536,384]{1,0:T(8,128)(2,1)S(1)} %copy-done.9), custom_call_target="tpu_custom_call" | custom-call | flops 9059696640 | bytes 25165824 | tf_op jit(solution)/shard_map/outer_rec/pallas_call | solution.py:1467
  571.2 62.3 %d_normed_one.1 = (bf16[768,640]{1,0:T(8,128)(2,1)}, f32[8,2560]{1,0:T(8,128)}, f32[8,128]{1,0:T(8,128)}) custom-call(bf16[1536,768]{1,0:T(8,128)(2,1)} %get-tuple-element.110.right1.act, bf16[2560,768]{1,0:T(8,128)(2,1)} %pad_maximum_fusion.w, bf16[1536,2560]{1,0:T(8,128)(2,1)} %get-tuple-element.79.x_all.refs_0_, f32[192,2560]{1,0:T(8,128)} %get-tuple-element.111.refs_1_, ...), custom_call_target="tpu_custom_call" | custom-call | flops 6039797760 | bytes 41943040 | tf_op jit(solution)/shard_map/d_normed_one/pallas_call | solution.py:617
  639.9 60.3 %out_two.1 = (bf16[768,640]{1,0:T(8,128)(2,1)}, f32[8,128]{1,0:T(8,128)}) custom-call(bf16[1536,1024]{1,0:T(8,128)(2,1)} %get-tuple-element.114.right.act, bf16[1024,2560]{1,0:T(8,128)(2,1)} %get-tuple-element.87.w_down.w, f32[192,2560]{1,0:T(8,128)} %get-tuple-element.96.refs_0_), custom_call_target="tpu_custom_call" | custom-call | flops 8053063680 | bytes 41943040 | tf_op jit(solution)/shard_map/out_two/pallas_call | solution.py:617
  701.4 2.7 maximum_bitcast_fusion.3
  704.1 50.1 %small_sums.1 = (f32[8,768]{1,0:T(8,128)S(1)}, f32[4,8,384]{2,1,0:T(8,128)S(1)}, bf16[4,4,128,384]{3,2,1,0:T(8,128)(2,1)S(1)}, bf16[4,160,2048]{2,1,0:T(8,128)(2,1)S(1)}) custom-call(f32[8,1152]{1,0:T(8,128)S(1)} %select_maximum_fusion.mixed, bf16[128,384]{1,0:T(8,128)(2,1)S(1)} %copy-done.7, bf16[4,160,2048]{2,1,0:T(8,128)(2,1)S(1)} %bitcast.114), custom_call_target="tpu_custom_call" | custom-call | tf_op jit(solution)/shard_map/small_sums/pallas_call | solution.py:820
  759.3 1.6 bitcast_convert_fusion
  761.8 1.7 copy-done.6
  763.5 17.6 %deal_rec.1 = bf16[4,160,1152]{2,1,0:T(8,128)(2,1)S(1)} custom-call(bf16[4,160,1152]{2,1,0:T(8,128)(2,1)S(1)} %bitcast.116), custom_call_target="tpu_custom_call" | custom-call | tf_op jit(solution)/shard_map/deal_rec/pallas_call | solution.py:723
  785.3 2.6 maximum_convert_fusion
  (118 shorter events, 35.0 us)
Async XLA Ops:
  7.2 0.9 copy-start
  7.2 432.6 %reduce-scatter.4.cloned.1.call-start = ((), (), s32[]{:S(2)}) async-start(), calls=%async_computation.3 | async-start | bytes 6553600 | tf_op jit(solution)/shard_map/reduce_scatter | solution.py:1594
  8.0 72.8 %copy-start.16 = (f32[1,128]{1,0:T(1,128)}, f32[1,128]{1,0:T(1,128)S(1)}, u32[]{:S(2)}) copy-start(f32[1,128]{1,0:T(1,128)S(1)} %dynamic-slice_bitcast_fusion.3) | copy-start | bytes 1540
  331.7 1.9 copy-start.10
  347.7 285.8 %reduce-scatter.6.cloned.1.call-start = ((), (), s32[]{:S(2)}) async-start(), calls=%async_computation.4 | async-start | bytes 13107200 | tf_op jit(solution)/shard_map/reduce_scatter | solution.py:1609
  439.8 322.0 %reduce-scatter.8.cloned.1.call-start = ((), (), s32[]{:S(2)}) async-start(), calls=%async_computation.5 | async-start | bytes 7372800 | tf_op jit(solution)/shard_map/reduce_scatter | solution.py:1643
  452.0 96.2 %copy-start.9 = (bf16[1536,384]{1,0:T(8,128)(2,1)S(1)}, bf16[1536,384]{1,0:T(8,128)(2,1)}, u32[]{:S(2)}) copy-start(bf16[1536,384]{1,0:T(8,128)(2,1)} %get-tuple-element.83.act.right2) | copy-start | bytes 3538948
  548.1 1.7 copy-start.8
  633.6 4.4 copy-start.11
  633.6 4.6 copy-start.15
  633.6 4.6 copy-start.17
  639.9 64.2 %copy-start.2 = (bf16[1,4,160,2048]{3,2,1,0:T(8,128)(2,1)S(1)}, bf16[1,4,160,2048]{3,2,1,0:T(8,128)(2,1)}, u32[]{:S(2)}) copy-start(bf16[1,4,160,2048]{3,2,1,0:T(8,128)(2,1)} %reduce-scatter.6.cloned.1.call-done) | copy-start | bytes 7864324
  639.9 64.2 %copy-start.7 = (bf16[128,384]{1,0:T(8,128)(2,1)S(1)}, bf16[128,384]{1,0:T(8,128)(2,1)}, u32[]{:S(2)}) copy-start(bf16[128,384]{1,0:T(8,128)(2,1)} %get-tuple-element.124.gate_part) | copy-start | bytes 294916
  754.2 1.5 copy-start.3
  755.7 1.1 copy-start.5
  761.2 20.1 %copy-start.14 = (f32[2,5,256,256]{3,2,1,0:T(8,128)}, f32[2,5,256,256]{3,2,1,0:T(8,128)S(1)}, u32[]{:S(2)}) copy-start(f32[2,5,256,256]{3,2,1,0:T(8,128)S(1)} %fusion.4) | copy-start | bytes 7864324
  761.8 1.7 copy-start.6
  781.3 2.0 copy-start.4
  785.3 2.6 copy-start.13
  785.3 5.1 copy-start.1
  787.9 1.6 copy-start.12
Sparse Core Ops, SparseCore 0:
  347.8 91.8 reduce-scatter.3
  442.1 185.3 reduce-scatter.5
  633.7 113.2 reduce-scatter.7

commit v5 on v4

--- a/solution.py
+++ b/solution.py
@@ -319,7 +319,7 @@
     own_block = (tokens, block_view(tokens, x_all, place.row, place.col, None))
     dealer.deal(pieces[2])
     dealer.deal(pieces[3])
-    mine = gains_all.at[place.col]
+    mine = gains_all.at[:, pl.ds(pl.multiple_of(place.col * geo[1], LANES), geo[1])]
     for name in ("x", "y", "xy"):
         copies.start(gains, mine, name)
     stay = Stay([own_block] + own_pieces(place, pieces) + [(gains, mine)], bufs, local)
@@ -342,7 +342,7 @@
         out_shape=(
             jax.ShapeDtypeStruct((2 * tokens.shape[0], width), low),
             jax.ShapeDtypeStruct((width, 3 * bw + LANES), low),
-            jax.ShapeDtypeStruct((n_col,) + gains.shape, f32),
+            jax.ShapeDtypeStruct((gains.shape[0], width), f32),
         ),
         in_specs=[anywhere] * 3,
         out_specs=(anywhere,) * 3,
@@ -394,20 +394,32 @@
     own, width = n2.shape
     n_col = buf.shape[0] // 2
     span = wd.shape[0]
-    step = 256
+    step = 512
     gather = slot_gather(copies, n2, buf, own)
     me = place.row * n_col + place.col
-    loads = [
-        copies.keep(n2, buf.at[me], local.at[0]),
-        copies.keep(w_in, wi, local.at[1]),
-        copies.keep(w_down, wd, local.at[2]),
-        copies.keep(g_all, g, local.at[3]),
-    ]
-    for load in loads:
+    n_steps = span // step
+    near_slots = [place.col, n_col + place.col]
+    far_slots = [r * n_col + place.chip(k) for k in (1, 2, 3) for r in (0, 1)]
+
+    def load_rows(slot, i):
+        rows = pl.ds(pl.multiple_of(slot * own, ROWS), own)
+        return copies.keep(g_all.at[rows, :], g.at[rows, :], local.at[i])
+
+    first = [copies.keep(n2, buf.at[me], local.at[3])]
+    first += [load_rows(slot, 4 + i) for i, slot in enumerate(near_slots)]
+    weights = []
+    for i in range(n_steps):
+        at = pl.ds(i * step, step)
+        weights.append(
+            (
+                copies.keep(w_in.at[:, :, at], wi.at[:, :, at], local.at[12 + 2 * i]),
+                copies.keep(w_down.at[at, :], wd.at[at, :], local.at[13 + 2 * i]),
+            )
+        )
+    others = [load_rows(slot, 6 + i) for i, slot in enumerate(far_slots)]
+    for load in first:
         load.wait()
     hide = spare(place.col)
-
-    n_steps = span // step
 
     def work(slots, first, size, lo, hi):
         rows = [pl.ds(pl.multiple_of(s * own + first, ROWS), size) for s in slots]
@@ -443,7 +455,12 @@
     half = own // 2
     near = both_cores(place.chip(1), place.chip(2))
     copies.land(gather.own)
-    work(both_cores(place.col), 0, own, 0, n_steps)
+    for i in range(n_steps):
+        for load in weights[i]:
+            load.wait()
+        work(both_cores(place.col), 0, own, i, i + 1)
+    for load in others:
+        load.wait()
     core0 = gather.pass_half(0)
     copies.land(*core0)
     work(near, 0, half, 0, n_steps // 2)
@@ -454,10 +471,10 @@
     corner = gather.last()
     work(near, half, half, n_steps // 2, n_steps)
     copies.land(corner)
-    out_n2 = copies.keep(buf, n2_all, local.at[4])
+    out_n2 = copies.keep(buf, n2_all, local.at[0])
     work(both_cores(place.chip(3)), 0, own, 0, n_steps)
-    out_h = copies.keep(hid, hidden, local.at[5])
-    out_d = copies.keep(dgl, d_glu, local.at[6])
+    out_h = copies.keep(hid, hidden, local.at[1])
+    out_d = copies.keep(dgl, d_glu, local.at[2])
     copies.finish()
     out_n2.wait()
     out_h.wait()
@@ -486,7 +503,7 @@
             pltpu.VMEM((group, 2 * span), low),
             pltpu.SemaphoreType.DMA((12,)),
             pltpu.SemaphoreType.DMA((12,)),
-            pltpu.SemaphoreType.DMA((7,)),
+            pltpu.SemaphoreType.DMA((12 + 2 * (span // 256),)),
         ],
         compiler_params=pltpu.CompilerParams(
             collective_id=3, has_side_effects=True, vmem_limit_bytes=58 * MIB
@@ -499,25 +516,55 @@
     return n_all.reshape(group, width), h, d
 
 
-def scatter_kernel(shape, finish, n_more, n_outs, homes, act, w, *refs):
+def start_home(copies, source, home, buf, sem):
+    place = copies.place
+    own, part = source.shape[0], home.shape[1]
+    spot = home.at[pl.ds(pl.multiple_of(place.col * own, ROWS), own), :]
+
+    def columns_of(chip):
+        return source.at[:, pl.ds(pl.multiple_of(chip * part, LANES), part)]
+
+    for name, j in (("xy", 3), ("x", 1), ("y", 2)):
+        copies.start(columns_of(place.chip(j)), spot, name)
+    return Stay([(columns_of(place.col), spot)], [buf], sem)
+
+
+def scatter_kernel(shape, finish, n_more, n_outs, pick, beside, act, w, *refs):
     n_parts, across, own, width = shape
+    side = []
+    if beside is not None:
+        n_in, n_out, n_hold = beside.counts
+        side, refs = list(refs[:n_in]), refs[n_in:]
     more, refs = refs[:n_more], refs[n_more:]
     outs, refs = refs[:n_outs], refs[n_outs:]
-    actv, wv, other, mine, from_core, from_x, from_y, turn, fin, back, send, recv, local, home_sem = refs[:14]
-    held = refs[14:]
+    if beside is not None:
+        side += refs[:n_out]
+        side += refs[len(refs) - n_hold :]
+        refs = refs[n_out : len(refs) - n_hold]
+    actv, wv, other, mine, from_core, from_x, from_y, turn, fin, send, recv, local = refs[:12]
+    held = refs[12 : 12 + n_more]
     place = Place()
-    place.meet(("x", "y", "xy", "core") if homes else ("x", "y", "core"))
+    place.meet(["x", "y", "core"] + ([] if beside is None else beside.names()))
     copies = Copies(place, send, recv)
+    if beside is not None:
+        beside.start(copies, *side)
     cut = own // 2
     n_col = act.shape[0] // own // 2
     k = act.shape[1] // n_parts
-    step = 256
-    loads = [copies.keep(act, actv, local.at[0]), copies.keep(w, wv, local.at[1])]
+    step = 512
+    loads = [copies.keep(act, actv, local.at[0])]
+    if pick is None:
+        loads.append(copies.keep(w, wv, local.at[1]))
+    else:
+        for i, (src, dst, size) in enumerate(pick(place.col)):
+            loads.append(
+                copies.keep(w.at[:, pl.ds(src, size)], wv.at[:, pl.ds(dst, size)], local.at[1 + i])
+            )
     my_rows = pl.ds(pl.multiple_of((place.row * n_col + place.col) * own, ROWS), own)
     extra = []
     for i, (ref, buf) in enumerate(zip(more, held)):
         src = ref.at[my_rows, :] if ref.shape[0] > own else ref
-        extra.append(copies.keep(src, buf, local.at[2 + i]))
+        extra.append(copies.keep(src, buf, local.at[4 + i]))
     for load in loads:
         load.wait()
     top, bottom = pl.ds(0, cut), pl.ds(cut, cut)
@@ -558,6 +605,8 @@
         mine[j] = mine[j] + from_core[j].astype(f32)
         turn[j] = mine[j].astype(low)
 
+    if beside is not None:
+        beside.turn()
     core3 = work(3)
     core1 = work(1)
     add_core(3, core3)
@@ -581,49 +630,56 @@
     fin[bottom, :] = mine[0, bottom, :] + from_y[1].astype(f32) + from_x[2].astype(f32)
     for load in extra:
         load.wait()
-    for ref in outs[(1 if homes else 0) :]:
+    for ref in outs:
         if ref.shape[0] == 8:
             ref[...] = jnp.zeros_like(ref)
     rows_at_once = 64
 
     def rows_done(i, carry):
         rows = pl.ds(pl.multiple_of(i * rows_at_once, rows_at_once), rows_at_once)
-        finish(rows, fin, held, back, outs[(1 if homes else 0) :])
+        finish(rows, fin, held, outs)
         return carry
 
     lax.fori_loop(0, own // rows_at_once, rows_done, 0)
-    if homes:
-        home = outs[0]
-        part = width // n_col
-
-        def columns_of(chip):
-            return back.at[:, pl.ds(pl.multiple_of(chip * part, LANES), part)]
-
-        spot = home.at[pl.ds(pl.multiple_of(place.col * own, ROWS), own), :]
-        for name, j in (("xy", 3), ("x", 1), ("y", 2)):
-            copies.start(columns_of(place.chip(j)), spot, name)
-        stay = copies.keep(columns_of(place.col), spot, home_sem)
-        stay.wait()
+    if beside is not None:
+        beside.finish(copies, *side)
     copies.finish()
 
 
-def multiply_scatter(act, w, across, number, name, finish, more, outs, homes):
+def multiply_scatter(act, w, across, number, name, finish, more, outs, pick=None, beside=None):
     n_parts = w.shape[0] if w.ndim == 3 else 1
     group = act.shape[0]
     n_col = lax.axis_size("col")
     own = group // (2 * n_col)
     width = w.shape[-2] if across else w.shape[-1]
     held = [((own, r.shape[1]) if r.shape[0] > own else r.shape, r.dtype) for r in more]
+    out_specs = [in_vmem] * len(outs)
+    scratch = [pltpu.VMEM(*h) for h in held]
+    n_outs, side_in, copy_count = len(outs), (), 13
+    in_specs = [anywhere] * (2 + len(more))
+    if beside is not None:
+        side_in, side_out, side_scratch = beside.inputs, beside.outputs, beside.scratch
+        in_specs = in_specs[:2] + beside.in_specs + in_specs[2:]
+        outs += side_out
+        out_specs += beside.out_specs
+        scratch += side_scratch
+        copy_count += beside.copy_count
     return pl.pallas_call(
         functools.partial(
-            scatter_kernel, (n_parts, across, own, width), finish, len(more), len(outs), homes
+            scatter_kernel,
+            (n_parts, across, own, width),
+            finish,
+            len(more),
+            n_outs,
+            pick,
+            beside,
         ),
         out_shape=tuple(jax.ShapeDtypeStruct(*s) for s in outs),
-        in_specs=[anywhere] * (2 + len(more)),
-        out_specs=tuple(anywhere if homes and i == 0 else in_vmem for i in range(len(outs))),
+        in_specs=in_specs,
+        out_specs=tuple(out_specs),
         scratch_shapes=[
             pltpu.VMEM(act.shape, low),
-            pltpu.VMEM(w.shape, low),
+            pltpu.VMEM(w.shape if pick is None else (width, act.shape[1]), low),
             pltpu.VMEM((4, own, width), low),
             pltpu.VMEM((4, own, width), f32),
             pltpu.VMEM((4, own, width), low),
@@ -631,13 +687,11 @@
             pltpu.VMEM((3, own // 2, width), low),
             pltpu.VMEM((4, own, width), low),
             pltpu.VMEM((own, width), f32),
-            pltpu.VMEM((own, width), low),
-            pltpu.SemaphoreType.DMA((13,)),
-            pltpu.SemaphoreType.DMA((13,)),
-            pltpu.SemaphoreType.DMA((2 + len(more),)),
-            pltpu.SemaphoreType.DMA,
+            pltpu.SemaphoreType.DMA((copy_count,)),
+            pltpu.SemaphoreType.DMA((copy_count,)),
+            pltpu.SemaphoreType.DMA((4 + len(held),)),
         ]
-        + [pltpu.VMEM(*h) for h in held],
+        + scratch,
         compiler_params=pltpu.CompilerParams(
             collective_id=number, has_side_effects=True, vmem_limit_bytes=60 * MIB
         ),
@@ -645,7 +699,114 @@
             flops=2 * group * width * act.shape[1], bytes_accessed=40 * MIB, transcendentals=0
         ),
         name=name,
-    )(act, w, *more)
+    )(act, w, *side_in, *more)
+
+
+def home_kernel(rows, home, send, recv, buf, sem):
+    place = Place()
+    place.meet(("x", "y", "xy"))
+    copies = Copies(place, send, recv)
+    stay = start_home(copies, rows, home, buf, sem)
+    stay.turn()
+    copies.finish()
+    stay.finish()
+
+
+def take_home(rows, n_col):
+    own, width = rows.shape
+    home = (n_col * own, width // n_col)
+    return pl.pallas_call(
+        home_kernel,
+        out_shape=jax.ShapeDtypeStruct(home, low),
+        in_specs=[anywhere],
+        out_specs=anywhere,
+        scratch_shapes=[
+            pltpu.SemaphoreType.DMA((3,)),
+            pltpu.SemaphoreType.DMA((3,)),
+            pltpu.VMEM((own, home[1]), low),
+            pltpu.SemaphoreType.DMA((1,)),
+        ],
+        compiler_params=pltpu.CompilerParams(collective_id=11, has_side_effects=True),
+        name="take_home",
+    )(rows)
+
+
+class GateReduce:
+    counts = (2, 2, 3)
+
+    def __init__(self, gates, small):
+        self.n_dp = gates.shape[0]
+        part = gates.shape[1:]
+        self.inputs = (gates, small)
+        self.outputs = ((part, low), (small.shape, f32))
+        self.copy_count = 2 * (self.n_dp - 1)
+        self.scratch = [
+            pltpu.VMEM(gates.shape, low),
+            pltpu.VMEM((self.n_dp - 1,) + part, low),
+            pltpu.VMEM((self.n_dp - 1,) + small.shape, f32),
+        ]
+
+    in_specs, out_specs = [in_vmem] * 2, [in_vmem] * 2
+
+    def turn(self):
+        pass
+
+    def names(self):
+        return [f"d{d}" for d in range(1, self.n_dp)]
+
+    def start(self, copies, gates, small, part_out, small_out, held, far, far_small):
+        dp = copies.place.dp
+        held[...] = gates[...]
+        self.numbers = []
+        for i, name in enumerate(self.names()):
+            other = jnp.bitwise_xor(dp, i + 1)
+            self.numbers.append(copies.start(held.at[other], far.at[i], name))
+            self.numbers.append(copies.start(small, far_small.at[i], name))
+
+    def finish(self, copies, gates, small, part_out, small_out, held, far, far_small):
+        copies.land(*self.numbers)
+        total = held[copies.place.dp].astype(f32)
+        value = small[...]
+        for i in range(self.n_dp - 1):
+            total = total + far[i].astype(f32)
+            value = value + far_small[i]
+        part_out[...] = total.astype(low)
+        small_out[...] = value
+
+
+class GateGather:
+    counts = (2, 2, 3)
+    in_specs, out_specs = [in_vmem, anywhere], [in_vmem, anywhere]
+
+    def __init__(self, part, grads, n_dp):
+        self.n_dp = n_dp
+        self.inputs = (part, grads)
+        self.outputs = (((n_dp,) + part.shape, low), (grads.shape, grads.dtype))
+        self.copy_count = n_dp + 2
+        self.scratch = [
+            pltpu.VMEM((n_dp,) + part.shape, low),
+            pltpu.VMEM(grads.shape[1:], grads.dtype),
+            pltpu.SemaphoreType.DMA((1,)),
+        ]
+
+    def names(self):
+        return ["xy"] + [f"d{d}" for d in range(1, self.n_dp)]
+
+    def start(self, copies, part, grads, all_out, grads_out, held, buf, sem):
+        col = copies.place.col
+        mine = held.at[copies.place.dp]
+        self.numbers = [copies.start(part, mine, name) for name in self.names()[1:]]
+        start_deal(copies, grads, grads_out)
+        self.stay = Stay([(grads.at[col], grads_out.at[col])], [buf], sem)
+
+    def turn(self):
+        self.stay.turn()
+
+    def finish(self, copies, part, grads, all_out, grads_out, held, buf, sem):
+        held[copies.place.dp] = part[...]
+        copies.land(*self.numbers)
+        all_out[...] = held[...]
+        self.stay.finish()
 
 
 def square_sum(ref, row, x):
@@ -656,7 +817,7 @@
     return lax.rsqrt(jnp.mean(x * x, axis=-1, keepdims=True) + epsilon)
 
 
-def after_out_one(rows, fin, held, back, outs):
+def after_out_one(rows, fin, held, outs):
     x, gain = held
     resid_out, n2_out, squares = outs
     out_one = fin[rows, :]
@@ -675,7 +836,7 @@
     return scale * gained - x * (scale * scale * scale * inner)
 
 
-def after_normed_two(rows, fin, held, back, outs):
+def after_normed_two(rows, fin, held, outs):
     resid, upstream, gain = held
     d_resid_out, d_out, grad_gain = outs
     d_resid = upstream[rows, :].astype(f32) + norm_back(
@@ -685,18 +846,18 @@
     d_out[rows, :] = d_resid.astype(low)
 
 
-def after_normed_one(rows, fin, held, back, outs):
+def after_normed_one(rows, fin, held, outs):
     x, d_resid, gain = held
-    grad_gain, squares = outs
+    back, grad_gain, squares = outs
     x_here = x[rows, :].astype(f32)
     passed = norm_back(fin[rows, :], x_here, gain[0:1, :], grad_gain)
     back[rows, :] = (d_resid[rows, :] + passed).astype(low)
     square_sum(squares, 0, x_here)
 
 
-def after_out_two(rows, fin, held, back, outs):
+def after_out_two(rows, fin, held, outs):
     (resid,) = held
-    (squares,) = outs
+    back, squares = outs
     out_two = fin[rows, :]
     back[rows, :] = (resid[rows, :] + out_two).astype(low)
     square_sum(squares, 0, out_two)
@@ -743,106 +904,106 @@
 
 def sums_kernel(
     n_dp,
-    split,
     mixed,
-    gate_part,
-    grads,
+    small,
+    gates,
+    rows,
     sums_out,
     chans_out,
     gates_out,
-    grads_out,
+    home,
     got,
     total,
+    shared,
     ch,
-    shared,
+    gv,
     send,
     recv,
-    local,
     *bufs,
 ):
     place = Place()
     far = [f"d{d}" for d in range(1, n_dp)]
     place.meet(list(PLANE) + far)
     copies = Copies(place, send, recv)
-    dp, col = place.dp, place.col
-    own_gates = gates_out.at[col]
-    parts = [copies.start(gate_part, own_gates.at[dp], name) for name in far]
     planes = [copies.start(mixed, got.at[i], name) for i, name in enumerate(far)]
-    start_deal(copies, grads, grads_out)
-    stay = Stay(
-        [(gate_part, own_gates.at[dp]), (grads.at[col], grads_out.at[col])], bufs, local
-    )
-    stay.turn()
-    copies.land(*planes)
-    value = mixed[...]
-    for i in range(n_dp - 1):
-        value = value + got[i]
-    total[...] = value
-    ch[col] = value[:, :split]
+    col = place.col
+    ch[col] = small[...]
+    gv[col] = gates[...]
     for name in ("x", "y", "xy"):
         copies.start(ch.at[col], ch.at[col], name)
-    rest = slice(split, None)
-    others = [
-        copies.start(total.at[:, rest], shared.at[i], name) for i, name in enumerate(PLANE)
-    ]
-    stay.finish()
-    copies.land(*parts)
     half = n_dp // 2
     halves = (pl.ds(0, half), pl.ds(half, half))
 
     def gate_view(chip, h):
-        return gates_out.at[chip, halves[h]]
+        return gv.at[chip, halves[h]]
 
     direct = {
         (name, h): copies.start(gate_view(col, h), gate_view(col, h), name)
         for h in (0, 1)
         for name in ("x", "y")
     }
-    copies.land(*others)
-    value = total[:, rest]
-    for i in range(len(PLANE)):
-        value = value + shared[i]
-    sums_out[...] = value
+    stay_home = start_home(copies, rows, home, bufs[0], bufs[1])
+    stay_home.turn()
     copies.land(direct["x", 0])
     far_x = gate_view(place.chip(1), 0)
     copies.start(far_x, far_x, "y")
     copies.land(direct["y", 1])
     far_y = gate_view(place.chip(2), 1)
     copies.start(far_y, far_y, "x")
+    copies.land(*planes)
+    value = mixed[...]
+    for i in range(n_dp - 1):
+        value = value + got[i]
+    total[...] = value
+    others = [copies.start(total, shared.at[i], name) for i, name in enumerate(PLANE)]
+    copies.land(*others)
+    for i in range(len(PLANE)):
+        value = value + shared[i]
+    sums_out[...] = value
     copies.finish()
     chans_out[...] = ch[...]
-
-
-def sum_everywhere(mixed, split, gate_part, grads, n_dp, n_col):
-    count = 2 * n_dp + 20
-    rows, columns = mixed.shape
-    rest = columns - split
+    gates_out[...] = gv[...]
+    stay_home.finish()
+
+
+def sum_everywhere(mixed, small, gates, rows_low, n_dp, n_col):
+    count = n_dp + 22
+    home = (n_col * rows_low.shape[0], rows_low.shape[1] // n_col)
     return pl.pallas_call(
-        functools.partial(sums_kernel, n_dp, split),
+        functools.partial(sums_kernel, n_dp),
         out_shape=(
-            jax.ShapeDtypeStruct((rows, rest), f32),
-            jax.ShapeDtypeStruct((n_col, rows, split), f32),
-            jax.ShapeDtypeStruct((n_col, n_dp) + gate_part.shape, gate_part.dtype),
-            jax.ShapeDtypeStruct(grads.shape, grads.dtype),
+            jax.ShapeDtypeStruct(mixed.shape, f32),
+            jax.ShapeDtypeStruct((n_col,) + small.shape, f32),
+            jax.ShapeDtypeStruct((n_col,) + gates.shape, low),
+            jax.ShapeDtypeStruct(home, low),
         ),
-        in_specs=[in_vmem] + [anywhere] * 2,
-        out_specs=(in_vmem, in_vmem) + (anywhere,) * 2,
+        in_specs=[in_vmem] * 3 + [anywhere],
+        out_specs=(in_vmem,) * 3 + (anywhere,),
         scratch_shapes=[
-            pltpu.VMEM((n_dp - 1, rows, columns), f32),
-            pltpu.VMEM((rows, columns), f32),
-            pltpu.VMEM((n_col, rows, split), f32),
-            pltpu.VMEM((len(PLANE), rows, rest), f32),
+            pltpu.VMEM((n_dp - 1,) + mixed.shape, f32),
+            pltpu.VMEM(mixed.shape, f32),
+            pltpu.VMEM((len(PLANE),) + mixed.shape, f32),
+            pltpu.VMEM((n_col,) + small.shape, f32),
+            pltpu.VMEM((n_col,) + gates.shape, low),
             pltpu.SemaphoreType.DMA((count,)),
             pltpu.SemaphoreType.DMA((count,)),
-            pltpu.SemaphoreType.DMA((2,)),
-            pltpu.VMEM(gate_part.shape, gate_part.dtype),
-            pltpu.VMEM(grads.shape[1:], grads.dtype),
+            pltpu.VMEM((rows_low.shape[0], home[1]), low),
+            pltpu.SemaphoreType.DMA((1,)),
         ],
         compiler_params=pltpu.CompilerParams(
             collective_id=5, has_side_effects=True, vmem_limit_bytes=24 * MIB
         ),
         name="small_sums",
-    )(mixed, gate_part, grads)
+    )(mixed, small, gates, rows_low)
+
+
+def own_lanes(place, geo):
+    n_col, part, bw, tiles, wide = geo
+    found = [
+        pl.ds(pl.multiple_of(place.col * bw + k * LANES, LANES), LANES) for k in range(bw // LANES)
+    ]
+    shared_tile = n_col * bw + lax.div(place.col, 2) * LANES
+    return found + [pl.ds(pl.multiple_of(shared_tile, LANES), LANES)]
 
 
 def one_less_exp(z):
@@ -870,8 +1031,7 @@
     x_all,
     w_rec,
     gain,
-    gates_blk,
-    gates_tile,
+    gates,
     bias,
     soft,
     conv_w,
@@ -931,12 +1091,17 @@
     own_block = (cotangent, block_view(cotangent, g_all, place.row, place.col, None))
     stay = Stay([own_block] + own_pieces(place, pieces), bufs, stay_sems)
     high_tile = place.col >= 2
+    mine = own_lanes(place, geo)
+    conv_lanes = mine[:-1] + [
+        slice(n_col * bw + k * LANES, n_col * bw + (k + 1) * LANES) for k in range(bw // LANES)
+    ]
+    tile_cols = pl.ds(pl.multiple_of(lax.div(place.col, 2) * LANES, LANES), LANES)
     idle_tile = lax.rem(place.col, 2) == 1
 
     def normed(x):
         x = x.astype(f32)
         scale = lax.rsqrt(jnp.sum(x * x, axis=-1, keepdims=True) / width + epsilon)
-        return (x * scale * gain[...]).astype(low)
+        return (x * scale * gain[0:1, :]).astype(low)
 
     copies.land(halo)
     xb[0:8, :] = dot(normed(before[...]), wv[:, : 2 * bw])[ROWS - 8 :]
@@ -957,16 +1122,20 @@
         for lane in range(2 * bw // LANES):
             at = slice(lane * LANES, (lane + 1) * LANES)
             near = reach[:, at]
-            total = conv_b[0:1, at] + conv_w[0:1, at] * near[8:]
+            tap = conv_lanes[lane]
+            total = conv_b[0:1, tap] + conv_w[0:1, tap] * near[8:]
             for t in range(1, conv_w.shape[0]):
                 lagged = pltpu.roll(near, t, 0)[8:]
-                total = total + jnp.where(spot >= t, conv_w[t : t + 1, at] * lagged, 0.0)
+                total = total + jnp.where(spot >= t, conv_w[t : t + 1, tap] * lagged, 0.0)
             conv.append(total.astype(low))
         c = jnp.concatenate(conv, axis=1)
         cv[rows, :] = c
         pre = [
-            jnp.concatenate([dot(c[:, :bw], gates_blk[j]), dot(c[:, bw:], gates_tile[j])], axis=1)
-            + bias[j : j + 1, :]
+            jnp.concatenate(
+                [dot(c[:, :bw], gates[j, place.col]), dot(c[:, bw:], gates[j, n_col, :, tile_cols])],
+                axis=1,
+            )
+            + jnp.concatenate([bias[j : j + 1, at] for at in mine], axis=1)
             for j in range(2)
         ]
         prev[rows, :chans] = pre[0]
@@ -978,7 +1147,7 @@
                 own_c = conv[lane].astype(f32)
             else:
                 own_c = jnp.where(high_tile, conv[lane + 1].astype(f32), conv[lane].astype(f32))
-            log_a = -8.0 * jax.nn.sigmoid(pre[1][:, at]) * soft[0:1, at]
+            log_a = -8.0 * jax.nn.sigmoid(pre[1][:, at]) * soft[0:1, mine[lane]]
             a = jnp.where(reset, 0.0, jnp.exp(log_a))
             m = jnp.where(reset, 1.0, jnp.sqrt(one_less_exp(2.0 * log_a)))
             u = own_c * jax.nn.sigmoid(pre[0][:, at]) * m
@@ -1069,7 +1238,7 @@
     return pl.pallas_call(
         functools.partial(forward_kernel, geo),
         out_shape=tuple(of(*s) for s in kept + dealt),
-        in_specs=[anywhere] * 2 + [in_vmem] * 8 + [anywhere] * 4,
+        in_specs=[anywhere] * 2 + [in_vmem] * 7 + [anywhere] * 4,
         out_specs=(anywhere,) * 12,
         scratch_shapes=[
             pltpu.VMEM((group, width), low),
@@ -1111,8 +1280,7 @@
     pre_in,
     c_in,
     x_in,
-    gates_blk,
-    gates_rows,
+    gates,
     soft,
     conv_w,
     places,
@@ -1126,6 +1294,7 @@
     wv,
     dbv,
     yv,
+    slv,
     hs,
     prev,
     cv,
@@ -1137,8 +1306,6 @@
     dcv,
     drv,
     gg,
-    glo,
-    gfar,
     carry,
     message,
     down_buf,
@@ -1148,18 +1315,16 @@
     stay_sem,
 ):
     place = Place()
-    n_dp = glo.shape[0]
-    far = [f"d{d}" for d in range(1, n_dp)]
-    place.meet(["x", "y", "xy", "core", "next", "prev"] + far)
+    place.meet(["x", "y", "xy", "core", "next", "prev"])
     copies = Copies(place, send, recv)
     n_col, part, bw, tiles, wide = geo
     chans = bw + LANES
-    own = d_out.shape[0]
+    own_rows = d_out.shape[0]
     group = yv.shape[0]
     tile = 256
     n_tiles = group // tile
     lanes = [slice(k * LANES, (k + 1) * LANES) for k in range(chans // LANES)]
-    gather = slot_gather(copies, d_out, buf, own)
+    gather = slot_gather(copies, d_out, buf, own_rows)
     me = place.row * n_col + place.col
     load = copies.keep(w_out, wv, local.at[0])
     mine = copies.keep(d_out, buf.at[me], local.at[1])
@@ -1180,17 +1345,34 @@
     mine.wait()
     high_tile = place.col >= 2
     idle_tile = lax.rem(place.col, 2) == 1
+    mine_at = own_lanes(place, geo)
+    tile_rows = pl.ds(pl.multiple_of(lax.div(place.col, 2) * LANES, LANES), LANES)
 
     def work(chip):
         slots = (chip, n_col + chip)
         value = dot(jnp.concatenate([buf[s] for s in slots], axis=0), wv[...], ((1,), (1,)))
         for n, s in enumerate(slots):
-            rows = pl.ds(pl.multiple_of(s * own, ROWS), own)
-            dbv[rows, :] = value[n * own : (n + 1) * own]
+            rows = pl.ds(pl.multiple_of(s * own_rows, ROWS), own_rows)
+            dbv[rows, :] = value[n * own_rows : (n + 1) * own_rows]
+
+    def before_rows(k, unused):
+        rows = pl.ds(pl.multiple_of(k * tile, tile), tile)
+        for at in lanes:
+            value, slope = tanh_parts(yv[rows, at])
+            yv[rows, at] = value
+            slv[rows, at] = slope
+        prev[rows, :] = jax.nn.sigmoid(prev[rows, :])
+        return unused
 
     copies.land(gather.own)
     work(place.col)
-    x0, y0, x1, y1 = gather.pass_on()
+    for each in loads:
+        each.wait()
+    third = n_tiles // 3
+    lax.fori_loop(0, third, before_rows, 0)
+    x0, y0 = gather.pass_half(0)
+    lax.fori_loop(third, 2 * third, before_rows, 0)
+    x1, y1 = gather.pass_half(1)
     start_deal(copies, down, down_out)
     stay = Stay([(down.at[place.col], down_out.at[place.col])], [down_buf], stay_sem)
     stay.turn()
@@ -1199,15 +1381,17 @@
     corner = gather.last()
     copies.land(x0, x1)
     work(place.chip(1))
+    lax.fori_loop(2 * third, n_tiles, before_rows, 0)
     copies.land(corner)
     out = copies.keep(buf, d_all, local.at[8])
     work(place.chip(3))
-    for each in loads:
-        each.wait()
+
+    def own(at):
+        return mine_at[at.start // LANES]
 
     def coeffs(rows, at, spot):
-        rate = jax.nn.sigmoid(prev[rows, slice(chans + at.start, chans + at.stop)])
-        log_a = -8.0 * rate * soft[0:1, at]
+        rate = prev[rows, slice(chans + at.start, chans + at.stop)]
+        log_a = -8.0 * rate * soft[0:1, own(at)]
         return rate, log_a, jnp.where(spot == 0, 0.0, jnp.exp(log_a))
 
     carry[0:1] = jnp.zeros_like(carry[0:1])
@@ -1222,7 +1406,7 @@
             d_branch = dbv[rows, at]
             if at.start >= bw:
                 d_branch = jnp.where(idle_tile, 0.0, d_branch)
-            value, slope = tanh_parts(yv[rows, at])
+            value, slope = yv[rows, at], slv[rows, at]
             state = hs[pl.ds(pl.multiple_of(r0 + 8, 8), tile), at]
             d_state = d_branch * value
             drv[rows, slice(chans + at.start, chans + at.stop)] = (d_branch * state * slope).astype(low)
@@ -1258,13 +1442,13 @@
                     cv[rows, slice(at.start + LANES, at.stop + LANES)].astype(f32),
                     cv[rows, at].astype(f32),
                 )
-            gate = jax.nn.sigmoid(prev[rows, at])
+            gate = prev[rows, at]
             rate, log_a, a = coeffs(rows, at, spot)
             m = jnp.where(reset, 1.0, jnp.sqrt(one_less_exp(2.0 * log_a)))
             gated = gate * m
             d_log = jnp.where(reset, 0.0, g * before * a - g * c * gate * a * a / m)
             d_pre_in = (g * c * gated * (1.0 - gate)).astype(low)
-            d_pre_rate = (d_log * (-8.0 * soft[0:1, at]) * rate * (1.0 - rate)).astype(low)
+            d_pre_rate = (d_log * (-8.0 * soft[0:1, own(at)]) * rate * (1.0 - rate)).astype(low)
             dpv[rows, at] = d_pre_in
             dpv[rows, slice(chans + at.start, chans + at.stop)] = d_pre_rate
             dcv[rows, at] = g * gated
@@ -1298,8 +1482,8 @@
             five = jnp.concatenate(
                 [jnp.where(high_tile, far, here), jnp.where(high_tile, here, far)], axis=1
             )
-            d_blk = d_blk + dot(p_blk, gates_blk[j], ((1,), (1,)))
-            d_tile = d_tile + dot(five, gates_rows[j], ((1,), (1,)))
+            d_blk = d_blk + dot(p_blk, gates[j, place.col], ((1,), (1,)))
+            d_tile = d_tile + dot(five, gates[j, n_col, tile_rows, :], ((1,), (1,)))
             gg[j, :, :bw] += dot(c[:, :bw], p_blk, ((0,), (0,)))
             gg[j, :, bw:] += dot(c[:, bw:], here, ((0,), (0,)))
         dcv[rows, :bw] = d_blk
@@ -1312,14 +1496,10 @@
     lax.fori_loop(1, n_tiles // 2, through_blocks, 0)
     copies.land(swaps[2], swaps[3])
     lax.fori_loop(n_tiles // 2, n_tiles, through_blocks, 0)
-    part_rows = gate_out.shape[0]
-    for p in range(n_dp):
+    part_rows = gate_out.shape[1]
+    for p in range(gate_out.shape[0]):
         j, first_row = divmod(p * part_rows, bw)
-        glo[p] = gg[j, first_row : first_row + part_rows].astype(low)
-    parts = [
-        copies.start(glo.at[jnp.bitwise_xor(place.dp, d + 1)], gfar.at[d], name)
-        for d, name in enumerate(far)
-    ]
+        gate_out[p] = gg[j, first_row : first_row + part_rows].astype(low)
     copies.land(later)
 
     def through_conv(k, unused):
@@ -1334,10 +1514,10 @@
             else:
                 x = jnp.where(high_tile, xb[ext, slice(at.start + LANES, at.stop + LANES)], xb[ext, at])
             d_c = reach[:tile]
-            d_x = conv_w[0:1, at] * d_c
+            d_x = conv_w[0:1, own(at)] * d_c
             sums[3:4, at] += jnp.sum(d_c * x[8:], axis=0, keepdims=True)
             for t in range(1, conv_w.shape[0]):
-                term = jnp.where(spot >= t, conv_w[t : t + 1, at] * reach, 0.0)
+                term = jnp.where(spot >= t, conv_w[t : t + 1, own(at)] * reach, 0.0)
                 d_x = d_x + pltpu.roll(term, tile + 8 - t, 0)[:tile]
                 lagged = pltpu.roll(x, t, 0)[8:]
                 here = jnp.where(spot[:tile] >= t, d_c * lagged, 0.0)
@@ -1347,19 +1527,16 @@
         return unused
 
     lax.fori_loop(0, n_tiles, through_conv, 0)
+    for at in lanes:
+        sums[2:3, at] = sums[2:3, at] * soft[1:2, own(at)]
     out_rec = copies.keep(drv, d_rec_out, local.at[9])
-    copies.land(*parts)
-    total = glo[place.dp].astype(f32)
-    for d in range(n_dp - 1):
-        total = total + gfar[d].astype(f32)
-    gate_out[...] = total.astype(low)
     copies.finish()
     out.wait()
     out_rec.wait()
     stay.finish()
 
 
-def rec_backward(d_out, w_out, kept, gates_blk, gates_rows, soft, conv_w, places, down, geo, n_dp):
+def rec_backward(d_out, w_out, kept, gates, soft, conv_w, places, down, geo, n_dp):
     n_col, part, bw, tiles, wide = geo
     own, width = d_out.shape
     slots = 2 * n_col
@@ -1370,15 +1547,16 @@
         out_shape=(
             jax.ShapeDtypeStruct((slots, own, width), low),
             jax.ShapeDtypeStruct((group, 2 * chans), low),
-            jax.ShapeDtypeStruct((part_rows, chans), low),
+            jax.ShapeDtypeStruct((n_dp, part_rows, chans), low),
             jax.ShapeDtypeStruct((8, chans), f32),
             jax.ShapeDtypeStruct(down.shape, low),
         ),
-        in_specs=[anywhere] * 8 + [in_vmem] * 5 + [anywhere],
+        in_specs=[anywhere] * 8 + [in_vmem] * 4 + [anywhere],
         out_specs=(anywhere, anywhere, in_vmem, in_vmem, anywhere),
         scratch_shapes=[
             pltpu.VMEM((slots, own, width), low),
             pltpu.VMEM(w_out.shape, low),
+            pltpu.VMEM((group, chans), f32),
             pltpu.VMEM((group, chans), f32),
             pltpu.VMEM((group, chans), f32),
             pltpu.VMEM((group + 8, chans), f32),
@@ -1392,13 +1570,11 @@
             pltpu.VMEM((group + 8, chans), f32),
             pltpu.VMEM((group, 2 * chans), low),
             pltpu.VMEM((2, bw, chans), f32),
-            pltpu.VMEM((n_dp, part_rows, chans), low),
-            pltpu.VMEM((n_dp - 1, part_rows, chans), low),
             pltpu.VMEM((8, chans), f32),
             pltpu.VMEM((8, chans), f32),
             pltpu.VMEM(down.shape[1:], low),
-            pltpu.SemaphoreType.DMA((20 + n_dp,)),
-            pltpu.SemaphoreType.DMA((20 + n_dp,)),
+            pltpu.SemaphoreType.DMA((22,)),
+            pltpu.SemaphoreType.DMA((22,)),
             pltpu.SemaphoreType.DMA((10,)),
             pltpu.SemaphoreType.DMA((1,)),
         ],
@@ -1406,7 +1582,7 @@
             collective_id=4, has_side_effects=True, vmem_limit_bytes=60 * MIB
         ),
         name="rec_backward",
-    )(d_out, w_out, *kept, gates_blk, gates_rows, soft, conv_w, places, down)
+    )(d_out, w_out, *kept, gates, soft, conv_w, places, down)
     return d_all.reshape(group, width), d_rec, gate_grads, sums, down_dealt
 
 
@@ -1531,47 +1707,15 @@
 
     geo = (n_col, part, bw, tiles, wide)
     x_all, w_rec, gains_all = open_gather(tokens, rec_in, gains, geo)
-    gains_all = gains_all.transpose(1, 0, 2).reshape(gains.shape[0], width)
-    w_x, w_y = w_rec[:, : 2 * bw], w_rec[:, 2 * bw :]
-
-    tile_at = shared + (col // 2) * LANES
-
-    def own_channels(x):
-        blk = lax.dynamic_slice_in_dim(x, col * bw, bw, axis=-1)
-        tile = lax.dynamic_slice_in_dim(x, tile_at, LANES, axis=-1)
-        return jnp.concatenate([blk, tile], axis=-1)
-
-    def block_channels(x):
-        blk = lax.dynamic_slice_in_dim(x, col * bw, bw, axis=-1)
-        return jnp.concatenate([blk, x[..., shared:]], axis=-1)
-
-    bias = own_channels(gate_bias)
-    decay_o = own_channels(decay)
-    conv_w_c = block_channels(conv_w)
-    conv_b_c = block_channels(conv_b)
-    conv_w_o = own_channels(conv_w)
-    gates_blk = lax.dynamic_index_in_dim(gates, col, axis=1, keepdims=False)
-    gates_five = gates[:, n_col]
-    gates_tile = lax.dynamic_slice_in_dim(gates_five, (col // 2) * LANES, LANES, axis=2)
-    gates_rows = lax.dynamic_slice_in_dim(gates_five, (col // 2) * LANES, LANES, axis=1)
-
     base = dp * group
     places = places_of(base + jnp.arange(group + 8, dtype=jnp.int32), lengths)
     places = jnp.broadcast_to(places[:, None], (group + 8, LANES))
-    soft = jax.nn.softplus(decay_o)[None, :]
+    soft = jnp.stack([jax.nn.softplus(decay), jax.nn.sigmoid(decay)])
 
     n1, x_rows, y_branch, pre_both, conv_low, state, branch, first, g_all, w_out, w_in, w_down = rec_forward(
         x_all,
         w_rec,
-        (
-            gains_all[0:1],
-            gates_blk,
-            gates_tile,
-            bias,
-            soft,
-            conv_w_c,
-            conv_b_c[None, :],
-        ),
+        (gains_all, gates, gate_bias, soft, conv_w, conv_b[None, :]),
         places,
         cotangent,
         rec_out,
@@ -1580,19 +1724,19 @@
         geo,
     )
     rows_f, rows_b = ((own, width), f32), ((own, width), low)
-    line, squares, home = ((8, width), f32), ((8, LANES), f32), ((given, part), low)
+    line, squares = ((8, width), f32), ((8, LANES), f32)
     resid, normed_two, squares_one = multiply_scatter(
-        branch, w_out, False, 6, "out_one", after_out_one, (x_all, gains_all), (rows_f, rows_b, squares), False
+        branch, w_out, False, 6, "out_one", after_out_one, (x_all, gains_all), (rows_f, rows_b, squares)
     )
 
     def spare(at):
         return spare_window(at, tiles, n_col, wide)
 
     n2, hidden, d_glu = glu(normed_two, w_in, w_down, g_all, spare)
-    g_down = outer(g_all, hidden, n_dp, n_col, 512, "outer_down")
+    g_down = outer(g_all, hidden, n_dp, n_col, span, "outer_down")
     d_glu, hidden, g_down = lax.optimization_barrier((d_glu, hidden, g_down))
     sum_down = lax.psum_scatter(g_down, "dp", scatter_dimension=0)
-    g_in = outer(n2, d_glu, n_dp, n_col, 512, "outer_in")
+    g_in = outer(n2, d_glu, n_dp, n_col, span, "outer_in")
     d_glu, g_in = lax.optimization_barrier((d_glu, g_in))
     d_resid, d_out, gain_two = multiply_scatter(
         d_glu,
@@ -1603,46 +1747,54 @@
         after_normed_two,
         (resid, g_all, gains_all),
         (rows_f, rows_b, line),
-        False,
     )
     g_in, sum_down, d_out = lax.optimization_barrier((g_in, sum_down, d_out))
     sum_in = lax.psum_scatter(g_in, "dp", scatter_dimension=0)
 
-    d_out_all, d_rec, gate_sums, small, down = rec_backward(
+    d_out_all, d_rec, gate_grads, small, down = rec_backward(
         d_out,
         w_out,
         (y_branch, state, first, pre_both, conv_low, x_rows),
-        gates_blk,
-        gates_rows,
+        gates,
         soft,
-        conv_w_o,
+        conv_w,
         places,
         sum_down,
         geo,
         n_dp,
     )
-    small = small.at[2].multiply(jax.nn.sigmoid(decay_o))
-    w_x_own = jnp.concatenate(
-        [w_x[:, :bw], lax.dynamic_slice_in_dim(w_x, bw + (col // 2) * LANES, LANES, axis=1)], axis=1
-    )
-    w_back = jnp.concatenate([w_x_own, w_y], axis=1)
+
+    def pick(at):
+        tile = pl.multiple_of(bw + lax.div(at, 2) * LANES, LANES)
+        return ((0, 0, bw), (tile, bw, LANES), (2 * bw, chans, chans))
+
     g_rec = outer_pair(n1, d_rec, d_out_all, branch, n_dp, n_col, chans, "outer_rec")
     g_rec, d_rec = lax.optimization_barrier((g_rec, d_rec))
-    grad_input, gain_one, squares_x = multiply_scatter(
+    grad_rows, gain_one, squares_x, gate_part, small = multiply_scatter(
         d_rec,
-        w_back,
+        w_rec,
         True,
         9,
         "d_normed_one",
         after_normed_one,
         (x_all, d_resid, gains_all),
-        (home, line, squares),
-        True,
+        (rows_b, line, squares),
+        pick=pick,
+        beside=GateReduce(gate_grads, small),
     )
+    grad_input = take_home(grad_rows, n_col)
     g_rec, sum_in, grad_input, hidden = lax.optimization_barrier((g_rec, sum_in, grad_input, hidden))
     sum_rec = lax.psum_scatter(g_rec, "dp", scatter_dimension=0)
-    result, squares_two = multiply_scatter(
-        hidden, w_down, False, 8, "out_two", after_out_two, (resid,), (home, squares), True
+    result_rows, squares_two, gate_planes, into = multiply_scatter(
+        hidden,
+        w_down,
+        False,
+        8,
+        "out_two",
+        after_out_two,
+        (resid,),
+        (rows_b, squares),
+        beside=GateGather(gate_part, sum_in, n_dp),
     )
 
     def windows(got, first):
@@ -1660,16 +1812,16 @@
     lines = small.shape[0]
     gain_sums = jnp.concatenate([gain_one[:1], gain_two[:1]]).reshape(lines, 2 * width // lines)
     stat_block = jnp.pad(square_sums[None, :], ((0, lines - 1), (0, LANES - 4)))
-    mixed = jnp.concatenate([small, gain_sums, stat_block], axis=1)
-    sums, chan_sums, gate_parts, into = sum_everywhere(
-        mixed, chans, gate_sums, sum_in, n_dp, n_col
+    mixed = jnp.concatenate([gain_sums, stat_block], axis=1)
+    sums, chan_sums, gate_parts, result = sum_everywhere(
+        mixed, small, gate_planes, result_rows, n_dp, n_col
     )
-    sum_rec, into = lax.optimization_barrier((sum_rec, into))
-    recs = deal_back(sum_rec, 10, "deal_rec")
     grad_mlp_in = jnp.stack(
         [jnp.concatenate(windows(into[..., j * span : (j + 1) * span], 0), axis=-1) for j in range(2)]
     ).astype(f32)
     grad_mlp_out = jnp.concatenate(windows(down, 0), axis=-1).astype(f32).T
+    sum_rec, grad_mlp_in, grad_mlp_out = lax.optimization_barrier((sum_rec, grad_mlp_in, grad_mlp_out))
+    recs = deal_back(sum_rec, 10, "deal_rec")
     grad_rec_in = jnp.stack(
         [jnp.concatenate(channels_of(recs, j * chans), axis=-1) for j in range(2)]
     ).astype(f32)

time: 810 us -> 782 us (0.965)
  Pallas kernels: 722 us -> 691 us
  waiting for transfers between devices: 4.57 us -> 28.9 us
  local copies, waits for them, and re-layouts: 38.3 us -> 24 us
    reduce_scatter x1, waiting for transfers between devices: 0.02 us -> 16.4 us  [body(): sum_in = lax.psum_scatter(g_in, 'dp', scatter_dimension=0)]
    pallas_call x1, Pallas kernels: 96.1 us -> 82.7 us  [rec_backward(): pl.pallas_call(functools.partial(backward_kernel, geo), out_shape=(jax.Sh...]
    slice x5 -> x0, local copies, waits for them, and re-layouts: 9.66 us -> none  [the longest x2 5.14 us: body(): w_x, w_y = (w_rec[:, :2 * bw], w_rec[:, 2 * bw:])]
    pallas_call x1 -> x2, Pallas kernels: 50.1 us -> 46.5 us  [the longest x1 30.5 us: sum_everywhere(): pl.pallas_call(functools.partial(sums_kernel, n_dp), out_shape=(jax.Shape...]
  transfers between devices with their start and end apart: 3 -> 3, of which waited for: 1 -> 2; matrix products, arithmetic and copies ran while one was open for 3% -> 2% of each run, Pallas kernels for 47% -> 45%
where the time goes in v5:
time: 782 us; the launch traced here: 771 us
  Pallas kernels  691 us (88%)
  waiting for transfers between devices  28.9 us (4%)
  local copies, waits for them, and re-layouts  24 us (3%)
  between operations  14.7 us (2%)
  other arithmetic  12.4 us (2%)
    pallas_call x4, Pallas kernels, multiply_scatter(): pl.pallas_call(functools.partial(scatter_kernel, (n_parts, across, own, w...  220 us
    pallas_call x1, Pallas kernels, rec_forward(): pl.pallas_call(functools.partial(forward_kernel, geo), out_shape=tuple((o...  151 us
    pallas_call x1, Pallas kernels, rec_backward(): pl.pallas_call(functools.partial(backward_kernel, geo), out_shape=(jax.Sh...  82.7 us
    pallas_call x1, Pallas kernels, open_gather(): pl.pallas_call(functools.partial(open_kernel, geo), out_shape=(jax.ShapeD...  65.1 us
    pallas_call x1, Pallas kernels, glu(): pl.pallas_call(functools.partial(glu_kernel, spare), out_shape=(jax.Shape...  49.2 us
    pallas_call x2, Pallas kernels, outer(): pl.pallas_call(functools.partial(outer_one_kernel, n_dp), grid=(n_col, co...  35.4 us
    pallas_call x1, Pallas kernels, sum_everywhere(): pl.pallas_call(functools.partial(sums_kernel, n_dp), out_shape=(jax.Shape...  30.5 us
    pallas_call x1, Pallas kernels, outer_pair(): pl.pallas_call(functools.partial(outer_kernel, n_dp, steps1), grid=(n_col...  21.7 us
  transfers between devices with their start and end apart: 3, of which 2 were waited for; matrix products, arithmetic and copies ran while one was open for 2% of the time, Pallas kernels for 45%

profile of v5, /device:TPU:0, one launch (start us, length us, event | category | flops | bytes accessed | tf_op | source)
XLA Modules:
  0.0 771.1 jit_solution(2070202139012543150)
XLA Ops:
  9.0 1.3 broadcast_in_dim.20.conv_b
  11.7 65.1 %open_gather.1 = (bf16[1536,2560]{1,0:T(8,128)(2,1)}, bf16[2560,896]{1,0:T(8,128)(2,1)}, f32[2,2560]{1,0:T(2,128)}) custom-call(bf16[768,640]{1,0:T(8,128)(2,1)} %tokens.1, bf16[2,640,1280]{2,1,0:T(8,128)(2,1)} %rec_in.1, f32[2,640]{1,0:T(2,128)} %gains.1), custom_call_target="tpu_custom_call" | custom-call | tf_op jit(solution)/shard_map/open_gather/pallas_call | solution.py:340
  77.9 150.5 %rec_forward.1 = (bf16[1536,2560]{1,0:T(8,128)(2,1)}, f32[1544,512]{1,0:T(8,128)}, f32[1536,384]{1,0:T(8,128)}, f32[1536,768]{1,0:T(8,128)}, bf16[1536,512]{1,0:...) custom-call(bf16[1536,2560]{1,0:T(8,128)(2,1)} %get-tuple-element.72, ...), custom_call_target="tpu_custom_call" | custom-call | tf_op jit(solution)/shard_map/rec_forward/pallas_call | solution.py:1238
  228.4 44.7 %out_one.1 = (f32[192,2560]{1,0:T(8,128)}, bf16[192,2560]{1,0:T(8,128)(2,1)}, f32[8,128]{1,0:T(8,128)}) custom-call(bf16[1536,384]{1,0:T(8,128)(2,1)} %get-tuple-element.76.act.right2, bf16[384,2560]{1,0:T(8,128)(2,1)} %get-tuple-element.77.w.w_out, bf16[1536,2560]{1,0:T(8,128)(2,1)} %get-tuple-element.72.x_all.refs_0_.refs_2_, ...), custom_call_target="tpu_custom_call" | custom-call | flops 3019898880 | bytes 41943040 | tf_op jit(solution)/shard_map/out_one/pallas_call | solution.py:667
  273.2 49.2 %glu.1 = (bf16[8,192,2560]{2,1,0:T(8,128)(2,1)}, bf16[1536,1024]{1,0:T(8,128)(2,1)}, bf16[1536,2048]{1,0:T(8,128)(2,1)}) custom-call(bf16[192,2560]{1,0:T(8,128)(2,1)} %get-tuple-element.78.n2, bf16[2,2560,1024]{2,1,0:T(8,128)(2,1)} %get-tuple-element.79.w_in.w, bf16[1024,2560]{1,0:T(8,128)(2,1)} %get-tuple-element.80.w_down.w, ...), custom_call_target="tpu_custom_call" | custom-call | flops 24159191040 | bytes 62914560 | tf_op jit(solution)/shard_map/glu/pallas_call | solution.py:488
  322.4 1.9 copy-done.6
  324.2 11.6 %outer_down.1 = bf16[4,4,160,1024]{3,2,1,0:T(8,128)(2,1)} custom-call(bf16[1536,2560]{1,0:T(8,128)(2,1)} %get-tuple-element.81.g_all.left.refs_1_, bf16[1536,1024]{1,0:T(8,128)(2,1)S(1)} %copy-done.6), custom_call_target="tpu_custom_call" | custom-call | flops 8053063680 | bytes 16252928 | tf_op jit(solution)/shard_map/outer_down/pallas_call | solution.py:1618
  335.9 23.8 %outer_in.1 = bf16[4,4,160,2048]{3,2,1,0:T(8,128)(2,1)} custom-call(bf16[1536,2560]{1,0:T(8,128)(2,1)} %bitcast.108, bf16[1536,2048]{1,0:T(8,128)(2,1)} %get-tuple-element.88.right.act), custom_call_target="tpu_custom_call" | custom-call | flops 16106127360 | bytes 24641536 | tf_op jit(solution)/shard_map/outer_in/pallas_call | solution.py:1618
  359.7 55.7 %d_normed_two.1 = (f32[192,2560]{1,0:T(8,128)}, bf16[192,2560]{1,0:T(8,128)(2,1)}, f32[8,2560]{1,0:T(8,128)}) custom-call(bf16[1536,2048]{1,0:T(8,128)(2,1)} %get-tuple-element.88.right.act, bf16[2,2560,1024]{2,1,0:T(8,128)(2,1)} %get-tuple-element.79.w_in.w, f32[192,2560]{1,0:T(8,128)} %get-tuple-element.89.refs_0_.refs_2_, ...), custom_call_target="tpu_custom_call" | custom-call | flops 16106127360 | bytes 41943040 | tf_op jit(solution)/shard_map/d_normed_two/pallas_call | solution.py:667
  415.4 12.5 %reduce-scatter.4.cloned.1.call-done = bf16[1,4,160,1024]{3,2,1,0:T(8,128)(2,1)} async-done(((bf16[4,4,160,1024]{3,2,1,0:T(8,128)(2,1)}), bf16[1,4,160,1024]{3,2,1,0:T(8,128)(2,1)}) %reduce-scatter.4.cloned.1.call-update) | async-done | bytes 1310736 | tf_op jit(solution)/shard_map/reduce_scatter | solution.py:1738
  428.0 82.7 %rec_backward.1 = (bf16[8,192,2560]{2,1,0:T(8,128)(2,1)}, bf16[1536,768]{1,0:T(8,128)(2,1)}, bf16[4,128,384]{2,1,0:T(8,128)(2,1)}, f32[8,384]{1,0:T(8,128)}, bf16[4,160,1024]{2,1,0:T(8,128)(2,1)}) custom-call(bf16[192,2560]{1,0:T(8,128)(2,1)} %get-tuple-element.91.d_out, bf16[384,2560]{1,0:T(8,128)(2,1)} %get-tuple-element.77.w.w_out, ...), custom_call_target="tpu_custom_call" | custom-call | tf_op jit(solution)/shard_map/rec_backward/pallas_call | solution.py:1545
  510.7 1.8 copy-done.4
  512.5 21.7 %outer_rec.1 = bf16[4,4,160,1152]{3,2,1,0:T(8,128)(2,1)} custom-call(bf16[1536,2560]{1,0:T(8,128)(2,1)} %get-tuple-element.75.left1, bf16[1536,768]{1,0:T(8,128)(2,1)S(1)} %copy-done.4, bf16[1536,2560]{1,0:T(8,128)(2,1)} %bitcast.106, bf16[1536,384]{1,0:T(8,128)(2,1)S(1)} %copy-done.5), custom_call_target="tpu_custom_call" | custom-call | flops 9059696640 | bytes 25165824 | tf_op jit(solution)/shard_map/outer_rec/pallas_call | solution.py:1643
  534.2 49.8 %d_normed_one.1 = (bf16[192,2560]{1,0:T(8,128)(2,1)}, f32[8,2560]{1,0:T(8,128)}, f32[8,128]{1,0:T(8,128)}, bf16[128,384]{1,0:T(8,128)(2,1)}, f32[8,384]{1,0:T(8,128)}) custom-call(bf16[1536,768]{1,0:T(8,128)(2,1)} %get-tuple-element.101.right1.act, bf16[2560,896]{1,0:T(8,128)(2,1)} %get-tuple-element.73.w_rec.w, ...), custom_call_target="tpu_custom_call" | custom-call | flops 6039797760 | bytes 41943040 | tf_op jit(solution)/shard_map/d_normed_one/pallas_call | solution.py:667
  584.0 16.0 %take_home.1 = bf16[768,640]{1,0:T(8,128)(2,1)} custom-call(bf16[192,2560]{1,0:T(8,128)(2,1)} %get-tuple-element.111.rows), custom_call_target="tpu_custom_call" | custom-call | tf_op jit(solution)/shard_map/take_home/pallas_call | solution.py:718
  600.0 16.4 %reduce-scatter.6.cloned.1.call-done = bf16[1,4,160,2048]{3,2,1,0:T(8,128)(2,1)} async-done(((bf16[4,4,160,2048]{3,2,1,0:T(8,128)(2,1)}), bf16[1,4,160,2048]{3,2,1,0:T(8,128)(2,1)}) %reduce-scatter.6.cloned.1.call-update) | async-done | bytes 2621456 | tf_op jit(solution)/shard_map/reduce_scatter | solution.py:1752
  621.0 1.6 convert_bitcast_fusion
  622.6 69.5 %out_two.1 = (bf16[192,2560]{1,0:T(8,128)(2,1)}, f32[8,128]{1,0:T(8,128)}, bf16[4,128,384]{2,1,0:T(8,128)(2,1)}, bf16[4,160,2048]{2,1,0:T(8,128)(2,1)}) custom-call(bf16[1536,1024]{1,0:T(8,128)(2,1)} %get-tuple-element.113.right.act, bf16[1024,2560]{1,0:T(8,128)(2,1)} %get-tuple-element.80.w_down.w, bf16[128,384]{1,0:T(8,128)(2,1)} %get-tuple-element.114.refs_0_, ...), custom_call_target="tpu_custom_call" | custom-call | flops 8053063680 | bytes 41943040 | tf_op jit(solution)/shard_map/out_two/pallas_call | solution.py:667
  693.3 2.7 maximum_bitcast_fusion.3
  698.2 30.5 %small_sums.1 = (f32[8,768]{1,0:T(8,128)S(1)}, f32[4,8,384]{2,1,0:T(8,128)S(1)}, bf16[4,4,128,384]{3,2,1,0:T(8,128)(2,1)S(1)}, bf16[768,640]{1,0:T(8,128)(2,1)S(1)}) custom-call(f32[8,768]{1,0:T(8,128)S(1)} %select_maximum_fusion.mixed, f32[8,384]{1,0:T(8,128)S(1)} %copy-done.3, bf16[4,128,384]{2,1,0:T(8,128)(2,1)S(1)} %copy-done.2, ...), custom_call_target="tpu_custom_call" | custom-call | tf_op jit(solution)/shard_map/small_sums/pallas_call | solution.py:972
  730.0 1.9 slice_bitcast_fusion.19
  735.4 2.6 maximum_convert_fusion
  738.0 1.4 copy-done
  739.4 20.2 %deal_rec.1 = bf16[4,160,1152]{2,1,0:T(8,128)(2,1)S(1)} custom-call(bf16[4,160,1152]{2,1,0:T(8,128)(2,1)S(1)} %bitcast.101), custom_call_target="tpu_custom_call" | custom-call | tf_op jit(solution)/shard_map/deal_rec/pallas_call | solution.py:884
  (85 shorter events, 21.5 us)
Async XLA Ops:
  7.2 420.7 %reduce-scatter.4.cloned.1.call-start = ((), (), s32[]{:S(2)}) async-start(), calls=%async_computation.3 | async-start | bytes 6553600 | tf_op jit(solution)/shard_map/reduce_scatter | solution.py:1738
  322.4 1.9 copy-start.6
  335.8 280.6 %reduce-scatter.6.cloned.1.call-start = ((), (), s32[]{:S(2)}) async-start(), calls=%async_computation.4 | async-start | bytes 13107200 | tf_op jit(solution)/shard_map/reduce_scatter | solution.py:1752
  427.9 310.1 %reduce-scatter.8.cloned.1.call-start = ((), (), s32[]{:S(2)}) async-start(), calls=%async_computation.5 | async-start | bytes 7372800 | tf_op jit(solution)/shard_map/reduce_scatter | solution.py:1787
  428.0 82.7 %copy-start.5 = (bf16[1536,384]{1,0:T(8,128)(2,1)S(1)}, bf16[1536,384]{1,0:T(8,128)(2,1)}, u32[]{:S(2)}) copy-start(bf16[1536,384]{1,0:T(8,128)(2,1)} %get-tuple-element.76.act.right2) | copy-start | bytes 3538948
  510.6 1.8 copy-start.4
  616.4 4.4 copy-start.8
  622.6 73.4 %copy-start.3 = (f32[8,384]{1,0:T(8,128)S(1)}, f32[8,384]{1,0:T(8,128)}, u32[]{:S(2)}) copy-start(f32[8,384]{1,0:T(8,128)} %get-tuple-element.117.small) | copy-start | bytes 36868
  696.0 1.2 copy-start.1
  697.2 1.0 copy-start.2
  733.7 1.5 copy-start.9
  738.0 1.4 copy-start
  760.9 2.2 copy-start.7
Sparse Core Ops, SparseCore 0:
  335.9 91.8 reduce-scatter.3
  430.2 186.1 reduce-scatter.5
  618.7 113.6 reduce-scatter.7

commit v6 on v5

--- a/solution.py
+++ b/solution.py
@@ -904,14 +904,20 @@
 
 def sums_kernel(
     n_dp,
-    mixed,
+    gain_one,
+    gain_two,
+    squares_x,
+    squares_one,
+    squares_two,
     small,
     gates,
     rows,
-    sums_out,
+    gains_out,
+    squares_out,
     chans_out,
     gates_out,
     home,
+    mixed,
     got,
     total,
     shared,
@@ -925,6 +931,14 @@
     far = [f"d{d}" for d in range(1, n_dp)]
     place.meet(list(PLANE) + far)
     copies = Copies(place, send, recv)
+    n_col, part = ch.shape[0], gains_out.shape[1]
+    mixed[...] = jnp.zeros_like(mixed)
+    for c in range(n_col):
+        mixed[c : c + 1, :part] = gain_one[0:1, c * part : (c + 1) * part]
+        mixed[n_col + c : n_col + c + 1, :part] = gain_two[0:1, c * part : (c + 1) * part]
+    mixed[0:1, part:] = squares_x[0:1, :]
+    mixed[1:3, part:] = squares_one[0:2, :]
+    mixed[3:4, part:] = squares_two[0:1, :]
     planes = [copies.start(mixed, got.at[i], name) for i, name in enumerate(far)]
     col = place.col
     ch[col] = small[...]
@@ -959,30 +973,37 @@
     copies.land(*others)
     for i in range(len(PLANE)):
         value = value + shared[i]
-    sums_out[...] = value
+    got[0] = value
+    gains_out[0:1, :] = got[0, pl.ds(col, 1), :part]
+    gains_out[1:2, :] = got[0, pl.ds(n_col + col, 1), :part]
+    squares_out[...] = value[:, part:]
     copies.finish()
     chans_out[...] = ch[...]
     gates_out[...] = gv[...]
     stay_home.finish()
 
 
-def sum_everywhere(mixed, small, gates, rows_low, n_dp, n_col):
+def sum_everywhere(gain_one, gain_two, squares, small, gates, rows_low, n_dp, n_col):
     count = n_dp + 22
+    part = rows_low.shape[1] // n_col
+    mixed = (2 * n_col, part + LANES)
     home = (n_col * rows_low.shape[0], rows_low.shape[1] // n_col)
     return pl.pallas_call(
         functools.partial(sums_kernel, n_dp),
         out_shape=(
-            jax.ShapeDtypeStruct(mixed.shape, f32),
+            jax.ShapeDtypeStruct((2, part), f32),
+            jax.ShapeDtypeStruct((2 * n_col, LANES), f32),
             jax.ShapeDtypeStruct((n_col,) + small.shape, f32),
             jax.ShapeDtypeStruct((n_col,) + gates.shape, low),
             jax.ShapeDtypeStruct(home, low),
         ),
-        in_specs=[in_vmem] * 3 + [anywhere],
-        out_specs=(in_vmem,) * 3 + (anywhere,),
+        in_specs=[in_vmem] * 7 + [anywhere],
+        out_specs=(in_vmem,) * 4 + (anywhere,),
         scratch_shapes=[
-            pltpu.VMEM((n_dp - 1,) + mixed.shape, f32),
-            pltpu.VMEM(mixed.shape, f32),
-            pltpu.VMEM((len(PLANE),) + mixed.shape, f32),
+            pltpu.VMEM(mixed, f32),
+            pltpu.VMEM((n_dp - 1,) + mixed, f32),
+            pltpu.VMEM(mixed, f32),
+            pltpu.VMEM((len(PLANE),) + mixed, f32),
             pltpu.VMEM((n_col,) + small.shape, f32),
             pltpu.VMEM((n_col,) + gates.shape, low),
             pltpu.SemaphoreType.DMA((count,)),
@@ -994,7 +1015,7 @@
             collective_id=5, has_side_effects=True, vmem_limit_bytes=24 * MIB
         ),
         name="small_sums",
-    )(mixed, small, gates, rows_low)
+    )(gain_one, gain_two, *squares, small, gates, rows_low)
 
 
 def own_lanes(place, geo):
@@ -1808,13 +1829,15 @@
             got[c][..., first + bw : first + chans] for c in range(0, n_col, 2)
         ]
 
-    square_sums = jnp.stack([squares_x[0, 0], squares_one[0, 0], squares_one[1, 0], squares_two[0, 0]])
-    lines = small.shape[0]
-    gain_sums = jnp.concatenate([gain_one[:1], gain_two[:1]]).reshape(lines, 2 * width // lines)
-    stat_block = jnp.pad(square_sums[None, :], ((0, lines - 1), (0, LANES - 4)))
-    mixed = jnp.concatenate([gain_sums, stat_block], axis=1)
-    sums, chan_sums, gate_parts, result = sum_everywhere(
-        mixed, small, gate_planes, result_rows, n_dp, n_col
+    grad_gains, square_sums, chan_sums, gate_parts, result = sum_everywhere(
+        gain_one,
+        gain_two,
+        (squares_x, squares_one, squares_two),
+        small,
+        gate_planes,
+        result_rows,
+        n_dp,
+        n_col,
     )
     grad_mlp_in = jnp.stack(
         [jnp.concatenate(windows(into[..., j * span : (j + 1) * span], 0), axis=-1) for j in range(2)]
@@ -1827,9 +1850,7 @@
     ).astype(f32)
     grad_rec_out = jnp.concatenate(channels_of(recs, 2 * chans), axis=-1).astype(f32).T
     mine = jnp.concatenate(channels_of(chan_sums, 0), axis=-1)
-    gain_rows = sums[:, : 2 * width // lines].reshape(2, width)
-    grad_gains = lax.dynamic_slice_in_dim(gain_rows, col * part, part, axis=1)
-    stats = jnp.sqrt(sums[0, 2 * width // lines :][:4] / (n_dp * group * width))
+    stats = jnp.sqrt(square_sums[:4, 0] / (n_dp * group * width))
     gate_parts = gate_parts.reshape(n_col, 2, bw, chans).astype(f32)
     five = jnp.concatenate([gate_parts[c, :, :, bw:] for c in range(0, n_col, 2)], axis=-1)
     grad_gates = jnp.stack([gate_parts[c, :, :, :bw] for c in range(n_col)] + [five], axis=1)

time: 782 us -> 777 us (level)
  transfers between devices with their start and end apart: 3 -> 3, of which waited for: 2 -> 2; matrix products, arithmetic and copies ran while one was open for 2% -> 1% of each run, Pallas kernels for 45% -> 46%
where the time goes in v6:
time: 777 us; the launch traced here: 765 us
  Pallas kernels  691 us (89%)
  waiting for transfers between devices  28.9 us (4%)
  local copies, waits for them, and re-layouts  20.9 us (3%)
  between operations  14.7 us (2%)
  other arithmetic  9.82 us (1%)
    pallas_call x4, Pallas kernels, multiply_scatter(): pl.pallas_call(functools.partial(scatter_kernel, (n_parts, across, own, w...  220 us
    pallas_call x1, Pallas kernels, rec_forward(): pl.pallas_call(functools.partial(forward_kernel, geo), out_shape=tuple((o...  151 us
    pallas_call x1, Pallas kernels, rec_backward(): pl.pallas_call(functools.partial(backward_kernel, geo), out_shape=(jax.Sh...  82.7 us
    pallas_call x1, Pallas kernels, open_gather(): pl.pallas_call(functools.partial(open_kernel, geo), out_shape=(jax.ShapeD...  65.1 us
    pallas_call x1, Pallas kernels, glu(): pl.pallas_call(functools.partial(glu_kernel, spare), out_shape=(jax.Shape...  49.2 us
    pallas_call x2, Pallas kernels, outer(): pl.pallas_call(functools.partial(outer_one_kernel, n_dp), grid=(n_col, co...  35.4 us
    pallas_call x1, Pallas kernels, sum_everywhere(): pl.pallas_call(functools.partial(sums_kernel, n_dp), out_shape=(jax.Shape...  30.5 us
    pallas_call x1, Pallas kernels, outer_pair(): pl.pallas_call(functools.partial(outer_kernel, n_dp, steps1), grid=(n_col...  21.7 us
  transfers between devices with their start and end apart: 3, of which 2 were waited for; matrix products, arithmetic and copies ran while one was open for 1% of the time, Pallas kernels for 46%

profile of v6, /device:TPU:0, one launch (start us, length us, event | category | flops | bytes accessed | tf_op | source)
XLA Modules:
  0.0 765.4 jit_solution(4777238731018359575)
XLA Ops:
  9.0 1.3 broadcast_in_dim.18.conv_b
  11.7 65.1 %open_gather.1 = (bf16[1536,2560]{1,0:T(8,128)(2,1)}, bf16[2560,896]{1,0:T(8,128)(2,1)}, f32[2,2560]{1,0:T(2,128)}) custom-call(bf16[768,640]{1,0:T(8,128)(2,1)} %tokens.1, bf16[2,640,1280]{2,1,0:T(8,128)(2,1)} %rec_in.1, f32[2,640]{1,0:T(2,128)} %gains.1), custom_call_target="tpu_custom_call" | custom-call | tf_op jit(solution)/shard_map/open_gather/pallas_call | solution.py:340
  77.9 150.5 %rec_forward.1 = (bf16[1536,2560]{1,0:T(8,128)(2,1)}, f32[1544,512]{1,0:T(8,128)}, f32[1536,384]{1,0:T(8,128)}, f32[1536,768]{1,0:T(8,128)}, bf16[1536,512]{1,0:...) custom-call(bf16[1536,2560]{1,0:T(8,128)(2,1)} %get-tuple-element.73, ...), custom_call_target="tpu_custom_call" | custom-call | tf_op jit(solution)/shard_map/rec_forward/pallas_call | solution.py:1259
  228.4 44.7 %out_one.1 = (f32[192,2560]{1,0:T(8,128)}, bf16[192,2560]{1,0:T(8,128)(2,1)}, f32[8,128]{1,0:T(8,128)}) custom-call(bf16[1536,384]{1,0:T(8,128)(2,1)} %get-tuple-element.77.act.right2, bf16[384,2560]{1,0:T(8,128)(2,1)} %get-tuple-element.78.w.w_out, bf16[1536,2560]{1,0:T(8,128)(2,1)} %get-tuple-element.73.x_all.refs_0_.refs_2_, ...), custom_call_target="tpu_custom_call" | custom-call | flops 3019898880 | bytes 41943040 | tf_op jit(solution)/shard_map/out_one/pallas_call | solution.py:667
  273.2 49.2 %glu.1 = (bf16[8,192,2560]{2,1,0:T(8,128)(2,1)}, bf16[1536,1024]{1,0:T(8,128)(2,1)}, bf16[1536,2048]{1,0:T(8,128)(2,1)}) custom-call(bf16[192,2560]{1,0:T(8,128)(2,1)} %get-tuple-element.79.n2, bf16[2,2560,1024]{2,1,0:T(8,128)(2,1)} %get-tuple-element.80.w_in.w, bf16[1024,2560]{1,0:T(8,128)(2,1)} %get-tuple-element.81.w_down.w, ...), custom_call_target="tpu_custom_call" | custom-call | flops 24159191040 | bytes 62914560 | tf_op jit(solution)/shard_map/glu/pallas_call | solution.py:488
  322.4 1.9 copy-done.11
  324.3 11.5 %outer_down.1 = bf16[4,4,160,1024]{3,2,1,0:T(8,128)(2,1)} custom-call(bf16[1536,2560]{1,0:T(8,128)(2,1)} %get-tuple-element.82.g_all.left.refs_1_, bf16[1536,1024]{1,0:T(8,128)(2,1)S(1)} %copy-done.11), custom_call_target="tpu_custom_call" | custom-call | flops 8053063680 | bytes 16252928 | tf_op jit(solution)/shard_map/outer_down/pallas_call | solution.py:1639
  335.9 23.9 %outer_in.1 = bf16[4,4,160,2048]{3,2,1,0:T(8,128)(2,1)} custom-call(bf16[1536,2560]{1,0:T(8,128)(2,1)} %bitcast.100, bf16[1536,2048]{1,0:T(8,128)(2,1)} %get-tuple-element.89.right.act), custom_call_target="tpu_custom_call" | custom-call | flops 16106127360 | bytes 24641536 | tf_op jit(solution)/shard_map/outer_in/pallas_call | solution.py:1639
  359.7 55.7 %d_normed_two.1 = (f32[192,2560]{1,0:T(8,128)}, bf16[192,2560]{1,0:T(8,128)(2,1)}, f32[8,2560]{1,0:T(8,128)}) custom-call(bf16[1536,2048]{1,0:T(8,128)(2,1)} %get-tuple-element.89.right.act, bf16[2,2560,1024]{2,1,0:T(8,128)(2,1)} %get-tuple-element.80.w_in.w, f32[192,2560]{1,0:T(8,128)} %get-tuple-element.90.refs_0_.refs_2_, ...), custom_call_target="tpu_custom_call" | custom-call | flops 16106127360 | bytes 41943040 | tf_op jit(solution)/shard_map/d_normed_two/pallas_call | solution.py:667
  415.4 12.4 %reduce-scatter.4.cloned.1.call-done = bf16[1,4,160,1024]{3,2,1,0:T(8,128)(2,1)} async-done(((bf16[4,4,160,1024]{3,2,1,0:T(8,128)(2,1)}), bf16[1,4,160,1024]{3,2,1,0:T(8,128)(2,1)}) %reduce-scatter.4.cloned.1.call-update) | async-done | bytes 1310736 | tf_op jit(solution)/shard_map/reduce_scatter | solution.py:1759
  427.9 82.7 %rec_backward.1 = (bf16[8,192,2560]{2,1,0:T(8,128)(2,1)}, bf16[1536,768]{1,0:T(8,128)(2,1)}, bf16[4,128,384]{2,1,0:T(8,128)(2,1)}, f32[8,384]{1,0:T(8,128)}, bf16[4,160,1024]{2,1,0:T(8,128)(2,1)}) custom-call(bf16[192,2560]{1,0:T(8,128)(2,1)} %get-tuple-element.92.d_out, bf16[384,2560]{1,0:T(8,128)(2,1)} %get-tuple-element.78.w.w_out, ...), custom_call_target="tpu_custom_call" | custom-call | tf_op jit(solution)/shard_map/rec_backward/pallas_call | solution.py:1566
  510.6 1.8 copy-done.9
  512.4 21.7 %outer_rec.1 = bf16[4,4,160,1152]{3,2,1,0:T(8,128)(2,1)} custom-call(bf16[1536,2560]{1,0:T(8,128)(2,1)} %get-tuple-element.76.left1, bf16[1536,768]{1,0:T(8,128)(2,1)S(1)} %copy-done.9, bf16[1536,2560]{1,0:T(8,128)(2,1)} %bitcast.98, bf16[1536,384]{1,0:T(8,128)(2,1)S(1)} %copy-done.10), custom_call_target="tpu_custom_call" | custom-call | flops 9059696640 | bytes 25165824 | tf_op jit(solution)/shard_map/outer_rec/pallas_call | solution.py:1664
  534.2 49.8 %d_normed_one.1 = (bf16[192,2560]{1,0:T(8,128)(2,1)}, f32[8,2560]{1,0:T(8,128)}, f32[8,128]{1,0:T(8,128)}, bf16[128,384]{1,0:T(8,128)(2,1)}, f32[8,384]{1,0:T(8,128)}) custom-call(bf16[1536,768]{1,0:T(8,128)(2,1)} %get-tuple-element.102.right1.act, bf16[2560,896]{1,0:T(8,128)(2,1)} %get-tuple-element.74.w_rec.w, ...), custom_call_target="tpu_custom_call" | custom-call | flops 6039797760 | bytes 41943040 | tf_op jit(solution)/shard_map/d_normed_one/pallas_call | solution.py:667
  584.0 16.0 %take_home.1 = bf16[768,640]{1,0:T(8,128)(2,1)} custom-call(bf16[192,2560]{1,0:T(8,128)(2,1)} %get-tuple-element.112.rows), custom_call_target="tpu_custom_call" | custom-call | tf_op jit(solution)/shard_map/take_home/pallas_call | solution.py:718
  600.0 16.4 %reduce-scatter.6.cloned.1.call-done = bf16[1,4,160,2048]{3,2,1,0:T(8,128)(2,1)} async-done(((bf16[4,4,160,2048]{3,2,1,0:T(8,128)(2,1)}), bf16[1,4,160,2048]{3,2,1,0:T(8,128)(2,1)}) %reduce-scatter.6.cloned.1.call-update) | async-done | bytes 2621456 | tf_op jit(solution)/shard_map/reduce_scatter | solution.py:1773
  617.9 1.6 convert_bitcast_fusion
  619.5 69.6 %out_two.1 = (bf16[192,2560]{1,0:T(8,128)(2,1)}, f32[8,128]{1,0:T(8,128)}, bf16[4,128,384]{2,1,0:T(8,128)(2,1)}, bf16[4,160,2048]{2,1,0:T(8,128)(2,1)}) custom-call(bf16[1536,1024]{1,0:T(8,128)(2,1)} %get-tuple-element.114.right.act, bf16[1024,2560]{1,0:T(8,128)(2,1)} %get-tuple-element.81.w_down.w, bf16[128,384]{1,0:T(8,128)(2,1)} %get-tuple-element.115.refs_0_, ...), custom_call_target="tpu_custom_call" | custom-call | flops 8053063680 | bytes 41943040 | tf_op jit(solution)/shard_map/out_two/pallas_call | solution.py:667
  692.0 30.5 %small_sums.1 = (f32[2,640]{1,0:T(2,128)S(1)}, f32[8,128]{1,0:T(8,128)S(1)}, f32[4,8,384]{2,1,0:T(8,128)S(1)}, bf16[4,4,128,384]{3,2,1,0:T(8,128)(2,1)S(1)}, bf16[768,640]{1,0:T(8,128)(2,1)S(1)}) custom-call(f32[8,2560]{1,0:T(8,128)S(1)} %copy-done.4, f32[8,2560]{1,0:T(8,128)S(1)} %copy-done.3, f32[8,128]{1,0:T(8,128)S(1)} %copy-done.7, ...), custom_call_target="tpu_custom_call" | custom-call | tf_op jit(solution)/shard_map/small_sums/pallas_call | solution.py:991
  723.8 1.9 slice_bitcast_fusion.19
  727.6 1.5 copy-done.14
  729.3 2.6 maximum_convert_fusion
  731.9 1.4 copy-done
  733.2 20.2 %deal_rec.1 = bf16[4,160,1152]{2,1,0:T(8,128)(2,1)S(1)} custom-call(bf16[4,160,1152]{2,1,0:T(8,128)(2,1)S(1)} %bitcast.93), custom_call_target="tpu_custom_call" | custom-call | tf_op jit(solution)/shard_map/deal_rec/pallas_call | solution.py:884
  (84 shorter events, 17.0 us)
Async XLA Ops:
  7.2 420.7 %reduce-scatter.4.cloned.1.call-start = ((), (), s32[]{:S(2)}) async-start(), calls=%async_computation.3 | async-start | bytes 6553600 | tf_op jit(solution)/shard_map/reduce_scatter | solution.py:1759
  322.4 1.9 copy-start.11
  335.8 280.6 %reduce-scatter.6.cloned.1.call-start = ((), (), s32[]{:S(2)}) async-start(), calls=%async_computation.4 | async-start | bytes 13107200 | tf_op jit(solution)/shard_map/reduce_scatter | solution.py:1773
  427.9 304.0 %reduce-scatter.8.cloned.1.call-start = ((), (), s32[]{:S(2)}) async-start(), calls=%async_computation.5 | async-start | bytes 7372800 | tf_op jit(solution)/shard_map/reduce_scatter | solution.py:1808
  427.9 82.7 %copy-start.10 = (bf16[1536,384]{1,0:T(8,128)(2,1)S(1)}, bf16[1536,384]{1,0:T(8,128)(2,1)}, u32[]{:S(2)}) copy-start(bf16[1536,384]{1,0:T(8,128)(2,1)} %get-tuple-element.77.act.right2) | copy-start | bytes 3538948
  510.6 1.8 copy-start.9
  616.4 1.3 copy-start.13
  619.5 69.6 %copy-start.3 = (f32[8,2560]{1,0:T(8,128)S(1)}, f32[8,2560]{1,0:T(8,128)}, u32[]{:S(2)}) copy-start(f32[8,2560]{1,0:T(8,128)} %get-tuple-element.107.gain_two) | copy-start | bytes 245764
  619.5 69.6 %copy-start.4 = (f32[8,2560]{1,0:T(8,128)S(1)}, f32[8,2560]{1,0:T(8,128)}, u32[]{:S(2)}) copy-start(f32[8,2560]{1,0:T(8,128)} %get-tuple-element.106.gain_one) | copy-start | bytes 245764
  619.5 69.6 %copy-start.5 = (f32[8,384]{1,0:T(8,128)S(1)}, f32[8,384]{1,0:T(8,128)}, u32[]{:S(2)}) copy-start(f32[8,384]{1,0:T(8,128)} %get-tuple-element.118.small) | copy-start | bytes 36868
  619.5 69.6 %copy-start.6 = (f32[8,128]{1,0:T(8,128)S(1)}, f32[8,128]{1,0:T(8,128)}, u32[]{:S(2)}) copy-start(f32[8,128]{1,0:T(8,128)} %get-tuple-element.109.squares_one) | copy-start | bytes 12292
  619.5 69.6 %copy-start.7 = (f32[8,128]{1,0:T(8,128)S(1)}, f32[8,128]{1,0:T(8,128)}, u32[]{:S(2)}) copy-start(f32[8,128]{1,0:T(8,128)} %get-tuple-element.108.squares_x) | copy-start | bytes 12292
  689.1 1.2 copy-start.1
  690.3 1.0 copy-start.2
  691.3 0.7 copy-start.8
  727.6 1.5 copy-start.14
  731.9 1.4 copy-start
  754.7 2.2 copy-start.12
Sparse Core Ops, SparseCore 0:
  335.9 91.8 reduce-scatter.3
  430.2 186.1 reduce-scatter.5
  618.7 112.6 reduce-scatter.7

commit v7 on v6

--- a/solution.py
+++ b/solution.py
@@ -386,7 +386,7 @@
 
 
 def glu_kernel(
-    spare, n2, w_in, w_down, g_all, n2_all, hidden, d_glu, buf, wi, wd, g, hid, dgl, send, recv, local
+    spare, n2, w_in, w_down, g_all, n2_all, hidden, d_glu, buf, wi, wd, g, hid, dgl, send, recv, local, out_sems
 ):
     place = Place()
     place.meet(("x", "y", "core"))
@@ -472,13 +472,20 @@
     work(near, half, half, n_steps // 2, n_steps)
     copies.land(corner)
     out_n2 = copies.keep(buf, n2_all, local.at[0])
+    written = [out_n2]
+
+    def write(slots):
+        for slot in slots:
+            rows = pl.ds(pl.multiple_of(slot * own, ROWS), own)
+            for src, dst in ((hid, hidden), (dgl, d_glu)):
+                written.append(copies.keep(src.at[rows, :], dst.at[rows, :], out_sems.at[len(written) - 1]))
+
+    write(both_cores(place.col) + near)
     work(both_cores(place.chip(3)), 0, own, 0, n_steps)
-    out_h = copies.keep(hid, hidden, local.at[1])
-    out_d = copies.keep(dgl, d_glu, local.at[2])
+    write(both_cores(place.chip(3)))
     copies.finish()
-    out_n2.wait()
-    out_h.wait()
-    out_d.wait()
+    for copy in written:
+        copy.wait()
 
 
 def glu(n2, w_in, w_down, g_all, spare):
@@ -504,6 +511,7 @@
             pltpu.SemaphoreType.DMA((12,)),
             pltpu.SemaphoreType.DMA((12,)),
             pltpu.SemaphoreType.DMA((12 + 2 * (span // 256),)),
+            pltpu.SemaphoreType.DMA((2 * (group // own),)),
         ],
         compiler_params=pltpu.CompilerParams(
             collective_id=3, has_side_effects=True, vmem_limit_bytes=58 * MIB

time: 777 us -> 775 us (level)
  no operation moved by 1% of the time
where the time goes in v7:
time: 775 us; the launch traced here: 764 us
  Pallas kernels  690 us (89%)
  waiting for transfers between devices  28.9 us (4%)
  local copies, waits for them, and re-layouts  20.9 us (3%)
  between operations  14.7 us (2%)
  other arithmetic  9.82 us (1%)
    pallas_call x4, Pallas kernels, multiply_scatter(): pl.pallas_call(functools.partial(scatter_kernel, (n_parts, across, own, w...  220 us
    pallas_call x1, Pallas kernels, rec_forward(): pl.pallas_call(functools.partial(forward_kernel, geo), out_shape=tuple((o...  151 us
    pallas_call x1, Pallas kernels, rec_backward(): pl.pallas_call(functools.partial(backward_kernel, geo), out_shape=(jax.Sh...  82.7 us
    pallas_call x1, Pallas kernels, open_gather(): pl.pallas_call(functools.partial(open_kernel, geo), out_shape=(jax.ShapeD...  65.1 us
    pallas_call x1, Pallas kernels, glu(): pl.pallas_call(functools.partial(glu_kernel, spare), out_shape=(jax.Shape...  48 us
    pallas_call x2, Pallas kernels, outer(): pl.pallas_call(functools.partial(outer_one_kernel, n_dp), grid=(n_col, co...  35.4 us
    pallas_call x1, Pallas kernels, sum_everywhere(): pl.pallas_call(functools.partial(sums_kernel, n_dp), out_shape=(jax.Shape...  30.5 us
    pallas_call x1, Pallas kernels, outer_pair(): pl.pallas_call(functools.partial(outer_kernel, n_dp, steps1), grid=(n_col...  21.7 us
  transfers between devices with their start and end apart: 3, of which 2 were waited for; matrix products, arithmetic and copies ran while one was open for 1% of the time, Pallas kernels for 46%

profile of v7, /device:TPU:0, one launch (start us, length us, event | category | flops | bytes accessed | tf_op | source)
XLA Modules:
  0.0 764.2 jit_solution(12937965846967903350)
XLA Ops:
  9.0 1.3 broadcast_in_dim.18.conv_b
  11.7 65.1 %open_gather.1 = (bf16[1536,2560]{1,0:T(8,128)(2,1)}, bf16[2560,896]{1,0:T(8,128)(2,1)}, f32[2,2560]{1,0:T(2,128)}) custom-call(bf16[768,640]{1,0:T(8,128)(2,1)} %tokens.1, bf16[2,640,1280]{2,1,0:T(8,128)(2,1)} %rec_in.1, f32[2,640]{1,0:T(2,128)} %gains.1), custom_call_target="tpu_custom_call" | custom-call | tf_op jit(solution)/shard_map/open_gather/pallas_call | solution.py:340
  77.9 150.5 %rec_forward.1 = (bf16[1536,2560]{1,0:T(8,128)(2,1)}, f32[1544,512]{1,0:T(8,128)}, f32[1536,384]{1,0:T(8,128)}, f32[1536,768]{1,0:T(8,128)}, bf16[1536,512]{1,0:...) custom-call(bf16[1536,2560]{1,0:T(8,128)(2,1)} %get-tuple-element.73, ...), custom_call_target="tpu_custom_call" | custom-call | tf_op jit(solution)/shard_map/rec_forward/pallas_call | solution.py:1267
  228.4 44.7 %out_one.1 = (f32[192,2560]{1,0:T(8,128)}, bf16[192,2560]{1,0:T(8,128)(2,1)}, f32[8,128]{1,0:T(8,128)}) custom-call(bf16[1536,384]{1,0:T(8,128)(2,1)} %get-tuple-element.77.act.right2, bf16[384,2560]{1,0:T(8,128)(2,1)} %get-tuple-element.78.w.w_out, bf16[1536,2560]{1,0:T(8,128)(2,1)} %get-tuple-element.73.x_all.refs_0_.refs_2_, ...), custom_call_target="tpu_custom_call" | custom-call | flops 3019898880 | bytes 41943040 | tf_op jit(solution)/shard_map/out_one/pallas_call | solution.py:675
  273.2 48.0 %glu.1 = (bf16[8,192,2560]{2,1,0:T(8,128)(2,1)}, bf16[1536,1024]{1,0:T(8,128)(2,1)}, bf16[1536,2048]{1,0:T(8,128)(2,1)}) custom-call(bf16[192,2560]{1,0:T(8,128)(2,1)} %get-tuple-element.79.n2, bf16[2,2560,1024]{2,1,0:T(8,128)(2,1)} %get-tuple-element.80.w_in.w, bf16[1024,2560]{1,0:T(8,128)(2,1)} %get-tuple-element.81.w_down.w, ...), custom_call_target="tpu_custom_call" | custom-call | flops 24159191040 | bytes 62914560 | tf_op jit(solution)/shard_map/glu/pallas_call | solution.py:495
  321.3 1.9 copy-done.11
  323.1 11.5 %outer_down.1 = bf16[4,4,160,1024]{3,2,1,0:T(8,128)(2,1)} custom-call(bf16[1536,2560]{1,0:T(8,128)(2,1)} %get-tuple-element.82.g_all.left.refs_1_, bf16[1536,1024]{1,0:T(8,128)(2,1)S(1)} %copy-done.11), custom_call_target="tpu_custom_call" | custom-call | flops 8053063680 | bytes 16252928 | tf_op jit(solution)/shard_map/outer_down/pallas_call | solution.py:1647
  334.7 23.9 %outer_in.1 = bf16[4,4,160,2048]{3,2,1,0:T(8,128)(2,1)} custom-call(bf16[1536,2560]{1,0:T(8,128)(2,1)} %bitcast.100, bf16[1536,2048]{1,0:T(8,128)(2,1)} %get-tuple-element.89.right.act), custom_call_target="tpu_custom_call" | custom-call | flops 16106127360 | bytes 24641536 | tf_op jit(solution)/shard_map/outer_in/pallas_call | solution.py:1647
  358.6 55.7 %d_normed_two.1 = (f32[192,2560]{1,0:T(8,128)}, bf16[192,2560]{1,0:T(8,128)(2,1)}, f32[8,2560]{1,0:T(8,128)}) custom-call(bf16[1536,2048]{1,0:T(8,128)(2,1)} %get-tuple-element.89.right.act, bf16[2,2560,1024]{2,1,0:T(8,128)(2,1)} %get-tuple-element.80.w_in.w, f32[192,2560]{1,0:T(8,128)} %get-tuple-element.90.refs_0_.refs_2_, ...), custom_call_target="tpu_custom_call" | custom-call | flops 16106127360 | bytes 41943040 | tf_op jit(solution)/shard_map/d_normed_two/pallas_call | solution.py:675
  414.3 12.4 %reduce-scatter.4.cloned.1.call-done = bf16[1,4,160,1024]{3,2,1,0:T(8,128)(2,1)} async-done(((bf16[4,4,160,1024]{3,2,1,0:T(8,128)(2,1)}), bf16[1,4,160,1024]{3,2,1,0:T(8,128)(2,1)}) %reduce-scatter.4.cloned.1.call-update) | async-done | bytes 1310736 | tf_op jit(solution)/shard_map/reduce_scatter | solution.py:1767
  426.8 82.7 %rec_backward.1 = (bf16[8,192,2560]{2,1,0:T(8,128)(2,1)}, bf16[1536,768]{1,0:T(8,128)(2,1)}, bf16[4,128,384]{2,1,0:T(8,128)(2,1)}, f32[8,384]{1,0:T(8,128)}, bf16[4,160,1024]{2,1,0:T(8,128)(2,1)}) custom-call(bf16[192,2560]{1,0:T(8,128)(2,1)} %get-tuple-element.92.d_out, bf16[384,2560]{1,0:T(8,128)(2,1)} %get-tuple-element.78.w.w_out, ...), custom_call_target="tpu_custom_call" | custom-call | tf_op jit(solution)/shard_map/rec_backward/pallas_call | solution.py:1574
  509.5 1.8 copy-done.9
  511.3 21.7 %outer_rec.1 = bf16[4,4,160,1152]{3,2,1,0:T(8,128)(2,1)} custom-call(bf16[1536,2560]{1,0:T(8,128)(2,1)} %get-tuple-element.76.left1, bf16[1536,768]{1,0:T(8,128)(2,1)S(1)} %copy-done.9, bf16[1536,2560]{1,0:T(8,128)(2,1)} %bitcast.98, bf16[1536,384]{1,0:T(8,128)(2,1)S(1)} %copy-done.10), custom_call_target="tpu_custom_call" | custom-call | flops 9059696640 | bytes 25165824 | tf_op jit(solution)/shard_map/outer_rec/pallas_call | solution.py:1672
  533.0 49.8 %d_normed_one.1 = (bf16[192,2560]{1,0:T(8,128)(2,1)}, f32[8,2560]{1,0:T(8,128)}, f32[8,128]{1,0:T(8,128)}, bf16[128,384]{1,0:T(8,128)(2,1)}, f32[8,384]{1,0:T(8,128)}) custom-call(bf16[1536,768]{1,0:T(8,128)(2,1)} %get-tuple-element.102.right1.act, bf16[2560,896]{1,0:T(8,128)(2,1)} %get-tuple-element.74.w_rec.w, ...), custom_call_target="tpu_custom_call" | custom-call | flops 6039797760 | bytes 41943040 | tf_op jit(solution)/shard_map/d_normed_one/pallas_call | solution.py:675
  582.8 16.0 %take_home.1 = bf16[768,640]{1,0:T(8,128)(2,1)} custom-call(bf16[192,2560]{1,0:T(8,128)(2,1)} %get-tuple-element.112.rows), custom_call_target="tpu_custom_call" | custom-call | tf_op jit(solution)/shard_map/take_home/pallas_call | solution.py:726
  598.8 16.4 %reduce-scatter.6.cloned.1.call-done = bf16[1,4,160,2048]{3,2,1,0:T(8,128)(2,1)} async-done(((bf16[4,4,160,2048]{3,2,1,0:T(8,128)(2,1)}), bf16[1,4,160,2048]{3,2,1,0:T(8,128)(2,1)}) %reduce-scatter.6.cloned.1.call-update) | async-done | bytes 2621456 | tf_op jit(solution)/shard_map/reduce_scatter | solution.py:1781
  616.7 1.6 convert_bitcast_fusion
  618.3 69.6 %out_two.1 = (bf16[192,2560]{1,0:T(8,128)(2,1)}, f32[8,128]{1,0:T(8,128)}, bf16[4,128,384]{2,1,0:T(8,128)(2,1)}, bf16[4,160,2048]{2,1,0:T(8,128)(2,1)}) custom-call(bf16[1536,1024]{1,0:T(8,128)(2,1)} %get-tuple-element.114.right.act, bf16[1024,2560]{1,0:T(8,128)(2,1)} %get-tuple-element.81.w_down.w, bf16[128,384]{1,0:T(8,128)(2,1)} %get-tuple-element.115.refs_0_, ...), custom_call_target="tpu_custom_call" | custom-call | flops 8053063680 | bytes 41943040 | tf_op jit(solution)/shard_map/out_two/pallas_call | solution.py:675
  690.8 30.5 %small_sums.1 = (f32[2,640]{1,0:T(2,128)S(1)}, f32[8,128]{1,0:T(8,128)S(1)}, f32[4,8,384]{2,1,0:T(8,128)S(1)}, bf16[4,4,128,384]{3,2,1,0:T(8,128)(2,1)S(1)}, bf16[768,640]{1,0:T(8,128)(2,1)S(1)}) custom-call(f32[8,2560]{1,0:T(8,128)S(1)} %copy-done.4, f32[8,2560]{1,0:T(8,128)S(1)} %copy-done.3, f32[8,128]{1,0:T(8,128)S(1)} %copy-done.7, ...), custom_call_target="tpu_custom_call" | custom-call | tf_op jit(solution)/shard_map/small_sums/pallas_call | solution.py:999
  722.6 1.9 slice_bitcast_fusion.19
  726.4 1.5 copy-done.14
  728.1 2.6 maximum_convert_fusion
  730.7 1.4 copy-done
  732.1 20.2 %deal_rec.1 = bf16[4,160,1152]{2,1,0:T(8,128)(2,1)S(1)} custom-call(bf16[4,160,1152]{2,1,0:T(8,128)(2,1)S(1)} %bitcast.93), custom_call_target="tpu_custom_call" | custom-call | tf_op jit(solution)/shard_map/deal_rec/pallas_call | solution.py:892
  (84 shorter events, 17.0 us)
Async XLA Ops:
  7.2 419.5 %reduce-scatter.4.cloned.1.call-start = ((), (), s32[]{:S(2)}) async-start(), calls=%async_computation.3 | async-start | bytes 6553600 | tf_op jit(solution)/shard_map/reduce_scatter | solution.py:1767
  321.2 1.9 copy-start.11
  334.7 280.5 %reduce-scatter.6.cloned.1.call-start = ((), (), s32[]{:S(2)}) async-start(), calls=%async_computation.4 | async-start | bytes 13107200 | tf_op jit(solution)/shard_map/reduce_scatter | solution.py:1781
  426.7 304.0 %reduce-scatter.8.cloned.1.call-start = ((), (), s32[]{:S(2)}) async-start(), calls=%async_computation.5 | async-start | bytes 7372800 | tf_op jit(solution)/shard_map/reduce_scatter | solution.py:1816
  426.7 82.7 %copy-start.10 = (bf16[1536,384]{1,0:T(8,128)(2,1)S(1)}, bf16[1536,384]{1,0:T(8,128)(2,1)}, u32[]{:S(2)}) copy-start(bf16[1536,384]{1,0:T(8,128)(2,1)} %get-tuple-element.77.act.right2) | copy-start | bytes 3538948
  509.4 1.8 copy-start.9
  615.2 1.3 copy-start.13
  618.3 69.6 %copy-start.3 = (f32[8,2560]{1,0:T(8,128)S(1)}, f32[8,2560]{1,0:T(8,128)}, u32[]{:S(2)}) copy-start(f32[8,2560]{1,0:T(8,128)} %get-tuple-element.107.gain_two) | copy-start | bytes 245764
  618.3 69.6 %copy-start.4 = (f32[8,2560]{1,0:T(8,128)S(1)}, f32[8,2560]{1,0:T(8,128)}, u32[]{:S(2)}) copy-start(f32[8,2560]{1,0:T(8,128)} %get-tuple-element.106.gain_one) | copy-start | bytes 245764
  618.3 69.6 %copy-start.5 = (f32[8,384]{1,0:T(8,128)S(1)}, f32[8,384]{1,0:T(8,128)}, u32[]{:S(2)}) copy-start(f32[8,384]{1,0:T(8,128)} %get-tuple-element.118.small) | copy-start | bytes 36868
  618.3 69.6 %copy-start.6 = (f32[8,128]{1,0:T(8,128)S(1)}, f32[8,128]{1,0:T(8,128)}, u32[]{:S(2)}) copy-start(f32[8,128]{1,0:T(8,128)} %get-tuple-element.109.squares_one) | copy-start | bytes 12292
  618.3 69.6 %copy-start.7 = (f32[8,128]{1,0:T(8,128)S(1)}, f32[8,128]{1,0:T(8,128)}, u32[]{:S(2)}) copy-start(f32[8,128]{1,0:T(8,128)} %get-tuple-element.108.squares_x) | copy-start | bytes 12292
  687.9 1.2 copy-start.1
  689.1 1.0 copy-start.2
  690.1 0.7 copy-start.8
  726.4 1.5 copy-start.14
  730.7 1.4 copy-start
  753.5 2.2 copy-start.12
Sparse Core Ops, SparseCore 0:
  334.8 91.8 reduce-scatter.3
  429.0 186.1 reduce-scatter.5
  617.5 112.6 reduce-scatter.7
